TPU v7x, 256 devices: a whole 4x4x8 slice. The times are simulated.
256 devices in a mesh: dap: 128 (over y_lo, z, x, core), dp: 2 (over y_hi).
Axes of the slice: x: 4, y: 4 (y_hi: 2, y_lo: 2; y = y_hi * 2 + y_lo), z: 8, core: 2. Of those that a mesh axis runs over, the one named last changes fastest.
Arguments:
- alignment_features: bfloat16 [64, 2048, 256], P(None, ('dp', 'dap')), parts along dimension 1, may hold values from -8 to 8
- layer_norm_gain: float32 [256], replicated, may hold values from 0.1 to 1.9
- layer_norm_bias: float32 [256], replicated, may hold values from -1.2 to 1.2
- left_projection_weight: bfloat16 [256, 32], replicated, may hold values from -0.375 to 0.375
- left_projection_bias: float32 [32], replicated, may hold values from -1.8 to 1.8
- right_projection_weight: bfloat16 [256, 32], replicated, may hold values from -0.375 to 0.375
- right_projection_bias: float32 [32], replicated, may hold values from -1.8 to 1.8
- output_weight: bfloat16 [1024, 128], replicated, may hold values from -0.1875 to 0.1875
- output_bias: float32 [128], replicated, may hold values from -1.8 to 1.8
Outputs:
- pair_update: bfloat16 [2048, 1024, 128], P('dp', 'dap'), parts along dimension 0
There are 2 independent parts, one for each index of `dp`. A program takes and returns all parts, laid end to end along the dimension named above; an argument that names none is the same for every part. Nothing has to cross between parts.
All inputs are finite; a program needn't handle non-finite values.
Results may differ from a plain program's by a relative error of at most 0.0048.
Values may be sent and summed in bfloat16 or wider, within the bound.
No kernel may reach another device: no remote copies, remote signals or barrier semaphores. Data moves between devices by JAX's collectives and lax.ppermute only.
A program may use at most 64 MiB of HBM per device.

v0:
```python
import jax
import jax.numpy as jnp
from jax import lax
from jax.sharding import PartitionSpec as P

HID = 32
SEQS = 64


def apply_layer_norm(feats, gain, offset):
    values = feats.astype(jnp.float32)
    center = jnp.mean(values, axis=-1, keepdims=True)
    spread = jnp.mean((values - center) ** 2, axis=-1, keepdims=True)
    return ((values - center) * lax.rsqrt(spread + 1e-05) * gain + offset).astype(jnp.bfloat16)


def project(normalized_alignment, weight, bias):
    result = (
        jnp.einsum("sic,ch->ish", normalized_alignment, weight, preferred_element_type=jnp.float32)
        + bias
    )
    return result.astype(jnp.bfloat16)


def per_device(
    alignment_features,
    layer_norm_gain,
    layer_norm_bias,
    left_projection_weight,
    left_projection_bias,
    right_projection_weight,
    right_projection_bias,
    output_weight,
    output_bias,
):
    normalized_alignment = apply_layer_norm(alignment_features, layer_norm_gain, layer_norm_bias)
    left_local = project(normalized_alignment, left_projection_weight, left_projection_bias)
    right_local = project(normalized_alignment, right_projection_weight, right_projection_bias)
    local_rows = left_local.shape[0]
    scale = 1.0 / SEQS

    def finish(outer, count):
        outer = (outer * scale).astype(jnp.bfloat16).reshape(count, HID * HID)
        return (
            jnp.dot(outer, output_weight, preferred_element_type=jnp.float32) + output_bias
        ).astype(jnp.bfloat16)

    right_flat = right_local.reshape(local_rows, SEQS * HID)
    slab_rows = lax.all_gather(right_flat, "dap", axis=0, tiled=True)
    count = slab_rows.shape[0]
    right_cols = slab_rows.reshape(count, SEQS, HID)

    def one_row(left_row):
        outer = jnp.einsum("sc,jse->jce", left_row, right_cols, preferred_element_type=jnp.float32)
        return finish(outer, count)

    pair_rows = lax.map(one_row, left_local)
    return lax.all_to_all(pair_rows, "dap", split_axis=1, concat_axis=0, tiled=True)


def solution(mesh):
    in_specs = (P(None, ("dp", "dap"), None), P(), P(), P(), P(), P(), P(), P(), P())
    out_specs = P("dp", "dap", None)
    return jax.shard_map(
        per_device, mesh=mesh, in_specs=in_specs, out_specs=out_specs, check_vma=False
    )
```

profile of v0, /device:TPU:1, one launch (start us, length us, event | category | flops | bytes accessed | tf_op | source)
XLA Modules:
  0.0 356.5 jit_solution(17472937815275796598)
XLA Ops:
  6.5 0.0 copy-start
  6.5 0.0 copy-start.6
  6.6 0.0 all-gather.2.cloned.1.call-start
  6.6 1.2 convert_reduce_fusion
  7.8 1.2 fusion.13
  9.0 0.0 copy-done
  9.0 1.3 fusion.9
  10.3 0.8 reshape.26
  11.1 0.0 all-gather.2.cloned.1.call-update
  11.2 0.0 copy-done.1
  11.2 0.0 copy-done.5
  11.2 0.0 copy-done.4
  11.2 0.0 copy-done.3
  11.2 0.0 copy-done.6
  11.2 0.3 fusion.10
  11.5 0.1 copy.21
  11.7 218.6 %all-gather.2.cloned.1.call-done = bf16[1024,2048]{1,0:T(8,128)(2,1)} async-done(((bf16[8,2048]{1,0:T(8,128)(2,1)}), bf16[1024,2048]{1,0:T(8,128)(2,1)}) %all-gather.2.cloned.1.call-update) | async-done | bytes 4194320 | tf_op jit(solution)/shard_map/all_gather | solution.py:49
  230.3 6.4 %copy.20 = bf16[1024,2048]{0,1:T(8,128)(2,1)} copy(bf16[1024,2048]{1,0:T(8,128)(2,1)} %all-gather.2.cloned.1.call-done) | data formatting | bytes 8388608 | tf_op jit(solution)/shard_map/all_gather | solution.py:49
  236.8 6.5 %copy.22 = bf16[1024,64,32]{0,1,2:T(8,128)(2,1)} copy(bf16[1024,64,32]{0,2,1:T(8,128)(2,1)} %bitcast.44) | data formatting | bytes 8388608 | tf_op jit(solution)/shard_map/while | solution.py:57
  243.3 0.0 copy-done.2
  243.3 39.5 %while.10 = (s32[]{:T(128)}, bf16[8,1024,128]{2,1,0:T(8,128)(2,1)S(1)}, bf16[8,64,32]{1,2,0:T(8,128)(2,1)S(1)}, bf16[1024,64,32]{0,1,2:T(8,128)(2,1)}, bf16[1024...) while((s32[]{:T(128)}, bf16[8,1024,128]{2,1,0:T(8,128)(2,1)S(1)}, bf16[8,64,32]{1,2,0:T(8,128)(2,1)S(1)}, ...), condition=%wide.region_3.4_spmd, body=%wide.region_2.3_spmd.sunk | while | flops 405012480 | bytes 13115989 | solution.py:57
  243.3 2.9 fusion.34
  246.2 1.2 copy.26
  247.3 0.9 fusion.35
  248.2 2.9 fusion.34
  251.1 1.2 copy.26
  252.3 0.9 fusion.35
  253.1 2.9 fusion.34
  256.0 1.2 copy.26
  257.2 0.9 fusion.35
  258.1 2.9 fusion.34
  261.0 1.2 copy.26
  262.1 0.9 fusion.35
  263.0 2.9 fusion.34
  265.9 1.2 copy.26
  267.1 0.9 fusion.35
  267.9 2.9 fusion.34
  270.8 1.2 copy.26
  272.0 0.9 fusion.35
  272.9 2.9 fusion.34
  275.8 1.2 copy.26
  276.9 0.9 fusion.35
  277.8 2.9 fusion.34
  280.7 1.2 copy.26
  281.9 0.9 fusion.35
  282.7 1.4 copy.23
  284.1 63.6 %all_to_all.18 = bf16[8,1024,128]{2,0,1:T(8,128)(2,1)S(1)} all-to-all(bf16[8,1024,128]{2,0,1:T(8,128)(2,1)S(1)} %copy.23), channel_id=1, replica_groups=mesh['dap'=128,'dp'=2] {'dap'}, dimensions={1} | all-to-all | bytes 4194304 | tf_op jit(solution)/shard_map/all_to_all | solution.py:58
  347.7 1.9 copy.24
  (11 shorter events, 0.1 us)
Async XLA Ops:
  6.5 2.5 copy-start
  6.5 4.6 %copy-start.1 = (bf16[64,8,256]{2,1,0:T(8,128)(2,1)S(1)}, bf16[64,8,256]{2,1,0:T(8,128)(2,1)}, u32[]{:S(2)}) copy-start(bf16[64,8,256]{2,1,0:T(8,128)(2,1)} %param.11) | copy-start | bytes 786436
  6.5 4.6 %copy-start.5 = (f32[256]{0:T(256)S(1)}, f32[256]{0:T(256)}, u32[]{:S(2)}) copy-start(f32[256]{0:T(256)} %param.12) | copy-start | bytes 3076
  6.5 4.6 %copy-start.4 = (f32[256]{0:T(256)S(1)}, f32[256]{0:T(256)}, u32[]{:S(2)}) copy-start(f32[256]{0:T(256)} %param.13) | copy-start | bytes 3076
  6.5 4.7 %copy-start.3 = (bf16[256,32]{0,1:T(8,128)(2,1)S(1)}, bf16[256,32]{0,1:T(8,128)(2,1)}, u32[]{:S(2)}) copy-start(bf16[256,32]{0,1:T(8,128)(2,1)} %param.14) | copy-start | bytes 49156
  6.5 4.7 %copy-start.6 = (f32[32]{0:T(128)S(1)}, f32[32]{0:T(128)}, u32[]{:S(2)}) copy-start(f32[32]{0:T(128)} %param.15) | copy-start | bytes 388
  6.6 223.8 %all-gather.2.cloned.1.call-start = ((), (), s32[]{:S(2)}) async-start(), calls=%async_computation.1 | async-start | bytes 4227072 | tf_op jit(solution)/shard_map/all_gather | solution.py:49
  236.8 6.5 %copy-start.2 = (bf16[1024,128]{1,0:T(8,128)(2,1)S(1)}, bf16[1024,128]{1,0:T(8,128)(2,1)}, u32[]{:S(2)}) copy-start(bf16[1024,128]{1,0:T(8,128)(2,1)} %param.18) | copy-start | bytes 786436
  236.8 6.5 %copy-start.7 = (f32[128]{0:T(128)S(1)}, f32[128]{0:T(128)}, u32[]{:S(2)}) copy-start(f32[128]{0:T(128)} %param.19) | copy-start | bytes 1540
Sparse Core Ops, SparseCore 0:
  11.3 218.9 all-gather.1
where the time goes:
time: 357 us
  waiting for transfers between devices  219 us (61%)
  blocking collectives  63.6 us (18%)
  matrix products  31.7 us (9%)
  local copies, waits for them, and re-layouts  26.4 us (7%)
  between operations  13.5 us (4%)
    all_gather x1, waiting for transfers between devices, per_device(): slab_rows = lax.all_gather(right_flat, 'dap', axis=0, tiled=True)  219 us
    all_to_all x1, blocking collectives, per_device(): lax.all_to_all(pair_rows, 'dap', split_axis=1, concat_axis=0, tiled=True)  63.6 us
    dot_general x8, matrix products, one_row(): jnp.einsum('sc,jse->jce', left_row, right_cols, preferred_element_type=jn...  23.2 us
    convert_element_type x8, local copies, waits for them, and re-layouts, finish(): outer = (outer * scale).astype(jnp.bfloat16).reshape(count, HID * HID)  9.23 us
    while x3, local copies, waits for them, and re-layouts, per_device(): pair_rows = lax.map(one_row, left_local)  7.99 us
  transfers between devices with their start and end apart: 1, of which 1 were waited for; matrix products, arithmetic and copies ran while one was open for 0% of the time, Pallas kernels for 0%

commit v1 on v0

v1 whole, which is shorter than its diff:
```python
import jax
import jax.numpy as jnp
from jax import lax
from jax.sharding import PartitionSpec as P

HID = 32
SEQS = 64


def apply_layer_norm(feats, gain, offset):
    values = feats.astype(jnp.float32)
    center = jnp.mean(values, axis=-1, keepdims=True)
    spread = jnp.mean((values - center) ** 2, axis=-1, keepdims=True)
    return ((values - center) * lax.rsqrt(spread + 1e-05) * gain + offset).astype(jnp.bfloat16)


def per_device(
    alignment_features,
    layer_norm_gain,
    layer_norm_bias,
    left_projection_weight,
    left_projection_bias,
    right_projection_weight,
    right_projection_bias,
    output_weight,
    output_bias,
):
    normalized = apply_layer_norm(alignment_features, layer_norm_gain, layer_norm_bias)
    rows = normalized.shape[1]
    left = jnp.einsum(
        "sic,ch->ihs", normalized, left_projection_weight, preferred_element_type=jnp.float32
    )
    left = (left + left_projection_bias[None, :, None]).astype(jnp.bfloat16)
    left = left.reshape(rows, HID * SEQS)
    left_all = lax.all_gather(left, "dap", axis=0, tiled=True)

    right = jnp.einsum(
        "sic,ch->ish", normalized, right_projection_weight, preferred_element_type=jnp.float32
    )
    right = (right + right_projection_bias).astype(jnp.bfloat16)
    weight = output_weight.reshape(HID, HID, -1)
    table = jnp.einsum("jse,cez->csjz", right, weight, preferred_element_type=jnp.float32)
    table = (table * (1.0 / SEQS)).astype(jnp.bfloat16).reshape(HID * SEQS, rows, -1)

    pair = jnp.einsum("ik,kjz->ijz", left_all, table, preferred_element_type=jnp.float32)
    return (pair + output_bias).astype(jnp.bfloat16)


def solution(mesh):
    in_specs = (P(None, ("dp", "dap"), None), P(), P(), P(), P(), P(), P(), P(), P())
    out_specs = P("dp", "dap", None)
    return jax.shard_map(
        per_device, mesh=mesh, in_specs=in_specs, out_specs=out_specs, check_vma=False
    )
```

time: 357 us -> 249 us (0.70)
  blocking collectives: 63.6 us -> 0 us
  local copies, waits for them, and re-layouts: 26.4 us -> 3.56 us
  matrix products: 31.7 us -> 13 us
  waiting for transfers between devices: 219 us -> 215 us
    all_to_all x1 -> x0, blocking collectives: 63.6 us -> none  [per_device(): lax.all_to_all(pair_rows, 'dap', split_axis=1, concat_axis=0, tiled=True)]
    dot_general x18 -> x3, matrix products: 31.7 us -> 13 us  [the longest x1 7.95 us: per_device(): jnp.einsum('ik,kjz->ijz', left_all, table, preferred_element_type=jnp.flo...]
    while x3 -> x0, local copies, waits for them, and re-layouts: 7.99 us -> none  [per_device(): pair_rows = lax.map(one_row, left_local)]
    all_gather x1 -> x0, local copies, waits for them, and re-layouts: 6.44 us -> none  [per_device(): slab_rows = lax.all_gather(right_flat, 'dap', axis=0, tiled=True)]
    convert_element_type x9 -> x2, local copies, waits for them, and re-layouts: 9.25 us -> 2.81 us  [the longest x1 2.67 us: per_device(): return (pair + output_bias).astype(jnp.bfloat16)]
    all_gather x1, waiting for transfers between devices: 219 us -> 215 us  [per_device(): left_all = lax.all_gather(left, 'dap', axis=0, tiled=True)]
  transfers between devices with their start and end apart: 1 -> 1, of which waited for: 1 -> 1; matrix products, arithmetic and copies ran while one was open for 0% -> 2% of each run, Pallas kernels for 0% -> 0%
where the time goes in v1:
time: 249 us
  waiting for transfers between devices  215 us (86%)
  between operations  13.5 us (5%)
  matrix products  13 us (5%)
  local copies, waits for them, and re-layouts  3.56 us (1%)
  other arithmetic  3.5 us (1%)
    all_gather x1, waiting for transfers between devices, per_device(): left_all = lax.all_gather(left, 'dap', axis=0, tiled=True)  215 us
    dot_general x1, matrix products, per_device(): jnp.einsum('ik,kjz->ijz', left_all, table, preferred_element_type=jnp.flo...  7.95 us
  transfers between devices with their start and end apart: 1, of which 1 were waited for; matrix products, arithmetic and copies ran while one was open for 2% of the time, Pallas kernels for 0%

profile of v1, /device:TPU:1, one launch (start us, length us, event | category | flops | bytes accessed | tf_op | source)
XLA Modules:
  0.0 248.5 jit_solution(47726140877146435)
XLA Ops:
  6.5 0.0 copy-start
  6.5 0.0 copy-start.1
  6.5 0.0 all-gather.2.cloned.1.call-start
  6.5 1.1 convert_reduce_fusion
  7.7 1.2 fusion.10
  8.9 1.2 fusion.13
  10.1 0.9 fusion.5
  11.0 0.1 copy.11
  11.1 0.7 reshape.26
  11.9 0.0 all-gather.2.cloned.1.call-update
  11.9 0.0 copy-done
  11.9 4.2 %multiply_convert_fusion = bf16[8,64,32,128]{3,1,2,0:T(8,128)(2,1)} fusion(bf16[32,32,128,1]{2,1,0,3:T(8,128)(2,1)S(1)} %bitcast.31, bf16[64,8,256]{2,1,0:T(8,128)(2,1)S(1)} %fusion.13, f32[32]{0:T(128)} %param.15, bf16[256,32]{0,1:T(8,128)(2,1)} %param.14), kind=kOutput, calls=%fused_computation | convolution fusion | flops 146833408 | bytes 4735104 | tf_op jit(solution)/shard_map/jse,cez->csjz/dot_general | solution.py:42
  16.1 215.0 %all-gather.2.cloned.1.call-done = bf16[1024,2048]{1,0:T(8,128)(2,1)} async-done(((bf16[8,2048]{1,0:T(8,128)(2,1)}), bf16[1024,2048]{1,0:T(8,128)(2,1)}) %all-gather.2.cloned.1.call-update) | async-done | bytes 4194320 | tf_op jit(solution)/shard_map/all_gather | solution.py:35
  231.1 0.0 copy-done.1
  231.1 7.9 %add_convert_fusion = bf16[1024,8,128]{2,0,1:T(8,128)(2,1)S(1)} fusion(bf16[2048,8,128]{2,0,1:T(8,128)(2,1)} %bitcast.32, bf16[1024,2048]{1,0:T(8,128)(2,1)} %all-gather.2.cloned.1.call-done, f32[128]{0:T(128)S(1)} %copy-done.1), kind=kOutput, calls=%fused_computation.3 | convolution fusion | flops 4297064448 | bytes 10486272 | tf_op jit(solution)/shard_map/ik,kjz->ijz/dot_general | solution.py:45
  239.0 2.7 %copy.12 = bf16[1024,8,128]{2,1,0:T(8,128)(2,1)} copy(bf16[1024,8,128]{2,0,1:T(8,128)(2,1)S(1)} %add_convert_fusion) | data formatting | bytes 4194304 | tf_op jit(solution)/shard_map/convert_element_type | solution.py:46
  (2 shorter events, 0.0 us)
Async XLA Ops:
  6.5 5.4 %copy-start = (bf16[1024,128]{1,0:T(8,128)(2,1)S(1)}, bf16[1024,128]{1,0:T(8,128)(2,1)}, u32[]{:S(2)}) copy-start(bf16[1024,128]{1,0:T(8,128)(2,1)} %param.16) | copy-start | bytes 786436
  6.5 224.5 %copy-start.1 = (f32[128]{0:T(128)S(1)}, f32[128]{0:T(128)}, u32[]{:S(2)}) copy-start(f32[128]{0:T(128)} %param.17) | copy-start | bytes 1540
  6.5 224.5 %all-gather.2.cloned.1.call-start = ((), (), s32[]{:S(2)}) async-start(), calls=%async_computation | async-start | bytes 4227072 | tf_op jit(solution)/shard_map/all_gather | solution.py:35
Sparse Core Ops, SparseCore 0:
  12.0 218.9 all-gather.1

commit v2 on v1

v2 whole, which is shorter than its diff:
```python
import functools

import jax
import jax.numpy as jnp
from jax import lax
from jax.experimental import pallas as pl
from jax.experimental.pallas import tpu as pltpu
from jax.sharding import PartitionSpec as P

HID = 32
SEQS = 64
C_Z = 128
NY, NZ, NX, NC = 2, 8, 4, 2
PACK = 4


def device_index(y, z, x, c):
    return ((y % NY * NZ + z % NZ) * NX + x % NX) * NC + c % NC


def shift(move):
    pairs = []
    for y in range(NY):
        for z in range(NZ):
            for x in range(NX):
                for c in range(NC):
                    pairs.append((device_index(y, z, x, c), device_index(*move(y, z, x, c))))
    return pairs


Z_PAIR = shift(lambda y, z, x, c: (y, z ^ 1, x, c))
Z_PLUS = {k: shift(lambda y, z, x, c, k=k: (y, z + k, x, c)) for k in (2, 4, 6)}
Y_PAIR = shift(lambda y, z, x, c: (y + 1, z, x, c))
X_PLUS = {k: shift(lambda y, z, x, c, k=k: (y, z, x + k, c)) for k in (1, 3)}
CORE_PAIR = shift(lambda y, z, x, c: (y, z, x, c + 1))


def send(block, pairs):
    return lax.ppermute(block, "dap", pairs)


def layer_norm(feats, gain, offset):
    values = feats.astype(jnp.float32)
    center = jnp.mean(values, axis=-1, keepdims=True)
    spread = jnp.mean((values - center) ** 2, axis=-1, keepdims=True)
    return (values - center) * lax.rsqrt(spread + 1e-05) * gain + offset


def left_kernel(feats_ref, gain_ref, offset_ref, weight_ref, bias_ref, left_ref):
    groups = SEQS // PACK
    rows = feats_ref.shape[1]
    normed = layer_norm(feats_ref[...], gain_ref[...], offset_ref[...])
    normed = normed.reshape(groups, PACK, rows, -1)
    wide = jnp.concatenate([normed[:, k] for k in range(PACK)], axis=-1)
    wide = wide.reshape(groups * rows, -1).astype(jnp.bfloat16)
    weight = jnp.concatenate([weight_ref[...].astype(jnp.float32)] * PACK, axis=1)
    lane = lax.broadcasted_iota(jnp.int32, weight.shape, 1) // HID
    diagonal = jnp.concatenate(
        [jnp.where(lane == k, weight, 0.0) for k in range(PACK)], axis=0
    ).astype(jnp.bfloat16)
    out = jnp.dot(wide, diagonal, preferred_element_type=jnp.float32) + bias_ref[...]
    for g in range(groups):
        left_ref[:, g * PACK * HID : (g + 1) * PACK * HID] = out[
            g * rows : (g + 1) * rows
        ].astype(jnp.bfloat16)


def table_kernel(feats_ref, gain_ref, offset_ref, weight_ref, bias_ref, out_weight_ref, table_ref, right_ref):
    rows = feats_ref.shape[1]
    normed = layer_norm(feats_ref[...], gain_ref[...], offset_ref[...])
    normed = normed.reshape(SEQS * rows, -1).astype(jnp.bfloat16)
    right = jnp.dot(normed, weight_ref[...], preferred_element_type=jnp.float32) + bias_ref[...]
    right_ref[...] = right.astype(jnp.bfloat16)
    step = 2

    def body(b, carry):
        start = pl.multiple_of(b * step * rows, step * rows)
        part = jnp.dot(
            right_ref[pl.ds(start, step * rows), :],
            out_weight_ref[...],
            preferred_element_type=jnp.float32,
        ) * (1.0 / SEQS)
        part = part.reshape(step * rows, HID, C_Z)
        for s in range(step):
            at = pl.multiple_of((b * step + s) * HID, HID)
            for j in range(rows):
                table_ref[pl.ds(at, HID), j * C_Z : (j + 1) * C_Z] = part[s * rows + j].astype(
                    jnp.bfloat16
                )
        return carry

    lax.fori_loop(0, SEQS // step, body, 0)


def pair_kernel(place_ref, *refs, pieces, aliased):
    lefts = refs[: len(pieces)]
    table_ref, bias_ref = refs[len(pieces) : len(pieces) + 2]
    out_ref, acc_ref = refs[len(pieces) + 2 + aliased :]
    core = place_ref[1]
    for left_ref, (lane, first) in zip(lefts, pieces):
        rows = left_ref.shape[0]
        acc = acc_ref.at[pl.ds(0, rows)]
        acc[...] = jnp.dot(left_ref[...], table_ref[...], preferred_element_type=jnp.float32)
        c = core if lane == 0 else 1 - core

        def body(k, carry, first=first, c=c):
            part = acc_ref[pl.ds(pl.multiple_of(k * 8, 8), 8), :].reshape(8, 8, C_Z) + bias_ref[...]
            out_ref[place_ref[2 + first + k], 0, c] = part.astype(jnp.bfloat16)
            return carry

        lax.fori_loop(0, rows // 8, body, 0, unroll=True)


def pair_block(place, lefts, pieces, table, bias, turn, out):
    aliased = out is not None
    whole = pl.BlockSpec(memory_space=pltpu.VMEM)
    operands = [*lefts, table, bias] + ([out] if aliased else [])
    in_specs = [whole] * (len(lefts) + 2) + ([pl.BlockSpec(memory_space=pl.ANY)] if aliased else [])
    rows = max(left.shape[0] for left in lefts)
    return pl.pallas_call(
        functools.partial(pair_kernel, pieces=pieces, aliased=int(aliased)),
        grid_spec=pltpu.PrefetchScalarGridSpec(
            num_scalar_prefetch=1,
            grid=(1,),
            in_specs=in_specs,
            out_specs=pl.BlockSpec(
                (NY * NZ, 1, NC, 8, 8, C_Z),
                lambda i, place: (0, lax.rem(place[0] + turn, NX), 0, 0, 0, 0),
            ),
            scratch_shapes=[pltpu.VMEM((rows, 8 * C_Z), jnp.float32)],
        ),
        out_shape=jax.ShapeDtypeStruct((NY * NZ, NX, NC, 8, 8, C_Z), jnp.bfloat16),
        input_output_aliases={len(operands): 0} if aliased else {},
        compiler_params=pltpu.CompilerParams(vmem_limit_bytes=24 * 1024 * 1024),
    )(place, *operands)


def per_device(
    alignment_features,
    layer_norm_gain,
    layer_norm_bias,
    left_projection_weight,
    left_projection_bias,
    right_projection_weight,
    right_projection_bias,
    output_weight,
    output_bias,
):
    rows = alignment_features.shape[1]
    gain, offset = layer_norm_gain[None], layer_norm_bias[None]
    vmem = pltpu.CompilerParams(vmem_limit_bytes=32 * 1024 * 1024)
    left = pl.pallas_call(
        left_kernel,
        out_shape=jax.ShapeDtypeStruct((rows, SEQS * HID), jnp.bfloat16),
        compiler_params=vmem,
    )(
        alignment_features,
        gain,
        offset,
        left_projection_weight,
        jnp.tile(left_projection_bias, PACK)[None],
    )
    out_weight = output_weight.reshape(HID, HID, C_Z).transpose(1, 0, 2).reshape(HID, HID * C_Z)
    table = pl.pallas_call(
        table_kernel,
        out_shape=jax.ShapeDtypeStruct((SEQS * HID, rows * C_Z), jnp.bfloat16),
        scratch_shapes=[pltpu.VMEM((SEQS * rows, HID), jnp.bfloat16)],
        compiler_params=vmem,
    )(
        alignment_features,
        gain,
        offset,
        right_projection_weight,
        right_projection_bias[None],
        out_weight,
    )

    me = lax.axis_index("dap")
    core, x, z, y = me % NC, me // NC % NX, me // (NC * NX) % NZ, me // (NC * NX * NZ)
    slots = [
        (y ^ t) * NZ + ((z + NZ - back) % NZ ^ b)
        for t in range(NY)
        for back in (0, 4, 2, 6)
        for b in range(2)
    ]
    place = jnp.stack([x, core] + slots).astype(jnp.int32)
    bias = output_bias[None]

    pair = jnp.concatenate([left, send(left, Z_PAIR)], axis=0)
    ring = jnp.concatenate([pair] + [send(pair, Z_PLUS[k]) for k in (4, 2, 6)], axis=0)
    block = jnp.concatenate([ring, send(ring, Y_PAIR)], axis=0)

    def both(blocks):
        return blocks + [send(b, CORE_PAIR) for b in blocks]

    out = pair_block(place, both([block]), [(0, 0), (1, 0)], table, bias, 0, None)
    low, high = send(block, X_PLUS[1]), send(block, X_PLUS[3])
    half = block.shape[0] // 2
    far = [send(low[:half], X_PLUS[1]), send(high[half:], X_PLUS[3])]
    out = pair_block(place, both([low]), [(0, 0), (1, 0)], table, bias, 3, out)
    out = pair_block(place, both([high]), [(0, 0), (1, 0)], table, bias, 1, out)
    out = pair_block(place, both(far), [(0, 0), (0, 8), (1, 0), (1, 8)], table, bias, 2, out)
    return out.reshape(NY * NZ * NX * NC * 8, 8, C_Z)


def solution(mesh):
    in_specs = (P(None, ("dp", "dap"), None), P(), P(), P(), P(), P(), P(), P(), P())
    out_specs = P("dp", "dap", None)
    return jax.shard_map(
        per_device, mesh=mesh, in_specs=in_specs, out_specs=out_specs, check_vma=False
    )
```

time: 249 us -> 83.3 us (0.33)
  waiting for transfers between devices: 215 us -> 22.9 us
  starting transfers between devices: 0.01 us -> 29.2 us
  Pallas kernels: 0 us -> 22.1 us
  between operations: 13.5 us -> 0.19 us
  matrix products: 13 us -> 0 us
  local copies, waits for them, and re-layouts: 3.56 us -> 8.57 us
  other arithmetic: 3.5 us -> 0.01 us
    all_gather x1 -> x0, waiting for transfers between devices: 215 us -> none  [per_device(): left_all = lax.all_gather(left, 'dap', axis=0, tiled=True)]
    ppermute x0 -> x14, starting transfers between devices: none -> 29.2 us  [send(): return lax.ppermute(block, 'dap', pairs)]
    ppermute x0 -> x14, waiting for transfers between devices: none -> 22.9 us  [send(): return lax.ppermute(block, 'dap', pairs)]
    pallas_call x0 -> x6, Pallas kernels: none -> 22.1 us  [the longest x4 14.8 us: pair_block(): pl.pallas_call(functools.partial(pair_kernel, pieces=pieces, aliased=int(...]
    dot_general x3 -> x0, matrix products: 13 us -> none  [the longest x1 7.95 us: per_device(): jnp.einsum('ik,kjz->ijz', left_all, table, preferred_element_type=jnp.flo...]
    unnamed x4 -> x31, local copies, waits for them, and re-layouts: 0.01 us -> 7.57 us
    convert_element_type x2 -> x0, local copies, waits for them, and re-layouts: 2.81 us -> none  [the longest x1 2.67 us: per_device(): return (pair + output_bias).astype(jnp.bfloat16)]
  transfers between devices with their start and end apart: 1 -> 14, of which waited for: 1 -> 7; matrix products, arithmetic and copies ran while one was open for 2% -> 1% of each run, Pallas kernels for 0% -> 19%
where the time goes in v2:
time: 83.3 us; the launch traced here: 83 us
  starting transfers between devices  29.2 us (35%)
  waiting for transfers between devices  22.9 us (27%)
  Pallas kernels  22.1 us (27%)
  local copies, waits for them, and re-layouts  8.57 us (10%)
    ppermute x14, starting transfers between devices, send(): return lax.ppermute(block, 'dap', pairs)  29.2 us
    ppermute x14, waiting for transfers between devices, send(): return lax.ppermute(block, 'dap', pairs)  22.9 us
    pallas_call x4, Pallas kernels, pair_block(): pl.pallas_call(functools.partial(pair_kernel, pieces=pieces, aliased=int(...  14.8 us
    unnamed x31, local copies, waits for them, and re-layouts  7.57 us
    pallas_call x1, Pallas kernels, per_device(): pl.pallas_call(table_kernel, out_shape=jax.ShapeDtypeStruct((SEQS * HID,...  6.75 us
  transfers between devices with their start and end apart: 14, of which 7 were waited for; matrix products, arithmetic and copies ran while one was open for 1% of the time, Pallas kernels for 19%

profile of v2, /device:TPU:1, one launch (start us, length us, event | category | flops | bytes accessed | tf_op | source)
XLA Modules:
  0.0 83.0 jit_solution(3546952147462570275)
XLA Ops:
  0.0 0.8 %copy.13.weight_ref = bf16[256,32]{1,0:T(8,128)(2,1)S(1)} copy(bf16[256,32]{0,1:T(8,128)(2,1)} %param.12) | data formatting | bytes 32768 | tf_op args[3]
  0.9 0.7 tile.2
  1.5 0.1 broadcast_in_dim_tile.3.bias_ref
  1.6 0.9 %copy-done.2 = bf16[64,8,256]{2,1,0:T(8,128)(2,1)S(1)} copy-done((bf16[64,8,256]{2,1,0:T(8,128)(2,1)S(1)}, bf16[64,8,256]{2,1,0:T(8,128)(2,1)}, u32[]{:S(2)}) %copy-start.2) | copy-done | bytes 262168
  2.6 0.7 copy-done.5
  3.2 0.7 copy-done.7
  3.9 0.6 shard_map.91
  4.6 2.6 %collective-permute-start = (bf16[8,2048]{1,0:T(8,128)(2,1)S(1)}, bf16[8,2048]{1,0:T(8,128)(2,1)S(1)}, u32[]{:S(2)}, u32[]{:S(2)}) collective-permute-start(bf16[8,2048]{1,0:T(8,128)(2,1)S(1)} %shard_map.91), channel_id=1, source_target_pairs={{0,16},{2,18},{4,20},{6,22},{8,24},{10,26},{12,28},{14,30},{16,0},... | collective-permute-start | bytes 98312 | tf_op jit(solution)/shard_map/ppermute | solution.py:39
  7.1 1.3 %collective-permute-done = bf16[8,2048]{1,0:T(8,128)(2,1)S(1)} collective-permute-done((bf16[8,2048]{1,0:T(8,128)(2,1)S(1)}, bf16[8,2048]{1,0:T(8,128)(2,1)S(1)}, u32[]{:S(2)}, u32[]{:S(2)}) %collective-permute-start) | collective-permute-done | bytes 32800 | tf_op jit(solution)/shard_map/ppermute | solution.py:39
  8.4 6.8 %collective-permute-start.1 = (bf16[16,2048]{1,0:T(8,128)(2,1)S(1)}, bf16[16,2048]{1,0:T(8,128)(2,1)S(1)}, u32[]{:S(2)}, u32[]{:S(2)}) collective-permute-start(bf16[16,2048]{1,0:T(8,128)(2,1)S(1)} %pad_maximum_fusion), channel_id=1, source_target_pairs={{0,64},{2,66},{4,68},{6,70},{8,72},{10,74},{12,76},{14,78},{16,80}... | collective-permute-start | bytes 196616 | tf_op jit(solution)/shard_map/ppermute | solution.py:39
  15.2 1.2 %collective-permute-start.2 = (bf16[16,2048]{1,0:T(8,128)(2,1)S(1)}, bf16[16,2048]{1,0:T(8,128)(2,1)S(1)}, u32[]{:S(2)}, u32[]{:S(2)}) collective-permute-start(bf16[16,2048]{1,0:T(8,128)(2,1)S(1)} %pad_maximum_fusion), channel_id=1, source_target_pairs={{0,32},{2,34},{4,36},{6,38},{8,40},{10,42},{12,44},{14,46},{16,48}... | collective-permute-start | bytes 196616 | tf_op jit(solution)/shard_map/ppermute | solution.py:39
  16.4 2.4 %collective-permute-start.3 = (bf16[16,2048]{1,0:T(8,128)(2,1)S(1)}, bf16[16,2048]{1,0:T(8,128)(2,1)S(1)}, u32[]{:S(2)}, u32[]{:S(2)}) collective-permute-start(bf16[16,2048]{1,0:T(8,128)(2,1)S(1)} %pad_maximum_fusion), channel_id=1, source_target_pairs={{0,96},{2,98},{4,100},{6,102},{8,104},{10,106},{12,108},{14,110},{... | collective-permute-start | bytes 196616 | tf_op jit(solution)/shard_map/ppermute | solution.py:39
  18.8 0.0 collective-permute-done.1
  18.8 1.8 %collective-permute-done.2 = bf16[16,2048]{1,0:T(8,128)(2,1)S(1)} collective-permute-done((bf16[16,2048]{1,0:T(8,128)(2,1)S(1)}, bf16[16,2048]{1,0:T(8,128)(2,1)S(1)}, u32[]{:S(2)}, u32[]{:S(2)}) %collective-permute-start.2) | collective-permute-done | bytes 65568 | tf_op jit(solution)/shard_map/ppermute | solution.py:39
  20.7 1.5 %collective-permute-done.3 = bf16[16,2048]{1,0:T(8,128)(2,1)S(1)} collective-permute-done((bf16[16,2048]{1,0:T(8,128)(2,1)S(1)}, bf16[16,2048]{1,0:T(8,128)(2,1)S(1)}, u32[]{:S(2)}, u32[]{:S(2)}) %collective-permute-start.3) | collective-permute-done | bytes 65568 | tf_op jit(solution)/shard_map/ppermute | solution.py:39
  22.2 1.4 %collective-permute-start.4 = (bf16[64,2048]{1,0:T(8,128)(2,1)S(1)}, bf16[64,2048]{1,0:T(8,128)(2,1)S(1)}, u32[]{:S(2)}, u32[]{:S(2)}) collective-permute-start(bf16[64,2048]{1,0:T(8,128)(2,1)S(1)} %get-tuple-element.5), channel_id=1, source_target_pairs={{0,128},{2,130},{4,132},{6,134},{8,136},{10,138},{12,140},{14,142}... | collective-permute-start | bytes 786440 | tf_op jit(solution)/shard_map/ppermute | solution.py:39
  23.6 4.4 %collective-permute-done.4 = bf16[64,2048]{1,0:T(8,128)(2,1)S(1)} collective-permute-done((bf16[64,2048]{1,0:T(8,128)(2,1)S(1)}, bf16[64,2048]{1,0:T(8,128)(2,1)S(1)}, u32[]{:S(2)}, u32[]{:S(2)}) %collective-permute-start.4) | collective-permute-done | bytes 262176 | tf_op jit(solution)/shard_map/ppermute | solution.py:39
  28.0 1.3 %collective-permute-start.5 = (bf16[128,2048]{1,0:T(8,128)(2,1)S(1)}, bf16[128,2048]{1,0:T(8,128)(2,1)S(1)}, u32[]{:S(2)}, u32[]{:S(2)}) collective-permute-start(bf16[128,2048]{1,0:T(8,128)(2,1)S(1)} %constant_dynamic-update-slice_fusion.5.refs_0_), channel_id=1, source_target_pairs={{0,4},{2,6},{4,8},{6,10},{8,12},{10,14},{12,0},{14,2},{16,20},{18,... | collective-permute-start | bytes 1572872 | tf_op jit(solution)/shard_map/ppermute | solution.py:39
  29.3 1.5 %collective-permute-start.7 = (bf16[128,2048]{1,0:T(8,128)(2,1)S(1)}, bf16[128,2048]{1,0:T(8,128)(2,1)S(1)}, u32[]{:S(2)}, u32[]{:S(2)}) collective-permute-start(bf16[128,2048]{1,0:T(8,128)(2,1)S(1)} %constant_dynamic-update-slice_fusion.5.refs_0_), channel_id=1, source_target_pairs={{0,12},{2,14},{4,0},{6,2},{8,4},{10,6},{12,8},{14,10},{16,28},{18,... | collective-permute-start | bytes 1572872 | tf_op jit(solution)/shard_map/ppermute | solution.py:39
  30.7 3.6 %collective-permute-start.13 = (bf16[128,2048]{1,0:T(8,128)(2,1)S(1)}, bf16[128,2048]{1,0:T(8,128)(2,1)}, u32[]{:S(2)}, u32[]{:S(2)}) collective-permute-start(bf16[128,2048]{1,0:T(8,128)(2,1)S(1)} %constant_dynamic-update-slice_fusion.5.refs_0_), channel_id=1, source_target_pairs={{0,2},{2,0},{4,6},{6,4},{8,10},{10,8},{12,14},{14,12},{16,18},{18,... | collective-permute-start | bytes 1572872 | tf_op jit(solution)/shard_map/ppermute | solution.py:39
  34.3 5.3 %collective-permute-done.5.refs_0_ = bf16[128,2048]{1,0:T(8,128)(2,1)S(1)} collective-permute-done((bf16[128,2048]{1,0:T(8,128)(2,1)S(1)}, bf16[128,2048]{1,0:T(8,128)(2,1)S(1)}, u32[]{:S(2)}, u32[]{:S(2)}) %collective-permute-start.5) | collective-permute-done | bytes 524320 | tf_op jit(solution)/shard_map/ppermute | solution.py:39
  39.6 4.0 %collective-permute-start.12 = (bf16[128,2048]{1,0:T(8,128)(2,1)S(1)}, bf16[128,2048]{1,0:T(8,128)(2,1)S(1)}, u32[]{:S(2)}, u32[]{:S(2)}) collective-permute-start(bf16[128,2048]{1,0:T(8,128)(2,1)S(1)} %collective-permute-done.5.refs_0_), channel_id=1, source_target_pairs={{0,2},{2,0},{4,6},{6,4},{8,10},{10,8},{12,14},{14,12},{16,18},{18,... | collective-permute-start | bytes 1572872 | tf_op jit(solution)/shard_map/ppermute | solution.py:39
  43.6 0.0 collective-permute-done.7.refs_0_
  43.6 1.3 %collective-permute-start.8 = (bf16[64,2048]{1,0:T(8,128)(2,1)S(1)}, bf16[64,2048]{1,0:T(8,128)(2,1)S(1)}, u32[]{:S(2)}, u32[]{:S(2)}) collective-permute-start(bf16[64,2048]{1,0:T(8,128)(2,1)S(1)} %slice.9), channel_id=1, source_target_pairs={{0,12},{2,14},{4,0},{6,2},{8,4},{10,6},{12,8},{14,10},{16,28},{18,... | collective-permute-start | bytes 786440 | tf_op jit(solution)/shard_map/ppermute | solution.py:39
  45.0 1.7 %collective-permute-start.11 = (bf16[128,2048]{1,0:T(8,128)(2,1)S(1)}, bf16[128,2048]{1,0:T(8,128)(2,1)S(1)}, u32[]{:S(2)}, u32[]{:S(2)}) collective-permute-start(bf16[128,2048]{1,0:T(8,128)(2,1)S(1)} %collective-permute-done.7.refs_0_), channel_id=1, source_target_pairs={{0,2},{2,0},{4,6},{6,4},{8,10},{10,8},{12,14},{14,12},{16,18},{18,... | collective-permute-start | bytes 1572872 | tf_op jit(solution)/shard_map/ppermute | solution.py:39
  46.7 0.1 collective-permute-start.6
  46.8 5.0 %collective-permute-done.8.refs_1_ = bf16[64,2048]{1,0:T(8,128)(2,1)S(1)} collective-permute-done((bf16[64,2048]{1,0:T(8,128)(2,1)S(1)}, bf16[64,2048]{1,0:T(8,128)(2,1)S(1)}, u32[]{:S(2)}, u32[]{:S(2)}) %collective-permute-start.8) | collective-permute-done | bytes 262176 | tf_op jit(solution)/shard_map/ppermute | solution.py:39
  51.7 0.7 collective-permute-start.10
  52.4 3.6 %collective-permute-done.6.refs_0_ = bf16[64,2048]{1,0:T(8,128)(2,1)} collective-permute-done((bf16[64,2048]{1,0:T(8,128)(2,1)S(1)}, bf16[64,2048]{1,0:T(8,128)(2,1)}, u32[]{:S(2)}, u32[]{:S(2)}) %collective-permute-start.6) | collective-permute-done | bytes 262176 | tf_op jit(solution)/shard_map/ppermute | solution.py:39
  56.0 0.8 collective-permute-start.9
  56.8 0.1 copy.14
  56.9 0.1 copy.18
  57.0 0.1 copy.15.weight_ref
  57.2 0.0 copy-start.4
  57.2 6.8 %shard_map.92.refs_2_.refs_4_ = bf16[2048,1024]{1,0:T(8,128)(2,1)S(1)} custom-call(bf16[64,8,256]{2,1,0:T(8,128)(2,1)S(1)} %copy-done.3, f32[1,256]{1,0:T(1,128)S(1)} %bitcast.35, f32[1,256]{1,0:T(1,128)S(1)} %bitcast.37, bf16[256,32]{1,0:T(8,128)(2,1)S(1)} %copy.15.weight_ref, f32[1,32]{1,0:T(1,128)S(1)} %bitcast.38, bf16[32,4096]{1,0:T(8,128)(2,1)S(1)} %bitcast.29), custom_call_target="tpu_custom_call" | custom-call | tf_op jit(solution)/shard_map/pallas_call | solution.py:164
  64.0 1.9 %copy-done = bf16[2048,1024]{1,0:T(8,128)(2,1)} copy-done((bf16[2048,1024]{1,0:T(8,128)(2,1)}, bf16[2048,1024]{1,0:T(8,128)(2,1)S(1)}, u32[]{:S(2)}) %copy-start) | copy-done | bytes 4194328
  65.9 0.1 stack.75.place_ref
  66.0 0.0 collective-permute-done.13.refs_1_
  66.0 0.0 copy-done.4
  66.1 2.2 %copy-done.1 = bf16[2048,1024]{1,0:T(8,128)(2,1)S(1)} copy-done((bf16[2048,1024]{1,0:T(8,128)(2,1)S(1)}, bf16[2048,1024]{1,0:T(8,128)(2,1)}, u32[]{:S(2)}) %copy-start.1) | copy-done | bytes 4194328
  68.2 3.8 %shard_map.93.refs_4_ = bf16[16,4,2,8,8,128]{5,4,3,2,1,0:T(8,128)(2,1)} custom-call(s32[18]{0:T(128)S(1)} %stack.75.place_ref, bf16[128,2048]{1,0:T(8,128)(2,1)S(1)} %constant_dynamic-update-slice_fusion.5.refs_0_, bf16[128,2048]{1,0:T(8,128)(2,1)} %collective-permute-done.13.refs_1_, bf16[2048,1024]{1,0:T(8,128)(2,1)S(1)} %copy-done.1, f32[1,128]{1,0:T(1,128)S(1)} %bitcast.30), custom_call_target="tpu_custom_call" | custom-call | tf_op jit(solution)/shard_map/pallas_call | solution.py:120
  72.0 0.0 collective-permute-done.12.refs_1_
  72.0 2.7 %shard_map.94.refs_4_ = bf16[16,4,2,8,8,128]{5,4,3,2,1,0:T(8,128)(2,1)} custom-call(s32[18]{0:T(128)S(1)} %stack.75.place_ref, bf16[128,2048]{1,0:T(8,128)(2,1)S(1)} %collective-permute-done.5.refs_0_, bf16[128,2048]{1,0:T(8,128)(2,1)S(1)} %collective-permute-done.12.refs_1_, bf16[2048,1024]{1,0:T(8,128)(2,1)S(1)} %copy-done.1, ...), custom_call_target="tpu_custom_call", output_to_operand_aliasing={{}: (5, {})} | custom-call | tf_op jit(solution)/shard_map/pallas_call | solution.py:120
  74.8 0.0 collective-permute-done.11.refs_1_
  74.8 2.7 %shard_map.95.refs_6_ = bf16[16,4,2,8,8,128]{5,4,3,2,1,0:T(8,128)(2,1)} custom-call(s32[18]{0:T(128)S(1)} %stack.75.place_ref, bf16[128,2048]{1,0:T(8,128)(2,1)S(1)} %collective-permute-done.7.refs_0_, bf16[128,2048]{1,0:T(8,128)(2,1)S(1)} %collective-permute-done.11.refs_1_, bf16[2048,1024]{1,0:T(8,128)(2,1)S(1)} %copy-done.1, ...), custom_call_target="tpu_custom_call", output_to_operand_aliasing={{}: (5, {})} | custom-call | tf_op jit(solution)/shard_map/pallas_call | solution.py:120
  77.5 0.0 collective-permute-done.10.refs_3_
  77.5 0.0 collective-permute-done.9.refs_2_
  77.5 5.5 %shard_map.96 = bf16[16,4,2,8,8,128]{5,4,3,2,1,0:T(8,128)(2,1)} custom-call(s32[18]{0:T(128)S(1)} %stack.75.place_ref, bf16[64,2048]{1,0:T(8,128)(2,1)} %collective-permute-done.6.refs_0_, bf16[64,2048]{1,0:T(8,128)(2,1)S(1)} %collective-permute-done.8.refs_1_, bf16[64,2048]{1,0:T(8,128)(2,1)} %collective-permute-done.9.refs_2_, ...), custom_call_target="tpu_custom_call", output_to_operand_aliasing={{}: (7, {})} | custom-call | tf_op jit(solution)/shard_map/pallas_call | solution.py:120
  (26 shorter events, 0.1 us)
Async XLA Ops:
  0.0 57.0 %copy-start.11 = (bf16[256,32]{0,1:T(8,128)(2,1)S(1)}, bf16[256,32]{0,1:T(8,128)(2,1)}, u32[]{:S(2)}) copy-start(bf16[256,32]{0,1:T(8,128)(2,1)} %param.14) | copy-start | bytes 49156
  1.6 1.0 %copy-start.2 = (bf16[64,8,256]{2,1,0:T(8,128)(2,1)S(1)}, bf16[64,8,256]{2,1,0:T(8,128)(2,1)}, u32[]{:S(2)}) copy-start(bf16[64,8,256]{2,1,0:T(8,128)(2,1)} %feats_ref.3) | copy-start | bytes 786436
  2.5 0.7 copy-start.5
  3.2 0.7 copy-start.7
  3.9 53.3 %copy-start.3 = (bf16[64,8,256]{2,1,0:T(8,128)(2,1)S(1)}, bf16[64,8,256]{2,1,0:T(8,128)(2,1)}, u32[]{:S(2)}) copy-start(bf16[64,8,256]{2,1,0:T(8,128)(2,1)} %feats_ref.3) | copy-start | bytes 786436
  3.9 53.3 %copy-start.6 = (f32[256]{0:T(256)S(1)}, f32[256]{0:T(256)}, u32[]{:S(2)}) copy-start(f32[256]{0:T(256)} %param.10) | copy-start | bytes 3076
  3.9 53.3 %copy-start.8 = (f32[256]{0:T(256)S(1)}, f32[256]{0:T(256)}, u32[]{:S(2)}) copy-start(f32[256]{0:T(256)} %param.11) | copy-start | bytes 3076
  3.9 53.3 %copy-start.9 = (f32[32]{0:T(128)S(1)}, f32[32]{0:T(128)}, u32[]{:S(2)}) copy-start(f32[32]{0:T(128)} %param.15) | copy-start | bytes 388
  4.6 3.9 %collective-permute-start = (bf16[8,2048]{1,0:T(8,128)(2,1)S(1)}, bf16[8,2048]{1,0:T(8,128)(2,1)S(1)}, u32[]{:S(2)}, u32[]{:S(2)}) collective-permute-start(bf16[8,2048]{1,0:T(8,128)(2,1)S(1)} %shard_map.91), channel_id=1, source_target_pairs={{0,16},{2,18},{4,20},{6,22},{8,24},{10,26},{12,28},{14,30},{16,0},... | collective-permute-start | bytes 98312 | tf_op jit(solution)/shard_map/ppermute | solution.py:39
  8.4 48.4 %copy-start.10 = (bf16[1024,128]{1,0:T(8,128)(2,1)S(1)}, bf16[1024,128]{1,0:T(8,128)(2,1)}, u32[]{:S(2)}) copy-start(bf16[1024,128]{1,0:T(8,128)(2,1)} %param.16) | copy-start | bytes 786436
  8.4 10.4 %collective-permute-start.1 = (bf16[16,2048]{1,0:T(8,128)(2,1)S(1)}, bf16[16,2048]{1,0:T(8,128)(2,1)S(1)}, u32[]{:S(2)}, u32[]{:S(2)}) collective-permute-start(bf16[16,2048]{1,0:T(8,128)(2,1)S(1)} %pad_maximum_fusion), channel_id=1, source_target_pairs={{0,64},{2,66},{4,68},{6,70},{8,72},{10,74},{12,76},{14,78},{16,80}... | collective-permute-start | bytes 196616 | tf_op jit(solution)/shard_map/ppermute | solution.py:39
  15.2 5.4 %collective-permute-start.2 = (bf16[16,2048]{1,0:T(8,128)(2,1)S(1)}, bf16[16,2048]{1,0:T(8,128)(2,1)S(1)}, u32[]{:S(2)}, u32[]{:S(2)}) collective-permute-start(bf16[16,2048]{1,0:T(8,128)(2,1)S(1)} %pad_maximum_fusion), channel_id=1, source_target_pairs={{0,32},{2,34},{4,36},{6,38},{8,40},{10,42},{12,44},{14,46},{16,48}... | collective-permute-start | bytes 196616 | tf_op jit(solution)/shard_map/ppermute | solution.py:39
  16.4 5.7 %collective-permute-start.3 = (bf16[16,2048]{1,0:T(8,128)(2,1)S(1)}, bf16[16,2048]{1,0:T(8,128)(2,1)S(1)}, u32[]{:S(2)}, u32[]{:S(2)}) collective-permute-start(bf16[16,2048]{1,0:T(8,128)(2,1)S(1)} %pad_maximum_fusion), channel_id=1, source_target_pairs={{0,96},{2,98},{4,100},{6,102},{8,104},{10,106},{12,108},{14,110},{... | collective-permute-start | bytes 196616 | tf_op jit(solution)/shard_map/ppermute | solution.py:39
  22.2 5.8 %collective-permute-start.4 = (bf16[64,2048]{1,0:T(8,128)(2,1)S(1)}, bf16[64,2048]{1,0:T(8,128)(2,1)S(1)}, u32[]{:S(2)}, u32[]{:S(2)}) collective-permute-start(bf16[64,2048]{1,0:T(8,128)(2,1)S(1)} %get-tuple-element.5), channel_id=1, source_target_pairs={{0,128},{2,130},{4,132},{6,134},{8,136},{10,138},{12,140},{14,142}... | collective-permute-start | bytes 786440 | tf_op jit(solution)/shard_map/ppermute | solution.py:39
  28.0 11.7 %collective-permute-start.5 = (bf16[128,2048]{1,0:T(8,128)(2,1)S(1)}, bf16[128,2048]{1,0:T(8,128)(2,1)S(1)}, u32[]{:S(2)}, u32[]{:S(2)}) collective-permute-start(bf16[128,2048]{1,0:T(8,128)(2,1)S(1)} %constant_dynamic-update-slice_fusion.5.refs_0_), channel_id=1, source_target_pairs={{0,4},{2,6},{4,8},{6,10},{8,12},{10,14},{12,0},{14,2},{16,20},{18,... | collective-permute-start | bytes 1572872 | tf_op jit(solution)/shard_map/ppermute | solution.py:39
  29.3 14.3 %collective-permute-start.7 = (bf16[128,2048]{1,0:T(8,128)(2,1)S(1)}, bf16[128,2048]{1,0:T(8,128)(2,1)S(1)}, u32[]{:S(2)}, u32[]{:S(2)}) collective-permute-start(bf16[128,2048]{1,0:T(8,128)(2,1)S(1)} %constant_dynamic-update-slice_fusion.5.refs_0_), channel_id=1, source_target_pairs={{0,12},{2,14},{4,0},{6,2},{8,4},{10,6},{12,8},{14,10},{16,28},{18,... | collective-permute-start | bytes 1572872 | tf_op jit(solution)/shard_map/ppermute | solution.py:39
  30.7 35.3 %collective-permute-start.13 = (bf16[128,2048]{1,0:T(8,128)(2,1)S(1)}, bf16[128,2048]{1,0:T(8,128)(2,1)}, u32[]{:S(2)}, u32[]{:S(2)}) collective-permute-start(bf16[128,2048]{1,0:T(8,128)(2,1)S(1)} %constant_dynamic-update-slice_fusion.5.refs_0_), channel_id=1, source_target_pairs={{0,2},{2,0},{4,6},{6,4},{8,10},{10,8},{12,14},{14,12},{16,18},{18,... | collective-permute-start | bytes 1572872 | tf_op jit(solution)/shard_map/ppermute | solution.py:39
  39.6 32.4 %collective-permute-start.12 = (bf16[128,2048]{1,0:T(8,128)(2,1)S(1)}, bf16[128,2048]{1,0:T(8,128)(2,1)S(1)}, u32[]{:S(2)}, u32[]{:S(2)}) collective-permute-start(bf16[128,2048]{1,0:T(8,128)(2,1)S(1)} %collective-permute-done.5.refs_0_), channel_id=1, source_target_pairs={{0,2},{2,0},{4,6},{6,4},{8,10},{10,8},{12,14},{14,12},{16,18},{18,... | collective-permute-start | bytes 1572872 | tf_op jit(solution)/shard_map/ppermute | solution.py:39
  43.6 8.1 %collective-permute-start.8 = (bf16[64,2048]{1,0:T(8,128)(2,1)S(1)}, bf16[64,2048]{1,0:T(8,128)(2,1)S(1)}, u32[]{:S(2)}, u32[]{:S(2)}) collective-permute-start(bf16[64,2048]{1,0:T(8,128)(2,1)S(1)} %slice.9), channel_id=1, source_target_pairs={{0,12},{2,14},{4,0},{6,2},{8,4},{10,6},{12,8},{14,10},{16,28},{18,... | collective-permute-start | bytes 786440 | tf_op jit(solution)/shard_map/ppermute | solution.py:39
  45.0 29.8 %collective-permute-start.11 = (bf16[128,2048]{1,0:T(8,128)(2,1)S(1)}, bf16[128,2048]{1,0:T(8,128)(2,1)S(1)}, u32[]{:S(2)}, u32[]{:S(2)}) collective-permute-start(bf16[128,2048]{1,0:T(8,128)(2,1)S(1)} %collective-permute-done.7.refs_0_), channel_id=1, source_target_pairs={{0,2},{2,0},{4,6},{6,4},{8,10},{10,8},{12,14},{14,12},{16,18},{18,... | collective-permute-start | bytes 1572872 | tf_op jit(solution)/shard_map/ppermute | solution.py:39
  46.7 9.3 %collective-permute-start.6 = (bf16[64,2048]{1,0:T(8,128)(2,1)S(1)}, bf16[64,2048]{1,0:T(8,128)(2,1)}, u32[]{:S(2)}, u32[]{:S(2)}) collective-permute-start(bf16[64,2048]{1,0:T(8,128)(2,1)S(1)} %slice.8), channel_id=1, source_target_pairs={{0,4},{2,6},{4,8},{6,10},{8,12},{10,14},{12,0},{14,2},{16,20},{18,... | collective-permute-start | bytes 786440 | tf_op jit(solution)/shard_map/ppermute | solution.py:39
  51.7 25.8 %collective-permute-start.10 = (bf16[64,2048]{1,0:T(8,128)(2,1)S(1)}, bf16[64,2048]{1,0:T(8,128)(2,1)}, u32[]{:S(2)}, u32[]{:S(2)}) collective-permute-start(bf16[64,2048]{1,0:T(8,128)(2,1)S(1)} %collective-permute-done.8.refs_1_), channel_id=1, source_target_pairs={{0,2},{2,0},{4,6},{6,4},{8,10},{10,8},{12,14},{14,12},{16,18},{18,... | collective-permute-start | bytes 786440 | tf_op jit(solution)/shard_map/ppermute | solution.py:39
  56.0 21.5 %collective-permute-start.9 = (bf16[64,2048]{1,0:T(8,128)(2,1)}, bf16[64,2048]{1,0:T(8,128)(2,1)}, u32[]{:S(2)}, u32[]{:S(2)}) collective-permute-start(bf16[64,2048]{1,0:T(8,128)(2,1)} %collective-permute-done.6.refs_0_), channel_id=1, source_target_pairs={{0,2},{2,0},{4,6},{6,4},{8,10},{10,8},{12,14},{14,12},{16,18},{18,... | collective-permute-start | bytes 786440 | tf_op jit(solution)/shard_map/ppermute | solution.py:39
  57.2 8.8 %copy-start.4 = (f32[128]{0:T(128)S(1)}, f32[128]{0:T(128)}, u32[]{:S(2)}) copy-start(f32[128]{0:T(128)} %param.17) | copy-start | bytes 1540
  64.0 2.0 %copy-start = (bf16[2048,1024]{1,0:T(8,128)(2,1)}, bf16[2048,1024]{1,0:T(8,128)(2,1)S(1)}, u32[]{:S(2)}) copy-start(bf16[2048,1024]{1,0:T(8,128)(2,1)S(1)} %shard_map.92.refs_2_.refs_4_) | copy-start | bytes 12582916
  66.0 2.2 %copy-start.1 = (bf16[2048,1024]{1,0:T(8,128)(2,1)S(1)}, bf16[2048,1024]{1,0:T(8,128)(2,1)}, u32[]{:S(2)}) copy-start(bf16[2048,1024]{1,0:T(8,128)(2,1)} %copy-done) | copy-start | bytes 12582916

commit v3 on v2

--- a/solution.py
+++ b/solution.py
@@ -35,6 +35,10 @@
 CORE_PAIR = shift(lambda y, z, x, c: (y, z, x, c + 1))
 
 
+def cost(flops, bytes_accessed):
+    return pl.CostEstimate(flops=flops, bytes_accessed=bytes_accessed, transcendentals=0)
+
+
 def send(block, pairs):
     return lax.ppermute(block, "dap", pairs)
 
@@ -44,6 +48,10 @@
     center = jnp.mean(values, axis=-1, keepdims=True)
     spread = jnp.mean((values - center) ** 2, axis=-1, keepdims=True)
     return (values - center) * lax.rsqrt(spread + 1e-05) * gain + offset
+
+
+def dot_last(a, b):
+    return lax.dot_general(a, b, (((1,), (1,)), ((), ())), preferred_element_type=jnp.float32)
 
 
 def left_kernel(feats_ref, gain_ref, offset_ref, weight_ref, bias_ref, left_ref):
@@ -53,12 +61,13 @@
     normed = normed.reshape(groups, PACK, rows, -1)
     wide = jnp.concatenate([normed[:, k] for k in range(PACK)], axis=-1)
     wide = wide.reshape(groups * rows, -1).astype(jnp.bfloat16)
-    weight = jnp.concatenate([weight_ref[...].astype(jnp.float32)] * PACK, axis=1)
-    lane = lax.broadcasted_iota(jnp.int32, weight.shape, 1) // HID
+    weight = jnp.concatenate([weight_ref[...].astype(jnp.float32)] * PACK, axis=0)
+    turn = lax.broadcasted_iota(jnp.int32, weight.shape, 0) // HID
     diagonal = jnp.concatenate(
-        [jnp.where(lane == k, weight, 0.0) for k in range(PACK)], axis=0
+        [jnp.where(turn == k, weight, 0.0) for k in range(PACK)], axis=1
     ).astype(jnp.bfloat16)
-    out = jnp.dot(wide, diagonal, preferred_element_type=jnp.float32) + bias_ref[...]
+    bias = jnp.concatenate([bias_ref[...]] * PACK, axis=1)
+    out = dot_last(wide, diagonal) + bias
     for g in range(groups):
         left_ref[:, g * PACK * HID : (g + 1) * PACK * HID] = out[
             g * rows : (g + 1) * rows
@@ -69,7 +78,7 @@
     rows = feats_ref.shape[1]
     normed = layer_norm(feats_ref[...], gain_ref[...], offset_ref[...])
     normed = normed.reshape(SEQS * rows, -1).astype(jnp.bfloat16)
-    right = jnp.dot(normed, weight_ref[...], preferred_element_type=jnp.float32) + bias_ref[...]
+    right = dot_last(normed, weight_ref[...]) + bias_ref[...]
     right_ref[...] = right.astype(jnp.bfloat16)
     step = 2
 
@@ -95,20 +104,19 @@
 def pair_kernel(place_ref, *refs, pieces, aliased):
     lefts = refs[: len(pieces)]
     table_ref, bias_ref = refs[len(pieces) : len(pieces) + 2]
-    out_ref, acc_ref = refs[len(pieces) + 2 + aliased :]
+    out_ref, left_all, acc_ref = refs[len(pieces) + 2 + aliased :]
     core = place_ref[1]
-    for left_ref, (lane, first) in zip(lefts, pieces):
-        rows = left_ref.shape[0]
-        acc = acc_ref.at[pl.ds(0, rows)]
-        acc[...] = jnp.dot(left_ref[...], table_ref[...], preferred_element_type=jnp.float32)
+    lanes = out_ref.shape[2]
+    rows = lefts[0].shape[0]
+    for k, left_ref in enumerate(lefts):
+        left_all[k * rows : (k + 1) * rows, :] = left_ref[...]
+    acc_ref[...] = jnp.dot(left_all[...], table_ref[...], preferred_element_type=jnp.float32)
+    for n, (lane, first) in enumerate(pieces):
         c = core if lane == 0 else 1 - core
-
-        def body(k, carry, first=first, c=c):
-            part = acc_ref[pl.ds(pl.multiple_of(k * 8, 8), 8), :].reshape(8, 8, C_Z) + bias_ref[...]
-            out_ref[place_ref[2 + first + k], 0, c] = part.astype(jnp.bfloat16)
-            return carry
-
-        lax.fori_loop(0, rows // 8, body, 0, unroll=True)
+        for k in range(rows // 8):
+            at = n * rows + k * 8
+            part = acc_ref[at : at + 8, :].reshape(8, 8, C_Z) + bias_ref[...]
+            out_ref[place_ref[2 + first + k], 0, c if lanes == NC else 0] = part.astype(jnp.bfloat16)
 
 
 def pair_block(place, lefts, pieces, table, bias, turn, out):
@@ -116,7 +124,12 @@
     whole = pl.BlockSpec(memory_space=pltpu.VMEM)
     operands = [*lefts, table, bias] + ([out] if aliased else [])
     in_specs = [whole] * (len(lefts) + 2) + ([pl.BlockSpec(memory_space=pl.ANY)] if aliased else [])
-    rows = max(left.shape[0] for left in lefts)
+    rows = sum(left.shape[0] for left in lefts)
+    lanes = sorted({lane for lane, _ in pieces})
+    if len(lanes) == NC:
+        turn_lane = lambda place: 0
+    else:
+        turn_lane = lambda place: lax.rem(place[1] + lanes[0], NC)
     return pl.pallas_call(
         functools.partial(pair_kernel, pieces=pieces, aliased=int(aliased)),
         grid_spec=pltpu.PrefetchScalarGridSpec(
@@ -124,14 +137,18 @@
             grid=(1,),
             in_specs=in_specs,
             out_specs=pl.BlockSpec(
-                (NY * NZ, 1, NC, 8, 8, C_Z),
-                lambda i, place: (0, lax.rem(place[0] + turn, NX), 0, 0, 0, 0),
+                (NY * NZ, 1, len(lanes), 8, 8, C_Z),
+                lambda i, place: (0, lax.rem(place[0] + turn, NX), turn_lane(place), 0, 0, 0),
             ),
-            scratch_shapes=[pltpu.VMEM((rows, 8 * C_Z), jnp.float32)],
+            scratch_shapes=[
+                pltpu.VMEM((rows, SEQS * HID), jnp.bfloat16),
+                pltpu.VMEM((rows, 8 * C_Z), jnp.float32),
+            ],
         ),
         out_shape=jax.ShapeDtypeStruct((NY * NZ, NX, NC, 8, 8, C_Z), jnp.bfloat16),
         input_output_aliases={len(operands): 0} if aliased else {},
         compiler_params=pltpu.CompilerParams(vmem_limit_bytes=24 * 1024 * 1024),
+        cost_estimate=cost(2 * rows * 2048 * 1024, 10 << 20),
     )(place, *operands)
 
 
@@ -152,13 +169,13 @@
     left = pl.pallas_call(
         left_kernel,
         out_shape=jax.ShapeDtypeStruct((rows, SEQS * HID), jnp.bfloat16),
-        compiler_params=vmem,
+        compiler_params=pltpu.CompilerParams(vmem_limit_bytes=60 * 1024 * 1024),
     )(
         alignment_features,
         gain,
         offset,
-        left_projection_weight,
-        jnp.tile(left_projection_bias, PACK)[None],
+        left_projection_weight.T,
+        left_projection_bias[None],
     )
     out_weight = output_weight.reshape(HID, HID, C_Z).transpose(1, 0, 2).reshape(HID, HID * C_Z)
     table = pl.pallas_call(
@@ -166,11 +183,12 @@
         out_shape=jax.ShapeDtypeStruct((SEQS * HID, rows * C_Z), jnp.bfloat16),
         scratch_shapes=[pltpu.VMEM((SEQS * rows, HID), jnp.bfloat16)],
         compiler_params=vmem,
+        cost_estimate=cost(1 << 30, 24 << 20),
     )(
         alignment_features,
         gain,
         offset,
-        right_projection_weight,
+        right_projection_weight.T,
         right_projection_bias[None],
         out_weight,
     )
@@ -190,16 +208,21 @@
     ring = jnp.concatenate([pair] + [send(pair, Z_PLUS[k]) for k in (4, 2, 6)], axis=0)
     block = jnp.concatenate([ring, send(ring, Y_PAIR)], axis=0)
 
-    def both(blocks):
-        return blocks + [send(b, CORE_PAIR) for b in blocks]
-
-    out = pair_block(place, both([block]), [(0, 0), (1, 0)], table, bias, 0, None)
+    def other(blocks):
+        return [send(b, CORE_PAIR) for b in blocks]
+
+    whole = [(0, 0), (1, 0)]
     low, high = send(block, X_PLUS[1]), send(block, X_PLUS[3])
+    out = pair_block(place, [block] + other([block]), whole, table, bias, 0, None)
+    low, high, table, out = lax.optimization_barrier((low, high, table, out))
     half = block.shape[0] // 2
     far = [send(low[:half], X_PLUS[1]), send(high[half:], X_PLUS[3])]
-    out = pair_block(place, both([low]), [(0, 0), (1, 0)], table, bias, 3, out)
-    out = pair_block(place, both([high]), [(0, 0), (1, 0)], table, bias, 1, out)
-    out = pair_block(place, both(far), [(0, 0), (0, 8), (1, 0), (1, 8)], table, bias, 2, out)
+    out = pair_block(place, [low] + other([low]), whole, table, bias, 3, out)
+    out = pair_block(place, [high] + other([high]), whole, table, bias, 1, out)
+    far[0], far[1], out = lax.optimization_barrier((far[0], far[1], out))
+    far_other = other(far)
+    out = pair_block(place, far, [(0, 0), (0, 8)], table, bias, 2, out)
+    out = pair_block(place, far_other, [(1, 0), (1, 8)], table, bias, 2, out)
     return out.reshape(NY * NZ * NX * NC * 8, 8, C_Z)
 
 

time: 83.3 us -> 59.4 us (0.71)
  waiting for transfers between devices: 22.9 us -> 10.8 us
  local copies, waits for them, and re-layouts: 8.57 us -> 1.23 us
  starting transfers between devices: 29.2 us -> 25.2 us
  Pallas kernels: 22.1 us -> 21 us
    ppermute x14, waiting for transfers between devices: 22.9 us -> 10.8 us  [send(): return lax.ppermute(block, 'dap', pairs)]
    unnamed x31 -> x19, local copies, waits for them, and re-layouts: 7.57 us -> 0.96 us
    ppermute x14, starting transfers between devices: 29.2 us -> 25.2 us  [send(): return lax.ppermute(block, 'dap', pairs)]
    pallas_call x4 -> x5, Pallas kernels: 14.8 us -> 12.2 us  [pair_block(): pl.pallas_call(functools.partial(pair_kernel, pieces=pieces, aliased=int(...]
    pallas_call x1, Pallas kernels: 0.63 us -> 2.06 us  [per_device(): pl.pallas_call(left_kernel, out_shape=jax.ShapeDtypeStruct((rows, SEQS *...]
  transfers between devices with their start and end apart: 14 -> 14, of which waited for: 7 -> 6; matrix products, arithmetic and copies ran while one was open for 1% -> 2% of each run, Pallas kernels for 19% -> 28%
where the time goes in v3:
time: 59.4 us; the launch traced here: 59.2 us
  starting transfers between devices  25.2 us (42%)
  Pallas kernels  21 us (35%)
  waiting for transfers between devices  10.8 us (18%)
  local copies, waits for them, and re-layouts  1.23 us (2%)
  other arithmetic  0.77 us (1%)
    ppermute x14, starting transfers between devices, send(): return lax.ppermute(block, 'dap', pairs)  25.2 us
    pallas_call x5, Pallas kernels, pair_block(): pl.pallas_call(functools.partial(pair_kernel, pieces=pieces, aliased=int(...  12.2 us
    ppermute x14, waiting for transfers between devices, send(): return lax.ppermute(block, 'dap', pairs)  10.8 us
    pallas_call x1, Pallas kernels, per_device(): pl.pallas_call(table_kernel, out_shape=jax.ShapeDtypeStruct((SEQS * HID,...  6.75 us
    pallas_call x1, Pallas kernels, per_device(): pl.pallas_call(left_kernel, out_shape=jax.ShapeDtypeStruct((rows, SEQS *...  2.06 us
  transfers between devices with their start and end apart: 14, of which 6 were waited for; matrix products, arithmetic and copies ran while one was open for 2% of the time, Pallas kernels for 28%

profile of v3, /device:TPU:1, one launch (start us, length us, event | category | flops | bytes accessed | tf_op | source)
XLA Modules:
  0.0 59.2 jit_solution(13052785138851144294)
XLA Ops:
  0.0 0.0 copy-start.6
  0.0 0.0 copy-start.1
  0.0 0.0 copy-start.5
  0.0 2.1 %shard_map.91 = bf16[8,2048]{1,0:T(8,128)(2,1)} custom-call(bf16[64,8,256]{2,1,0:T(8,128)(2,1)} %feats_ref.3, f32[1,256]{1,0:T(1,128)} %bitcast.39, f32[1,256]{1,0:T(1,128)} %bitcast.41, bf16[32,256]{1,0:T(8,128)(2,1)} %bitcast.46, f32[1,32]{1,0:T(1,128)} %bitcast.47), custom_call_target="tpu_custom_call" | custom-call | tf_op jit(solution)/shard_map/pallas_call | solution.py:169
  2.1 2.5 %collective-permute-start = (bf16[8,2048]{1,0:T(8,128)(2,1)}, bf16[8,2048]{1,0:T(8,128)(2,1)S(1)}, u32[]{:S(2)}, u32[]{:S(2)}) collective-permute-start(bf16[8,2048]{1,0:T(8,128)(2,1)} %shard_map.91), channel_id=1, source_target_pairs={{0,16},{2,18},{4,20},{6,22},{8,24},{10,26},{12,28},{14,30},{16,0},... | collective-permute-start | bytes 98312 | tf_op jit(solution)/shard_map/ppermute | solution.py:43
  4.6 0.8 %constant_dynamic-update-slice_fusion.4 = (bf16[64,2048]{1,0:T(8,128)(2,1)S(1)}, bf16[128,2048]{1,0:T(8,128)(2,1)S(1)}) fusion(bf16[8,2048]{1,0:T(8,128)(2,1)} %shard_map.91), kind=kLoop, calls=%fused_computation.6 | loop fusion | bytes 98304
  5.4 0.7 %collective-permute-done = bf16[8,2048]{1,0:T(8,128)(2,1)S(1)} collective-permute-done((bf16[8,2048]{1,0:T(8,128)(2,1)}, bf16[8,2048]{1,0:T(8,128)(2,1)S(1)}, u32[]{:S(2)}, u32[]{:S(2)}) %collective-permute-start) | collective-permute-done | bytes 32800 | tf_op jit(solution)/shard_map/ppermute | solution.py:43
  6.1 0.8 %pad_maximum_fusion = bf16[16,2048]{1,0:T(8,128)(2,1)S(1)} fusion(bf16[8,2048]{1,0:T(8,128)(2,1)S(1)} %collective-permute-done, bf16[8,2048]{1,0:T(8,128)(2,1)} %shard_map.91), kind=kLoop, calls=%fused_computation.1 | loop fusion | flops 131072 | bytes 131072 | tf_op jit(solution)/shard_map/concatenate | solution.py:207
  6.8 6.7 %collective-permute-start.1 = (bf16[16,2048]{1,0:T(8,128)(2,1)S(1)}, bf16[16,2048]{1,0:T(8,128)(2,1)S(1)}, u32[]{:S(2)}, u32[]{:S(2)}) collective-permute-start(bf16[16,2048]{1,0:T(8,128)(2,1)S(1)} %pad_maximum_fusion), channel_id=1, source_target_pairs={{0,64},{2,66},{4,68},{6,70},{8,72},{10,74},{12,76},{14,78},{16,80}... | collective-permute-start | bytes 196616 | tf_op jit(solution)/shard_map/ppermute | solution.py:43
  13.6 1.2 %collective-permute-start.2 = (bf16[16,2048]{1,0:T(8,128)(2,1)S(1)}, bf16[16,2048]{1,0:T(8,128)(2,1)S(1)}, u32[]{:S(2)}, u32[]{:S(2)}) collective-permute-start(bf16[16,2048]{1,0:T(8,128)(2,1)S(1)} %pad_maximum_fusion), channel_id=1, source_target_pairs={{0,32},{2,34},{4,36},{6,38},{8,40},{10,42},{12,44},{14,46},{16,48}... | collective-permute-start | bytes 196616 | tf_op jit(solution)/shard_map/ppermute | solution.py:43
  14.8 2.4 %collective-permute-start.3 = (bf16[16,2048]{1,0:T(8,128)(2,1)S(1)}, bf16[16,2048]{1,0:T(8,128)(2,1)S(1)}, u32[]{:S(2)}, u32[]{:S(2)}) collective-permute-start(bf16[16,2048]{1,0:T(8,128)(2,1)S(1)} %pad_maximum_fusion), channel_id=1, source_target_pairs={{0,96},{2,98},{4,100},{6,102},{8,104},{10,106},{12,108},{14,110},{... | collective-permute-start | bytes 196616 | tf_op jit(solution)/shard_map/ppermute | solution.py:43
  17.2 0.0 collective-permute-done.1
  17.2 1.8 %collective-permute-done.2 = bf16[16,2048]{1,0:T(8,128)(2,1)S(1)} collective-permute-done((bf16[16,2048]{1,0:T(8,128)(2,1)S(1)}, bf16[16,2048]{1,0:T(8,128)(2,1)S(1)}, u32[]{:S(2)}, u32[]{:S(2)}) %collective-permute-start.2) | collective-permute-done | bytes 65568 | tf_op jit(solution)/shard_map/ppermute | solution.py:43
  19.0 1.5 %collective-permute-done.3 = bf16[16,2048]{1,0:T(8,128)(2,1)S(1)} collective-permute-done((bf16[16,2048]{1,0:T(8,128)(2,1)S(1)}, bf16[16,2048]{1,0:T(8,128)(2,1)S(1)}, u32[]{:S(2)}, u32[]{:S(2)}) %collective-permute-start.3) | collective-permute-done | bytes 65568 | tf_op jit(solution)/shard_map/ppermute | solution.py:43
  20.5 1.4 %collective-permute-start.4 = (bf16[64,2048]{1,0:T(8,128)(2,1)S(1)}, bf16[64,2048]{1,0:T(8,128)(2,1)S(1)}, u32[]{:S(2)}, u32[]{:S(2)}) collective-permute-start(bf16[64,2048]{1,0:T(8,128)(2,1)S(1)} %get-tuple-element.19), channel_id=1, source_target_pairs={{0,128},{2,130},{4,132},{6,134},{8,136},{10,138},{12,140},{14,142}... | collective-permute-start | bytes 786440 | tf_op jit(solution)/shard_map/ppermute | solution.py:43
  21.9 4.4 %collective-permute-done.4 = bf16[64,2048]{1,0:T(8,128)(2,1)S(1)} collective-permute-done((bf16[64,2048]{1,0:T(8,128)(2,1)S(1)}, bf16[64,2048]{1,0:T(8,128)(2,1)S(1)}, u32[]{:S(2)}, u32[]{:S(2)}) %collective-permute-start.4) | collective-permute-done | bytes 262176 | tf_op jit(solution)/shard_map/ppermute | solution.py:43
  26.3 3.1 %collective-permute-start.7 = (bf16[128,2048]{1,0:T(8,128)(2,1)S(1)}, bf16[128,2048]{1,0:T(8,128)(2,1)S(1)}, u32[]{:S(2)}, u32[]{:S(2)}) collective-permute-start(bf16[128,2048]{1,0:T(8,128)(2,1)S(1)} %constant_dynamic-update-slice_fusion.5.refs_0_), channel_id=1, source_target_pairs={{0,2},{2,0},{4,6},{6,4},{8,10},{10,8},{12,14},{14,12},{16,18},{18,... | collective-permute-start | bytes 1572872 | tf_op jit(solution)/shard_map/ppermute | solution.py:43
  29.4 1.2 %collective-permute-start.5 = (bf16[128,2048]{1,0:T(8,128)(2,1)S(1)}, bf16[128,2048]{1,0:T(8,128)(2,1)S(1)}, u32[]{:S(2)}, u32[]{:S(2)}) collective-permute-start(bf16[128,2048]{1,0:T(8,128)(2,1)S(1)} %constant_dynamic-update-slice_fusion.5.refs_0_), channel_id=1, source_target_pairs={{0,4},{2,6},{4,8},{6,10},{8,12},{10,14},{12,0},{14,2},{16,20},{18,... | collective-permute-start | bytes 1572872 | tf_op jit(solution)/shard_map/ppermute | solution.py:43
  30.7 1.5 %collective-permute-start.6 = (bf16[128,2048]{1,0:T(8,128)(2,1)S(1)}, bf16[128,2048]{1,0:T(8,128)(2,1)S(1)}, u32[]{:S(2)}, u32[]{:S(2)}) collective-permute-start(bf16[128,2048]{1,0:T(8,128)(2,1)S(1)} %constant_dynamic-update-slice_fusion.5.refs_0_), channel_id=1, source_target_pairs={{0,12},{2,14},{4,0},{6,2},{8,4},{10,6},{12,8},{14,10},{16,28},{18,... | collective-permute-start | bytes 1572872 | tf_op jit(solution)/shard_map/ppermute | solution.py:43
  32.1 0.0 copy-done.6
  32.1 0.1 copy.14
  32.2 0.1 copy.17
  32.4 0.1 stack.75.place_ref
  32.5 0.0 copy-done.3
  32.5 0.0 copy-done.4
  32.5 0.0 copy-done
  32.5 0.0 copy-start.2
  32.5 6.8 %shard_map.92.refs_2_ = bf16[2048,1024]{1,0:T(8,128)(2,1)S(1)} custom-call(bf16[64,8,256]{2,1,0:T(8,128)(2,1)S(1)} %copy-done, f32[1,256]{1,0:T(1,128)S(1)} %bitcast.40, f32[1,256]{1,0:T(1,128)S(1)} %bitcast.42, bf16[32,256]{1,0:T(8,128)(2,1)S(1)} %bitcast.33, f32[1,32]{1,0:T(1,128)S(1)} %bitcast.43, bf16[32,4096]{1,0:T(8,128)(2,1)S(1)} %bitcast.32), custom_call_target="tpu_custom_call" | custom-call | flops 1073741824 | bytes 25165824 | tf_op jit(solution)/shard_map/pallas_call | solution.py:181
  39.3 0.0 collective-permute-done.7.refs_1_
  39.3 2.7 %shard_map.93.refs_4_ = bf16[16,4,2,8,8,128]{5,4,3,2,1,0:T(8,128)(2,1)} custom-call(s32[18]{0:T(128)S(1)} %stack.75.place_ref, bf16[128,2048]{1,0:T(8,128)(2,1)S(1)} %constant_dynamic-update-slice_fusion.5.refs_0_, bf16[128,2048]{1,0:T(8,128)(2,1)S(1)} %collective-permute-done.7.refs_1_, bf16[2048,1024]{1,0:T(8,128)(2,1)S(1)} %shard_map.92.refs_2_, ...), custom_call_target="tpu_custom_call" | custom-call | flops 1073741824 | bytes 10485760 | tf_op jit(solution)/shard_map/pallas_call | solution.py:133
  42.0 2.1 %collective-permute-done.5.refs_0_ = bf16[128,2048]{1,0:T(8,128)(2,1)S(1)} collective-permute-done((bf16[128,2048]{1,0:T(8,128)(2,1)S(1)}, bf16[128,2048]{1,0:T(8,128)(2,1)S(1)}, u32[]{:S(2)}, u32[]{:S(2)}) %collective-permute-start.5) | collective-permute-done | bytes 524320 | tf_op jit(solution)/shard_map/ppermute | solution.py:43
  44.1 0.0 collective-permute-done.6.refs_0_
  44.1 0.9 %collective-permute-start.11 = (bf16[128,2048]{1,0:T(8,128)(2,1)S(1)}, bf16[128,2048]{1,0:T(8,128)(2,1)S(1)}, u32[]{:S(2)}, u32[]{:S(2)}) collective-permute-start(bf16[128,2048]{1,0:T(8,128)(2,1)S(1)} %collective-permute-done.5.refs_0_), channel_id=1, source_target_pairs={{0,2},{2,0},{4,6},{6,4},{8,10},{10,8},{12,14},{14,12},{16,18},{18,... | collective-permute-start | bytes 1572872 | tf_op jit(solution)/shard_map/ppermute | solution.py:43
  45.0 0.0 collective-permute-start.10
  45.1 1.3 %collective-permute-start.8 = (bf16[64,2048]{1,0:T(8,128)(2,1)S(1)}, bf16[64,2048]{1,0:T(8,128)(2,1)S(1)}, u32[]{:S(2)}, u32[]{:S(2)}) collective-permute-start(bf16[64,2048]{1,0:T(8,128)(2,1)S(1)} %slice.6), channel_id=1, source_target_pairs={{0,4},{2,6},{4,8},{6,10},{8,12},{10,14},{12,0},{14,2},{16,20},{18,... | collective-permute-start | bytes 786440 | tf_op jit(solution)/shard_map/ppermute | solution.py:43
  46.3 1.7 %collective-permute-start.9 = (bf16[64,2048]{1,0:T(8,128)(2,1)S(1)}, bf16[64,2048]{1,0:T(8,128)(2,1)S(1)}, u32[]{:S(2)}, u32[]{:S(2)}) collective-permute-start(bf16[64,2048]{1,0:T(8,128)(2,1)S(1)} %slice.7), channel_id=1, source_target_pairs={{0,12},{2,14},{4,0},{6,2},{8,4},{10,6},{12,8},{14,10},{16,28},{18,... | collective-permute-start | bytes 786440 | tf_op jit(solution)/shard_map/ppermute | solution.py:43
  48.1 0.0 collective-permute-done.11.refs_1_
  48.1 2.7 %shard_map.94.refs_4_ = bf16[16,4,2,8,8,128]{5,4,3,2,1,0:T(8,128)(2,1)} custom-call(s32[18]{0:T(128)S(1)} %stack.75.place_ref, bf16[128,2048]{1,0:T(8,128)(2,1)S(1)} %collective-permute-done.5.refs_0_, bf16[128,2048]{1,0:T(8,128)(2,1)S(1)} %collective-permute-done.11.refs_1_, ...), custom_call_target="tpu_custom_call", output_to_operand_aliasing={{}: (5, {})} | custom-call | flops 1073741824 | bytes 10485760 | tf_op jit(solution)/shard_map/pallas_call | solution.py:133
  50.8 0.0 collective-permute-done.10.refs_1_
  50.8 2.7 %shard_map.95.refs_4_ = bf16[16,4,2,8,8,128]{5,4,3,2,1,0:T(8,128)(2,1)} custom-call(s32[18]{0:T(128)S(1)} %stack.75.place_ref, bf16[128,2048]{1,0:T(8,128)(2,1)S(1)} %collective-permute-done.6.refs_0_, bf16[128,2048]{1,0:T(8,128)(2,1)S(1)} %collective-permute-done.10.refs_1_, ...), custom_call_target="tpu_custom_call", output_to_operand_aliasing={{}: (5, {})} | custom-call | flops 1073741824 | bytes 10485760 | tf_op jit(solution)/shard_map/pallas_call | solution.py:133
  53.5 0.2 collective-permute-done.8.refs_0_
  53.7 0.0 collective-permute-done.9.refs_1_
  53.7 1.4 %collective-permute-start.12 = (bf16[64,2048]{1,0:T(8,128)(2,1)S(1)}, bf16[64,2048]{1,0:T(8,128)(2,1)S(1)}, u32[]{:S(2)}, u32[]{:S(2)}) collective-permute-start(bf16[64,2048]{1,0:T(8,128)(2,1)S(1)} %collective-permute-done.8.refs_0_), channel_id=1, source_target_pairs={{0,2},{2,0},{4,6},{6,4},{8,10},{10,8},{12,14},{14,12},{16,18},{18,... | collective-permute-start | bytes 786440 | tf_op jit(solution)/shard_map/ppermute | solution.py:43
  55.1 0.0 collective-permute-start.13
  55.1 2.0 %shard_map.96.refs_4_ = bf16[16,4,2,8,8,128]{5,4,3,2,1,0:T(8,128)(2,1)} custom-call(s32[18]{0:T(128)S(1)} %stack.75.place_ref, bf16[64,2048]{1,0:T(8,128)(2,1)S(1)} %collective-permute-done.8.refs_0_, bf16[64,2048]{1,0:T(8,128)(2,1)S(1)} %collective-permute-done.9.refs_1_, bf16[2048,1024]{1,0:T(8,128)(2,1)S(1)} %shard_map.92.refs_2_, ...), custom_call_target="tpu_custom_call", output_to_operand_aliasing={{}: (5, {})} | custom-call | flops 536870912 | bytes 10485760 | tf_op jit(solution)/shard_map/pallas_call | solution.py:133
  57.1 0.0 collective-permute-done.12.refs_0_
  57.1 0.0 collective-permute-done.13.refs_1_
  57.1 2.0 %shard_map.97 = bf16[16,4,2,8,8,128]{5,4,3,2,1,0:T(8,128)(2,1)} custom-call(s32[18]{0:T(128)S(1)} %stack.75.place_ref, bf16[64,2048]{1,0:T(8,128)(2,1)S(1)} %collective-permute-done.12.refs_0_, bf16[64,2048]{1,0:T(8,128)(2,1)S(1)} %collective-permute-done.13.refs_1_, bf16[2048,1024]{1,0:T(8,128)(2,1)S(1)} %shard_map.92.refs_2_, ...), custom_call_target="tpu_custom_call", output_to_operand_aliasing={{}: (5, {})} | custom-call | flops 536870912 | bytes 10485760 | tf_op jit(solution)/shard_map/pallas_call | solution.py:133
  (13 shorter events, 0.1 us)
Async XLA Ops:
  0.0 32.5 %copy-start.3 = (f32[256]{0:T(256)S(1)}, f32[256]{0:T(256)}, u32[]{:S(2)}) copy-start(f32[256]{0:T(256)} %param.10) | copy-start | bytes 3076
  0.0 32.5 %copy-start.4 = (f32[256]{0:T(256)S(1)}, f32[256]{0:T(256)}, u32[]{:S(2)}) copy-start(f32[256]{0:T(256)} %param.11) | copy-start | bytes 3076
  0.0 32.5 %copy-start = (bf16[64,8,256]{2,1,0:T(8,128)(2,1)S(1)}, bf16[64,8,256]{2,1,0:T(8,128)(2,1)}, u32[]{:S(2)}) copy-start(bf16[64,8,256]{2,1,0:T(8,128)(2,1)} %feats_ref.3) | copy-start | bytes 786436
  0.0 32.1 %copy-start.6 = (bf16[1024,128]{1,0:T(8,128)(2,1)S(1)}, bf16[1024,128]{1,0:T(8,128)(2,1)}, u32[]{:S(2)}) copy-start(bf16[1024,128]{1,0:T(8,128)(2,1)} %param.16) | copy-start | bytes 786436
  0.0 32.5 %copy-start.1 = (bf16[256,32]{0,1:T(8,128)(2,1)S(1)}, bf16[256,32]{0,1:T(8,128)(2,1)}, u32[]{:S(2)}) copy-start(bf16[256,32]{0,1:T(8,128)(2,1)} %param.14) | copy-start | bytes 49156
  0.0 32.5 %copy-start.5 = (f32[32]{0:T(128)S(1)}, f32[32]{0:T(128)}, u32[]{:S(2)}) copy-start(f32[32]{0:T(128)} %param.15) | copy-start | bytes 388
  2.1 4.0 %collective-permute-start = (bf16[8,2048]{1,0:T(8,128)(2,1)}, bf16[8,2048]{1,0:T(8,128)(2,1)S(1)}, u32[]{:S(2)}, u32[]{:S(2)}) collective-permute-start(bf16[8,2048]{1,0:T(8,128)(2,1)} %shard_map.91), channel_id=1, source_target_pairs={{0,16},{2,18},{4,20},{6,22},{8,24},{10,26},{12,28},{14,30},{16,0},... | collective-permute-start | bytes 98312 | tf_op jit(solution)/shard_map/ppermute | solution.py:43
  6.8 10.3 %collective-permute-start.1 = (bf16[16,2048]{1,0:T(8,128)(2,1)S(1)}, bf16[16,2048]{1,0:T(8,128)(2,1)S(1)}, u32[]{:S(2)}, u32[]{:S(2)}) collective-permute-start(bf16[16,2048]{1,0:T(8,128)(2,1)S(1)} %pad_maximum_fusion), channel_id=1, source_target_pairs={{0,64},{2,66},{4,68},{6,70},{8,72},{10,74},{12,76},{14,78},{16,80}... | collective-permute-start | bytes 196616 | tf_op jit(solution)/shard_map/ppermute | solution.py:43
  13.6 5.4 %collective-permute-start.2 = (bf16[16,2048]{1,0:T(8,128)(2,1)S(1)}, bf16[16,2048]{1,0:T(8,128)(2,1)S(1)}, u32[]{:S(2)}, u32[]{:S(2)}) collective-permute-start(bf16[16,2048]{1,0:T(8,128)(2,1)S(1)} %pad_maximum_fusion), channel_id=1, source_target_pairs={{0,32},{2,34},{4,36},{6,38},{8,40},{10,42},{12,44},{14,46},{16,48}... | collective-permute-start | bytes 196616 | tf_op jit(solution)/shard_map/ppermute | solution.py:43
  14.8 5.7 %collective-permute-start.3 = (bf16[16,2048]{1,0:T(8,128)(2,1)S(1)}, bf16[16,2048]{1,0:T(8,128)(2,1)S(1)}, u32[]{:S(2)}, u32[]{:S(2)}) collective-permute-start(bf16[16,2048]{1,0:T(8,128)(2,1)S(1)} %pad_maximum_fusion), channel_id=1, source_target_pairs={{0,96},{2,98},{4,100},{6,102},{8,104},{10,106},{12,108},{14,110},{... | collective-permute-start | bytes 196616 | tf_op jit(solution)/shard_map/ppermute | solution.py:43
  20.5 5.8 %collective-permute-start.4 = (bf16[64,2048]{1,0:T(8,128)(2,1)S(1)}, bf16[64,2048]{1,0:T(8,128)(2,1)S(1)}, u32[]{:S(2)}, u32[]{:S(2)}) collective-permute-start(bf16[64,2048]{1,0:T(8,128)(2,1)S(1)} %get-tuple-element.19), channel_id=1, source_target_pairs={{0,128},{2,130},{4,132},{6,134},{8,136},{10,138},{12,140},{14,142}... | collective-permute-start | bytes 786440 | tf_op jit(solution)/shard_map/ppermute | solution.py:43
  26.3 13.0 %collective-permute-start.7 = (bf16[128,2048]{1,0:T(8,128)(2,1)S(1)}, bf16[128,2048]{1,0:T(8,128)(2,1)S(1)}, u32[]{:S(2)}, u32[]{:S(2)}) collective-permute-start(bf16[128,2048]{1,0:T(8,128)(2,1)S(1)} %constant_dynamic-update-slice_fusion.5.refs_0_), channel_id=1, source_target_pairs={{0,2},{2,0},{4,6},{6,4},{8,10},{10,8},{12,14},{14,12},{16,18},{18,... | collective-permute-start | bytes 1572872 | tf_op jit(solution)/shard_map/ppermute | solution.py:43
  29.4 14.7 %collective-permute-start.5 = (bf16[128,2048]{1,0:T(8,128)(2,1)S(1)}, bf16[128,2048]{1,0:T(8,128)(2,1)S(1)}, u32[]{:S(2)}, u32[]{:S(2)}) collective-permute-start(bf16[128,2048]{1,0:T(8,128)(2,1)S(1)} %constant_dynamic-update-slice_fusion.5.refs_0_), channel_id=1, source_target_pairs={{0,4},{2,6},{4,8},{6,10},{8,12},{10,14},{12,0},{14,2},{16,20},{18,... | collective-permute-start | bytes 1572872 | tf_op jit(solution)/shard_map/ppermute | solution.py:43
  30.7 13.5 %collective-permute-start.6 = (bf16[128,2048]{1,0:T(8,128)(2,1)S(1)}, bf16[128,2048]{1,0:T(8,128)(2,1)S(1)}, u32[]{:S(2)}, u32[]{:S(2)}) collective-permute-start(bf16[128,2048]{1,0:T(8,128)(2,1)S(1)} %constant_dynamic-update-slice_fusion.5.refs_0_), channel_id=1, source_target_pairs={{0,12},{2,14},{4,0},{6,2},{8,4},{10,6},{12,8},{14,10},{16,28},{18,... | collective-permute-start | bytes 1572872 | tf_op jit(solution)/shard_map/ppermute | solution.py:43
  32.5 6.8 %copy-start.2 = (f32[128]{0:T(128)S(1)}, f32[128]{0:T(128)}, u32[]{:S(2)}) copy-start(f32[128]{0:T(128)} %param.17) | copy-start | bytes 1540
  44.1 3.9 %collective-permute-start.11 = (bf16[128,2048]{1,0:T(8,128)(2,1)S(1)}, bf16[128,2048]{1,0:T(8,128)(2,1)S(1)}, u32[]{:S(2)}, u32[]{:S(2)}) collective-permute-start(bf16[128,2048]{1,0:T(8,128)(2,1)S(1)} %collective-permute-done.5.refs_0_), channel_id=1, source_target_pairs={{0,2},{2,0},{4,6},{6,4},{8,10},{10,8},{12,14},{14,12},{16,18},{18,... | collective-permute-start | bytes 1572872 | tf_op jit(solution)/shard_map/ppermute | solution.py:43
  45.0 5.8 %collective-permute-start.10 = (bf16[128,2048]{1,0:T(8,128)(2,1)S(1)}, bf16[128,2048]{1,0:T(8,128)(2,1)S(1)}, u32[]{:S(2)}, u32[]{:S(2)}) collective-permute-start(bf16[128,2048]{1,0:T(8,128)(2,1)S(1)} %collective-permute-done.6.refs_0_), channel_id=1, source_target_pairs={{0,2},{2,0},{4,6},{6,4},{8,10},{10,8},{12,14},{14,12},{16,18},{18,... | collective-permute-start | bytes 1572872 | tf_op jit(solution)/shard_map/ppermute | solution.py:43
  45.1 8.7 %collective-permute-start.8 = (bf16[64,2048]{1,0:T(8,128)(2,1)S(1)}, bf16[64,2048]{1,0:T(8,128)(2,1)S(1)}, u32[]{:S(2)}, u32[]{:S(2)}) collective-permute-start(bf16[64,2048]{1,0:T(8,128)(2,1)S(1)} %slice.6), channel_id=1, source_target_pairs={{0,4},{2,6},{4,8},{6,10},{8,12},{10,14},{12,0},{14,2},{16,20},{18,... | collective-permute-start | bytes 786440 | tf_op jit(solution)/shard_map/ppermute | solution.py:43
  46.3 7.4 %collective-permute-start.9 = (bf16[64,2048]{1,0:T(8,128)(2,1)S(1)}, bf16[64,2048]{1,0:T(8,128)(2,1)S(1)}, u32[]{:S(2)}, u32[]{:S(2)}) collective-permute-start(bf16[64,2048]{1,0:T(8,128)(2,1)S(1)} %slice.7), channel_id=1, source_target_pairs={{0,12},{2,14},{4,0},{6,2},{8,4},{10,6},{12,8},{14,10},{16,28},{18,... | collective-permute-start | bytes 786440 | tf_op jit(solution)/shard_map/ppermute | solution.py:43
  53.7 3.4 %collective-permute-start.12 = (bf16[64,2048]{1,0:T(8,128)(2,1)S(1)}, bf16[64,2048]{1,0:T(8,128)(2,1)S(1)}, u32[]{:S(2)}, u32[]{:S(2)}) collective-permute-start(bf16[64,2048]{1,0:T(8,128)(2,1)S(1)} %collective-permute-done.8.refs_0_), channel_id=1, source_target_pairs={{0,2},{2,0},{4,6},{6,4},{8,10},{10,8},{12,14},{14,12},{16,18},{18,... | collective-permute-start | bytes 786440 | tf_op jit(solution)/shard_map/ppermute | solution.py:43
  55.1 2.1 %collective-permute-start.13 = (bf16[64,2048]{1,0:T(8,128)(2,1)S(1)}, bf16[64,2048]{1,0:T(8,128)(2,1)S(1)}, u32[]{:S(2)}, u32[]{:S(2)}) collective-permute-start(bf16[64,2048]{1,0:T(8,128)(2,1)S(1)} %collective-permute-done.9.refs_1_), channel_id=1, source_target_pairs={{0,2},{2,0},{4,6},{6,4},{8,10},{10,8},{12,14},{14,12},{16,18},{18,... | collective-permute-start | bytes 786440 | tf_op jit(solution)/shard_map/ppermute | solution.py:43

commit v4 on v3

--- a/solution.py
+++ b/solution.py
@@ -28,11 +28,18 @@
     return pairs
 
 
+def side(c):
+    return 1 - 2 * c
+
+
+Z_EVEN = {k: shift(lambda y, z, x, c, k=k: (y, z + k, x, c)) for k in (2, 4, 6)}
+Y_PAIR = shift(lambda y, z, x, c: (y + 1, z, x, c))
 Z_PAIR = shift(lambda y, z, x, c: (y, z ^ 1, x, c))
-Z_PLUS = {k: shift(lambda y, z, x, c, k=k: (y, z + k, x, c)) for k in (2, 4, 6)}
-Y_PAIR = shift(lambda y, z, x, c: (y + 1, z, x, c))
-X_PLUS = {k: shift(lambda y, z, x, c, k=k: (y, z, x + k, c)) for k in (1, 3)}
+YZ_PAIR = shift(lambda y, z, x, c: (y + 1, z ^ 1, x, c))
+X_SIDE = shift(lambda y, z, x, c: (y, z, x + side(c), c))
+X_BACK = shift(lambda y, z, x, c: (y, z, x - side(c), c))
 CORE_PAIR = shift(lambda y, z, x, c: (y, z, x, c + 1))
+PARTS = [(t, b, back) for b in range(2) for t in range(NY) for back in (0, 4, 2, 6)]
 
 
 def cost(flops, bytes_accessed):
@@ -101,55 +108,59 @@
     lax.fori_loop(0, SEQS // step, body, 0)
 
 
-def pair_kernel(place_ref, *refs, pieces, aliased):
+def pair_kernel(*refs, pieces, aliased):
     lefts = refs[: len(pieces)]
     table_ref, bias_ref = refs[len(pieces) : len(pieces) + 2]
-    out_ref, left_all, acc_ref = refs[len(pieces) + 2 + aliased :]
-    core = place_ref[1]
-    lanes = out_ref.shape[2]
+    out_ref, left_all, acc_ref, ready, sems = refs[len(pieces) + 2 + aliased :]
     rows = lefts[0].shape[0]
-    for k, left_ref in enumerate(lefts):
-        left_all[k * rows : (k + 1) * rows, :] = left_ref[...]
+    for n, left_ref in enumerate(lefts):
+        left_all[n * rows : (n + 1) * rows, :] = left_ref[...]
     acc_ref[...] = jnp.dot(left_all[...], table_ref[...], preferred_element_type=jnp.float32)
-    for n, (lane, first) in enumerate(pieces):
+    me = lax.axis_index("dap")
+    core = lax.rem(me, NC)
+    x = lax.rem(lax.div(me, NC), NX)
+    z = lax.rem(lax.div(me, NC * NX), NZ)
+    y = lax.div(me, NC * NX * NZ)
+    copies = []
+    for n, (lane, ahead) in enumerate(pieces):
         c = core if lane == 0 else 1 - core
-        for k in range(rows // 8):
-            at = n * rows + k * 8
-            part = acc_ref[at : at + 8, :].reshape(8, 8, C_Z) + bias_ref[...]
-            out_ref[place_ref[2 + first + k], 0, c if lanes == NC else 0] = part.astype(jnp.bfloat16)
-
-
-def pair_block(place, lefts, pieces, table, bias, turn, out):
+        to_x = lax.rem(x + ahead * side(core) + NX, NX)
+        for k, (t, b, back) in enumerate(PARTS):
+            slot = n * len(PARTS) + k
+            part = acc_ref[slot * 8 : slot * 8 + 8, :].reshape(8, 8, C_Z) + bias_ref[...]
+            ready[slot] = part.astype(jnp.bfloat16)
+            to_y = lax.rem(y + t, NY)
+            to_z = lax.rem((z + b * (1 - 2 * lax.rem(z, 2))) - back + NZ, NZ)
+            to = ((to_y * NZ + to_z) * NX + to_x) * NC + c
+            copy = pltpu.make_async_copy(ready.at[slot], out_ref.at[to], sems.at[slot])
+            copy.start()
+            copies.append(copy)
+    for copy in copies:
+        copy.wait()
+
+
+def pair_block(lefts, pieces, table, bias, out):
     aliased = out is not None
-    whole = pl.BlockSpec(memory_space=pltpu.VMEM)
+    vmem, anywhere = pl.BlockSpec(memory_space=pltpu.VMEM), pl.BlockSpec(memory_space=pl.ANY)
     operands = [*lefts, table, bias] + ([out] if aliased else [])
-    in_specs = [whole] * (len(lefts) + 2) + ([pl.BlockSpec(memory_space=pl.ANY)] if aliased else [])
     rows = sum(left.shape[0] for left in lefts)
-    lanes = sorted({lane for lane, _ in pieces})
-    if len(lanes) == NC:
-        turn_lane = lambda place: 0
-    else:
-        turn_lane = lambda place: lax.rem(place[1] + lanes[0], NC)
+    depth, width = table.shape
+    blocks = rows // 8
     return pl.pallas_call(
         functools.partial(pair_kernel, pieces=pieces, aliased=int(aliased)),
-        grid_spec=pltpu.PrefetchScalarGridSpec(
-            num_scalar_prefetch=1,
-            grid=(1,),
-            in_specs=in_specs,
-            out_specs=pl.BlockSpec(
-                (NY * NZ, 1, len(lanes), 8, 8, C_Z),
-                lambda i, place: (0, lax.rem(place[0] + turn, NX), turn_lane(place), 0, 0, 0),
-            ),
-            scratch_shapes=[
-                pltpu.VMEM((rows, SEQS * HID), jnp.bfloat16),
-                pltpu.VMEM((rows, 8 * C_Z), jnp.float32),
-            ],
-        ),
-        out_shape=jax.ShapeDtypeStruct((NY * NZ, NX, NC, 8, 8, C_Z), jnp.bfloat16),
-        input_output_aliases={len(operands): 0} if aliased else {},
+        in_specs=[vmem] * (len(lefts) + 2) + ([anywhere] if aliased else []),
+        out_specs=anywhere,
+        out_shape=jax.ShapeDtypeStruct((NY * NZ * NX * NC, 8, 8, C_Z), jnp.bfloat16),
+        scratch_shapes=[
+            pltpu.VMEM((rows, depth), jnp.bfloat16),
+            pltpu.VMEM((rows, width), jnp.float32),
+            pltpu.VMEM((blocks, 8, 8, C_Z), jnp.bfloat16),
+            pltpu.SemaphoreType.DMA((blocks,)),
+        ],
+        input_output_aliases={len(operands) - 1: 0} if aliased else {},
         compiler_params=pltpu.CompilerParams(vmem_limit_bytes=24 * 1024 * 1024),
-        cost_estimate=cost(2 * rows * 2048 * 1024, 10 << 20),
-    )(place, *operands)
+        cost_estimate=cost(2 * rows * depth * width, 10 << 20),
+    )(*operands)
 
 
 def per_device(
@@ -193,36 +204,23 @@
         out_weight,
     )
 
-    me = lax.axis_index("dap")
-    core, x, z, y = me % NC, me // NC % NX, me // (NC * NX) % NZ, me // (NC * NX * NZ)
-    slots = [
-        (y ^ t) * NZ + ((z + NZ - back) % NZ ^ b)
-        for t in range(NY)
-        for back in (0, 4, 2, 6)
-        for b in range(2)
-    ]
-    place = jnp.stack([x, core] + slots).astype(jnp.int32)
     bias = output_bias[None]
 
-    pair = jnp.concatenate([left, send(left, Z_PAIR)], axis=0)
-    ring = jnp.concatenate([pair] + [send(pair, Z_PLUS[k]) for k in (4, 2, 6)], axis=0)
-    block = jnp.concatenate([ring, send(ring, Y_PAIR)], axis=0)
-
-    def other(blocks):
-        return [send(b, CORE_PAIR) for b in blocks]
-
-    whole = [(0, 0), (1, 0)]
-    low, high = send(block, X_PLUS[1]), send(block, X_PLUS[3])
-    out = pair_block(place, [block] + other([block]), whole, table, bias, 0, None)
-    low, high, table, out = lax.optimization_barrier((low, high, table, out))
-    half = block.shape[0] // 2
-    far = [send(low[:half], X_PLUS[1]), send(high[half:], X_PLUS[3])]
-    out = pair_block(place, [low] + other([low]), whole, table, bias, 3, out)
-    out = pair_block(place, [high] + other([high]), whole, table, bias, 1, out)
-    far[0], far[1], out = lax.optimization_barrier((far[0], far[1], out))
-    far_other = other(far)
-    out = pair_block(place, far, [(0, 0), (0, 8)], table, bias, 2, out)
-    out = pair_block(place, far_other, [(1, 0), (1, 8)], table, bias, 2, out)
+    ring = jnp.concatenate([left] + [send(left, Z_EVEN[k]) for k in (4, 2, 6)], axis=0)
+    block = jnp.concatenate(
+        [ring, send(ring, Y_PAIR), send(ring, Z_PAIR), send(ring, YZ_PAIR)], axis=0
+    )
+    ahead, behind = send(block, X_BACK), send(block, X_SIDE)
+    out = pair_block([block, send(block, CORE_PAIR)], [(0, 0), (1, 0)], table, bias, None)
+    ahead, behind, table, out = lax.optimization_barrier((ahead, behind, table, out))
+    others = [send(ahead, CORE_PAIR), send(behind, CORE_PAIR)]
+    far = send(behind, X_SIDE)
+    out = pair_block([ahead, behind], [(0, 1), (0, -1)], table, bias, out)
+    out = pair_block(others, [(1, -1), (1, 1)], table, bias, out)
+    far, out = lax.optimization_barrier((far, out))
+    far_other = send(far, CORE_PAIR)
+    out = pair_block([far], [(0, 2)], table, bias, out)
+    out = pair_block([far_other], [(1, 2)], table, bias, out)
     return out.reshape(NY * NZ * NX * NC * 8, 8, C_Z)
 
 

time: 59.4 us -> 56.8 us (0.956)
  starting transfers between devices: 25.2 us -> 22.2 us
  Pallas kernels: 21 us -> 18.7 us
  waiting for transfers between devices: 10.8 us -> 12.5 us
  local copies, waits for them, and re-layouts: 1.23 us -> 2.02 us
    ppermute x14 -> x13, starting transfers between devices: 25.2 us -> 22.2 us  [send(): return lax.ppermute(block, 'dap', pairs)]
    pallas_call x5, Pallas kernels: 12.2 us -> 9.91 us  [pair_block(): pl.pallas_call(functools.partial(pair_kernel, pieces=pieces, aliased=int(...]
    ppermute x14 -> x13, waiting for transfers between devices: 10.8 us -> 12.5 us  [send(): return lax.ppermute(block, 'dap', pairs)]
    reshape x1, local copies, waits for them, and re-layouts: 0.1 us -> 1.05 us  [per_device(): output_weight.reshape(HID, HID, C_Z).transpose(1, 0, 2)]
  transfers between devices with their start and end apart: 14 -> 13, of which waited for: 6 -> 6; matrix products, arithmetic and copies ran while one was open for 2% -> 4% of each run, Pallas kernels for 28% -> 27%
where the time goes in v4:
time: 56.8 us; the launch traced here: 56.5 us
  starting transfers between devices  22.2 us (39%)
  Pallas kernels  18.7 us (33%)
  waiting for transfers between devices  12.5 us (22%)
  local copies, waits for them, and re-layouts  2.02 us (4%)
  other arithmetic  0.77 us (1%)
    ppermute x13, starting transfers between devices, send(): return lax.ppermute(block, 'dap', pairs)  22.2 us
    ppermute x13, waiting for transfers between devices, send(): return lax.ppermute(block, 'dap', pairs)  12.5 us
    pallas_call x5, Pallas kernels, pair_block(): pl.pallas_call(functools.partial(pair_kernel, pieces=pieces, aliased=int(...  9.91 us
    pallas_call x1, Pallas kernels, per_device(): pl.pallas_call(table_kernel, out_shape=jax.ShapeDtypeStruct((SEQS * HID,...  6.75 us
    pallas_call x1, Pallas kernels, per_device(): pl.pallas_call(left_kernel, out_shape=jax.ShapeDtypeStruct((rows, SEQS *...  2.04 us
  transfers between devices with their start and end apart: 13, of which 6 were waited for; matrix products, arithmetic and copies ran while one was open for 4% of the time, Pallas kernels for 27%

profile of v4, /device:TPU:1, one launch (start us, length us, event | category | flops | bytes accessed | tf_op | source)
XLA Modules:
  0.0 56.5 jit_solution(10983428495762765365)
XLA Ops:
  0.0 0.0 copy-start.4
  0.0 0.0 copy-start.3
  0.0 0.0 copy-start.5
  0.0 0.0 copy-start.1
  0.0 2.0 %shard_map.91 = bf16[8,2048]{1,0:T(8,128)(2,1)} custom-call(bf16[64,8,256]{2,1,0:T(8,128)(2,1)} %feats_ref.3, f32[1,256]{1,0:T(1,128)} %bitcast.21, f32[1,256]{1,0:T(1,128)} %bitcast.23, bf16[32,256]{1,0:T(8,128)(2,1)} %bitcast.28, f32[1,32]{1,0:T(1,128)} %bitcast.29), custom_call_target="tpu_custom_call" | custom-call | tf_op jit(solution)/shard_map/pallas_call | solution.py:180
  2.1 6.8 %collective-permute-start.2 = (bf16[8,2048]{1,0:T(8,128)(2,1)}, bf16[8,2048]{1,0:T(8,128)(2,1)S(1)}, u32[]{:S(2)}, u32[]{:S(2)}) collective-permute-start(bf16[8,2048]{1,0:T(8,128)(2,1)} %shard_map.91), channel_id=1, source_target_pairs={{0,96},{2,98},{4,100},{6,102},{8,104},{10,106},{12,108},{14,110},{... | collective-permute-start | bytes 98312 | tf_op jit(solution)/shard_map/ppermute | solution.py:50
  8.9 0.0 collective-permute-start.1
  8.9 3.3 %collective-permute-start = (bf16[8,2048]{1,0:T(8,128)(2,1)}, bf16[8,2048]{1,0:T(8,128)(2,1)S(1)}, u32[]{:S(2)}, u32[]{:S(2)}) collective-permute-start(bf16[8,2048]{1,0:T(8,128)(2,1)} %shard_map.91), channel_id=1, source_target_pairs={{0,64},{2,66},{4,68},{6,70},{8,72},{10,74},{12,76},{14,78},{16,80}... | collective-permute-start | bytes 98312 | tf_op jit(solution)/shard_map/ppermute | solution.py:50
  12.2 0.8 %constant_dynamic-update-slice_fusion.6 = bf16[128,2048]{1,0:T(8,128)(2,1)S(1)} fusion(bf16[8,2048]{1,0:T(8,128)(2,1)} %shard_map.91), kind=kLoop, calls=%fused_computation.8 | loop fusion | bytes 65536
  13.0 0.0 collective-permute-done.2
  13.0 1.0 %collective-permute-done.1 = bf16[8,2048]{1,0:T(8,128)(2,1)S(1)} collective-permute-done((bf16[8,2048]{1,0:T(8,128)(2,1)}, bf16[8,2048]{1,0:T(8,128)(2,1)S(1)}, u32[]{:S(2)}, u32[]{:S(2)}) %collective-permute-start.1) | collective-permute-done | bytes 32800 | tf_op jit(solution)/shard_map/ppermute | solution.py:50
  14.0 1.8 %collective-permute-done = bf16[8,2048]{1,0:T(8,128)(2,1)S(1)} collective-permute-done((bf16[8,2048]{1,0:T(8,128)(2,1)}, bf16[8,2048]{1,0:T(8,128)(2,1)S(1)}, u32[]{:S(2)}, u32[]{:S(2)}) %collective-permute-start) | collective-permute-done | bytes 32800 | tf_op jit(solution)/shard_map/ppermute | solution.py:50
  15.8 0.8 %pad_maximum_fusion = bf16[32,2048]{1,0:T(8,128)(2,1)S(1)} fusion(bf16[8,2048]{1,0:T(8,128)(2,1)S(1)} %collective-permute-done.2, bf16[8,2048]{1,0:T(8,128)(2,1)S(1)} %collective-permute-done.1, bf16[8,2048]{1,0:T(8,128)(2,1)S(1)} %collective-permute-done, bf16[8,2048]{1,0:T(8,128)(2,1)} %shard_map.91), kind=kLoop, calls=%fused_computation.1 | loop fusion | flops 524288 | bytes 262144 | tf_op jit(solution)/shard_map/concatenate | solution.py:209
  16.6 1.8 %collective-permute-start.5 = (bf16[32,2048]{1,0:T(8,128)(2,1)S(1)}, bf16[32,2048]{1,0:T(8,128)(2,1)S(1)}, u32[]{:S(2)}, u32[]{:S(2)}) collective-permute-start(bf16[32,2048]{1,0:T(8,128)(2,1)S(1)} %pad_maximum_fusion), channel_id=1, source_target_pairs={{0,144},{2,146},{4,148},{6,150},{8,152},{10,154},{12,156},{14,158}... | collective-permute-start | bytes 393224 | tf_op jit(solution)/shard_map/ppermute | solution.py:50
  18.4 0.7 %collective-permute-start.4 = (bf16[32,2048]{1,0:T(8,128)(2,1)S(1)}, bf16[32,2048]{1,0:T(8,128)(2,1)S(1)}, u32[]{:S(2)}, u32[]{:S(2)}) collective-permute-start(bf16[32,2048]{1,0:T(8,128)(2,1)S(1)} %pad_maximum_fusion), channel_id=1, source_target_pairs={{0,16},{2,18},{4,20},{6,22},{8,24},{10,26},{12,28},{14,30},{16,0},... | collective-permute-start | bytes 393224 | tf_op jit(solution)/shard_map/ppermute | solution.py:50
  19.2 0.2 collective-permute-start.3
  19.3 5.3 %collective-permute-done.3 = bf16[32,2048]{1,0:T(8,128)(2,1)S(1)} collective-permute-done((bf16[32,2048]{1,0:T(8,128)(2,1)S(1)}, bf16[32,2048]{1,0:T(8,128)(2,1)S(1)}, u32[]{:S(2)}, u32[]{:S(2)}) %collective-permute-start.3) | collective-permute-done | bytes 131104 | tf_op jit(solution)/shard_map/ppermute | solution.py:50
  24.7 0.0 collective-permute-done.4
  24.7 0.0 collective-permute-done.5
  24.7 2.2 %collective-permute-start.8 = (bf16[128,2048]{1,0:T(8,128)(2,1)S(1)}, bf16[128,2048]{1,0:T(8,128)(2,1)S(1)}, u32[]{:S(2)}, u32[]{:S(2)}) collective-permute-start(bf16[128,2048]{1,0:T(8,128)(2,1)S(1)} %constant_dynamic-update-slice_fusion.refs_0_), channel_id=1, source_target_pairs={{0,2},{2,0},{4,6},{6,4},{8,10},{10,8},{12,14},{14,12},{16,18},{18,... | collective-permute-start | bytes 1572872 | tf_op jit(solution)/shard_map/ppermute | solution.py:50
  26.9 2.5 %collective-permute-start.7 = (bf16[128,2048]{1,0:T(8,128)(2,1)S(1)}, bf16[128,2048]{1,0:T(8,128)(2,1)S(1)}, u32[]{:S(2)}, u32[]{:S(2)}) collective-permute-start(bf16[128,2048]{1,0:T(8,128)(2,1)S(1)} %constant_dynamic-update-slice_fusion.refs_0_), channel_id=1, source_target_pairs={{0,4},{2,14},{4,8},{6,2},{8,12},{10,6},{12,0},{14,10},{16,20},{18,... | collective-permute-start | bytes 1572872 | tf_op jit(solution)/shard_map/ppermute | solution.py:50
  29.4 0.0 collective-permute-start.6
  29.4 1.1 %copy.14 = bf16[32,32,128]{2,0,1:T(8,128)(2,1)S(1)} copy(bf16[32,32,128]{2,1,0:T(8,128)(2,1)} %bitcast.27) | data formatting | bytes 524288 | tf_op jit(solution)/shard_map/reshape | solution.py:191
  30.5 0.1 copy.17
  30.6 0.0 copy-done
  30.6 0.0 copy-done.4
  30.6 0.0 copy-done.3
  30.6 0.0 copy-done.5
  30.6 0.0 copy-done.1
  30.6 0.0 copy-start.2
  30.6 6.8 %shard_map.92.refs_2_.refs_1_ = bf16[2048,1024]{1,0:T(8,128)(2,1)S(1)} custom-call(bf16[64,8,256]{2,1,0:T(8,128)(2,1)S(1)} %copy-done, f32[1,256]{1,0:T(1,128)S(1)} %bitcast.22, f32[1,256]{1,0:T(1,128)S(1)} %bitcast.24, bf16[32,256]{1,0:T(8,128)(2,1)S(1)} %bitcast.15, f32[1,32]{1,0:T(1,128)S(1)} %bitcast.25, bf16[32,4096]{1,0:T(8,128)(2,1)S(1)} %bitcast.14), custom_call_target="tpu_custom_call" | custom-call | flops 1073741824 | bytes 25165824 | tf_op jit(solution)/shard_map/pallas_call | solution.py:192
  37.4 0.0 collective-permute-done.8.refs_1_
  37.4 0.0 copy-done.2
  37.4 2.3 %shard_map.93.refs_4_ = bf16[128,8,8,128]{3,2,1,0:T(8,128)(2,1)} custom-call(bf16[128,2048]{1,0:T(8,128)(2,1)S(1)} %constant_dynamic-update-slice_fusion.refs_0_, bf16[128,2048]{1,0:T(8,128)(2,1)S(1)} %collective-permute-done.8.refs_1_, bf16[2048,1024]{1,0:T(8,128)(2,1)S(1)} %shard_map.92.refs_2_.refs_1_, f32[1,128]{1,0:T(1,128)S(1)} %bitcast.16), custom_call_target="tpu_custom_call" | custom-call | flops 1073741824 | bytes 10485760 | tf_op jit(solution)/shard_map/pallas_call | solution.py:149
  39.7 0.4 collective-permute-done.7.refs_1_
  40.1 2.2 %collective-permute-done.6.refs_0_ = bf16[128,2048]{1,0:T(8,128)(2,1)S(1)} collective-permute-done((bf16[128,2048]{1,0:T(8,128)(2,1)S(1)}, bf16[128,2048]{1,0:T(8,128)(2,1)S(1)}, u32[]{:S(2)}, u32[]{:S(2)}) %collective-permute-start.6) | collective-permute-done | bytes 524320 | tf_op jit(solution)/shard_map/ppermute | solution.py:50
  42.3 0.0 collective-permute-start.10
  42.3 0.5 collective-permute-start.11
  42.9 2.1 %collective-permute-start.9 = (bf16[128,2048]{1,0:T(8,128)(2,1)S(1)}, bf16[128,2048]{1,0:T(8,128)(2,1)S(1)}, u32[]{:S(2)}, u32[]{:S(2)}) collective-permute-start(bf16[128,2048]{1,0:T(8,128)(2,1)S(1)} %collective-permute-done.7.refs_1_), channel_id=1, source_target_pairs={{0,4},{2,14},{4,8},{6,2},{8,12},{10,6},{12,0},{14,10},{16,20},{18,... | collective-permute-start | bytes 1572872 | tf_op jit(solution)/shard_map/ppermute | solution.py:50
  45.0 2.3 %shard_map.94.refs_4_ = bf16[128,8,8,128]{3,2,1,0:T(8,128)(2,1)} custom-call(bf16[128,2048]{1,0:T(8,128)(2,1)S(1)} %collective-permute-done.6.refs_0_, bf16[128,2048]{1,0:T(8,128)(2,1)S(1)} %collective-permute-done.7.refs_1_, bf16[2048,1024]{1,0:T(8,128)(2,1)S(1)} %shard_map.92.refs_2_.refs_1_, ...), custom_call_target="tpu_custom_call", output_to_operand_aliasing={{}: (4, {})} | custom-call | flops 1073741824 | bytes 10485760 | tf_op jit(solution)/shard_map/pallas_call | solution.py:149
  47.2 0.0 collective-permute-done.10.refs_0_
  47.2 0.0 collective-permute-done.11.refs_1_
  47.3 2.3 %shard_map.95.refs_3_ = bf16[128,8,8,128]{3,2,1,0:T(8,128)(2,1)} custom-call(bf16[128,2048]{1,0:T(8,128)(2,1)S(1)} %collective-permute-done.10.refs_0_, bf16[128,2048]{1,0:T(8,128)(2,1)S(1)} %collective-permute-done.11.refs_1_, bf16[2048,1024]{1,0:T(8,128)(2,1)S(1)} %shard_map.92.refs_2_.refs_1_, ...), custom_call_target="tpu_custom_call", output_to_operand_aliasing={{}: (4, {})} | custom-call | flops 1073741824 | bytes 10485760 | tf_op jit(solution)/shard_map/pallas_call | solution.py:149
  49.5 1.6 %collective-permute-done.9.refs_0_ = bf16[128,2048]{1,0:T(8,128)(2,1)S(1)} collective-permute-done((bf16[128,2048]{1,0:T(8,128)(2,1)S(1)}, bf16[128,2048]{1,0:T(8,128)(2,1)S(1)}, u32[]{:S(2)}, u32[]{:S(2)}) %collective-permute-start.9) | collective-permute-done | bytes 524320 | tf_op jit(solution)/shard_map/ppermute | solution.py:50
  51.2 2.1 %collective-permute-start.12 = (bf16[128,2048]{1,0:T(8,128)(2,1)S(1)}, bf16[128,2048]{1,0:T(8,128)(2,1)S(1)}, u32[]{:S(2)}, u32[]{:S(2)}) collective-permute-start(bf16[128,2048]{1,0:T(8,128)(2,1)S(1)} %collective-permute-done.9.refs_0_), channel_id=1, source_target_pairs={{0,2},{2,0},{4,6},{6,4},{8,10},{10,8},{12,14},{14,12},{16,18},{18,... | collective-permute-start | bytes 1572872 | tf_op jit(solution)/shard_map/ppermute | solution.py:50
  53.3 1.6 %shard_map.96.refs_3_ = bf16[128,8,8,128]{3,2,1,0:T(8,128)(2,1)} custom-call(bf16[128,2048]{1,0:T(8,128)(2,1)S(1)} %collective-permute-done.9.refs_0_, bf16[2048,1024]{1,0:T(8,128)(2,1)S(1)} %shard_map.92.refs_2_.refs_1_, f32[1,128]{1,0:T(1,128)S(1)} %bitcast.19, bf16[128,8,8,128]{3,2,1,0:T(8,128)(2,1)} %shard_map.95.refs_3_), custom_call_target="tpu_custom_call", output_to_operand_aliasing={{}: (3, {})} | custom-call | flops 536870912 | bytes 10485760 | tf_op jit(solution)/shard_map/pallas_call | solution.py:149
  54.8 0.0 collective-permute-done.12.refs_0_
  54.8 1.5 %shard_map.97 = bf16[128,8,8,128]{3,2,1,0:T(8,128)(2,1)} custom-call(bf16[128,2048]{1,0:T(8,128)(2,1)S(1)} %collective-permute-done.12.refs_0_, bf16[2048,1024]{1,0:T(8,128)(2,1)S(1)} %shard_map.92.refs_2_.refs_1_, f32[1,128]{1,0:T(1,128)S(1)} %bitcast.20, bf16[128,8,8,128]{3,2,1,0:T(8,128)(2,1)} %shard_map.96.refs_3_), custom_call_target="tpu_custom_call", output_to_operand_aliasing={{}: (3, {})} | custom-call | flops 536870912 | bytes 10485760 | tf_op jit(solution)/shard_map/pallas_call | solution.py:149
  (7 shorter events, 0.0 us)
Async XLA Ops:
  0.0 30.6 %copy-start = (bf16[64,8,256]{2,1,0:T(8,128)(2,1)S(1)}, bf16[64,8,256]{2,1,0:T(8,128)(2,1)}, u32[]{:S(2)}) copy-start(bf16[64,8,256]{2,1,0:T(8,128)(2,1)} %feats_ref.3) | copy-start | bytes 786436
  0.0 30.6 %copy-start.4 = (f32[256]{0:T(256)S(1)}, f32[256]{0:T(256)}, u32[]{:S(2)}) copy-start(f32[256]{0:T(256)} %param.11) | copy-start | bytes 3076
  0.0 30.6 %copy-start.3 = (f32[256]{0:T(256)S(1)}, f32[256]{0:T(256)}, u32[]{:S(2)}) copy-start(f32[256]{0:T(256)} %param.10) | copy-start | bytes 3076
  0.0 30.6 %copy-start.5 = (f32[32]{0:T(128)S(1)}, f32[32]{0:T(128)}, u32[]{:S(2)}) copy-start(f32[32]{0:T(128)} %param.15) | copy-start | bytes 388
  0.0 30.6 %copy-start.1 = (bf16[256,32]{0,1:T(8,128)(2,1)S(1)}, bf16[256,32]{0,1:T(8,128)(2,1)}, u32[]{:S(2)}) copy-start(bf16[256,32]{0,1:T(8,128)(2,1)} %param.14) | copy-start | bytes 49156
  2.1 10.9 %collective-permute-start.2 = (bf16[8,2048]{1,0:T(8,128)(2,1)}, bf16[8,2048]{1,0:T(8,128)(2,1)S(1)}, u32[]{:S(2)}, u32[]{:S(2)}) collective-permute-start(bf16[8,2048]{1,0:T(8,128)(2,1)} %shard_map.91), channel_id=1, source_target_pairs={{0,96},{2,98},{4,100},{6,102},{8,104},{10,106},{12,108},{14,110},{... | collective-permute-start | bytes 98312 | tf_op jit(solution)/shard_map/ppermute | solution.py:50
  8.9 5.1 %collective-permute-start.1 = (bf16[8,2048]{1,0:T(8,128)(2,1)}, bf16[8,2048]{1,0:T(8,128)(2,1)S(1)}, u32[]{:S(2)}, u32[]{:S(2)}) collective-permute-start(bf16[8,2048]{1,0:T(8,128)(2,1)} %shard_map.91), channel_id=1, source_target_pairs={{0,32},{2,34},{4,36},{6,38},{8,40},{10,42},{12,44},{14,46},{16,48}... | collective-permute-start | bytes 98312 | tf_op jit(solution)/shard_map/ppermute | solution.py:50
  8.9 6.9 %collective-permute-start = (bf16[8,2048]{1,0:T(8,128)(2,1)}, bf16[8,2048]{1,0:T(8,128)(2,1)S(1)}, u32[]{:S(2)}, u32[]{:S(2)}) collective-permute-start(bf16[8,2048]{1,0:T(8,128)(2,1)} %shard_map.91), channel_id=1, source_target_pairs={{0,64},{2,66},{4,68},{6,70},{8,72},{10,74},{12,76},{14,78},{16,80}... | collective-permute-start | bytes 98312 | tf_op jit(solution)/shard_map/ppermute | solution.py:50
  16.6 8.1 %collective-permute-start.5 = (bf16[32,2048]{1,0:T(8,128)(2,1)S(1)}, bf16[32,2048]{1,0:T(8,128)(2,1)S(1)}, u32[]{:S(2)}, u32[]{:S(2)}) collective-permute-start(bf16[32,2048]{1,0:T(8,128)(2,1)S(1)} %pad_maximum_fusion), channel_id=1, source_target_pairs={{0,144},{2,146},{4,148},{6,150},{8,152},{10,154},{12,156},{14,158}... | collective-permute-start | bytes 393224 | tf_op jit(solution)/shard_map/ppermute | solution.py:50
  18.4 6.3 %collective-permute-start.4 = (bf16[32,2048]{1,0:T(8,128)(2,1)S(1)}, bf16[32,2048]{1,0:T(8,128)(2,1)S(1)}, u32[]{:S(2)}, u32[]{:S(2)}) collective-permute-start(bf16[32,2048]{1,0:T(8,128)(2,1)S(1)} %pad_maximum_fusion), channel_id=1, source_target_pairs={{0,16},{2,18},{4,20},{6,22},{8,24},{10,26},{12,28},{14,30},{16,0},... | collective-permute-start | bytes 393224 | tf_op jit(solution)/shard_map/ppermute | solution.py:50
  19.2 5.5 %collective-permute-start.3 = (bf16[32,2048]{1,0:T(8,128)(2,1)S(1)}, bf16[32,2048]{1,0:T(8,128)(2,1)S(1)}, u32[]{:S(2)}, u32[]{:S(2)}) collective-permute-start(bf16[32,2048]{1,0:T(8,128)(2,1)S(1)} %pad_maximum_fusion), channel_id=1, source_target_pairs={{0,128},{2,130},{4,132},{6,134},{8,136},{10,138},{12,140},{14,142}... | collective-permute-start | bytes 393224 | tf_op jit(solution)/shard_map/ppermute | solution.py:50
  24.7 12.7 %collective-permute-start.8 = (bf16[128,2048]{1,0:T(8,128)(2,1)S(1)}, bf16[128,2048]{1,0:T(8,128)(2,1)S(1)}, u32[]{:S(2)}, u32[]{:S(2)}) collective-permute-start(bf16[128,2048]{1,0:T(8,128)(2,1)S(1)} %constant_dynamic-update-slice_fusion.refs_0_), channel_id=1, source_target_pairs={{0,2},{2,0},{4,6},{6,4},{8,10},{10,8},{12,14},{14,12},{16,18},{18,... | collective-permute-start | bytes 1572872 | tf_op jit(solution)/shard_map/ppermute | solution.py:50
  26.9 13.2 %collective-permute-start.7 = (bf16[128,2048]{1,0:T(8,128)(2,1)S(1)}, bf16[128,2048]{1,0:T(8,128)(2,1)S(1)}, u32[]{:S(2)}, u32[]{:S(2)}) collective-permute-start(bf16[128,2048]{1,0:T(8,128)(2,1)S(1)} %constant_dynamic-update-slice_fusion.refs_0_), channel_id=1, source_target_pairs={{0,4},{2,14},{4,8},{6,2},{8,12},{10,6},{12,0},{14,10},{16,20},{18,... | collective-permute-start | bytes 1572872 | tf_op jit(solution)/shard_map/ppermute | solution.py:50
  29.4 12.9 %collective-permute-start.6 = (bf16[128,2048]{1,0:T(8,128)(2,1)S(1)}, bf16[128,2048]{1,0:T(8,128)(2,1)S(1)}, u32[]{:S(2)}, u32[]{:S(2)}) collective-permute-start(bf16[128,2048]{1,0:T(8,128)(2,1)S(1)} %constant_dynamic-update-slice_fusion.refs_0_), channel_id=1, source_target_pairs={{0,12},{2,6},{4,0},{6,10},{8,4},{10,14},{12,8},{14,2},{16,28},{18,... | collective-permute-start | bytes 1572872 | tf_op jit(solution)/shard_map/ppermute | solution.py:50
  30.6 6.8 %copy-start.2 = (f32[128]{0:T(128)S(1)}, f32[128]{0:T(128)}, u32[]{:S(2)}) copy-start(f32[128]{0:T(128)} %param.17) | copy-start | bytes 1540
  42.3 4.9 %collective-permute-start.10 = (bf16[128,2048]{1,0:T(8,128)(2,1)S(1)}, bf16[128,2048]{1,0:T(8,128)(2,1)S(1)}, u32[]{:S(2)}, u32[]{:S(2)}) collective-permute-start(bf16[128,2048]{1,0:T(8,128)(2,1)S(1)} %collective-permute-done.6.refs_0_), channel_id=1, source_target_pairs={{0,2},{2,0},{4,6},{6,4},{8,10},{10,8},{12,14},{14,12},{16,18},{18,... | collective-permute-start | bytes 1572872 | tf_op jit(solution)/shard_map/ppermute | solution.py:50
  42.3 4.9 %collective-permute-start.11 = (bf16[128,2048]{1,0:T(8,128)(2,1)S(1)}, bf16[128,2048]{1,0:T(8,128)(2,1)S(1)}, u32[]{:S(2)}, u32[]{:S(2)}) collective-permute-start(bf16[128,2048]{1,0:T(8,128)(2,1)S(1)} %collective-permute-done.7.refs_1_), channel_id=1, source_target_pairs={{0,2},{2,0},{4,6},{6,4},{8,10},{10,8},{12,14},{14,12},{16,18},{18,... | collective-permute-start | bytes 1572872 | tf_op jit(solution)/shard_map/ppermute | solution.py:50
  42.9 8.3 %collective-permute-start.9 = (bf16[128,2048]{1,0:T(8,128)(2,1)S(1)}, bf16[128,2048]{1,0:T(8,128)(2,1)S(1)}, u32[]{:S(2)}, u32[]{:S(2)}) collective-permute-start(bf16[128,2048]{1,0:T(8,128)(2,1)S(1)} %collective-permute-done.7.refs_1_), channel_id=1, source_target_pairs={{0,4},{2,14},{4,8},{6,2},{8,12},{10,6},{12,0},{14,10},{16,20},{18,... | collective-permute-start | bytes 1572872 | tf_op jit(solution)/shard_map/ppermute | solution.py:50
  51.2 3.6 %collective-permute-start.12 = (bf16[128,2048]{1,0:T(8,128)(2,1)S(1)}, bf16[128,2048]{1,0:T(8,128)(2,1)S(1)}, u32[]{:S(2)}, u32[]{:S(2)}) collective-permute-start(bf16[128,2048]{1,0:T(8,128)(2,1)S(1)} %collective-permute-done.9.refs_0_), channel_id=1, source_target_pairs={{0,2},{2,0},{4,6},{6,4},{8,10},{10,8},{12,14},{14,12},{16,18},{18,... | collective-permute-start | bytes 1572872 | tf_op jit(solution)/shard_map/ppermute | solution.py:50

commit v5 on v4

--- a/solution.py
+++ b/solution.py
@@ -39,7 +39,8 @@
 X_SIDE = shift(lambda y, z, x, c: (y, z, x + side(c), c))
 X_BACK = shift(lambda y, z, x, c: (y, z, x - side(c), c))
 CORE_PAIR = shift(lambda y, z, x, c: (y, z, x, c + 1))
-PARTS = [(t, b, back) for b in range(2) for t in range(NY) for back in (0, 4, 2, 6)]
+BACKS = (4, 2, 6)
+PARTS = [(t, b, back) for b in range(2) for t in range(NY) for back in (0, *BACKS)]
 
 
 def cost(flops, bytes_accessed):
@@ -48,6 +49,14 @@
 
 def send(block, pairs):
     return lax.ppermute(block, "dap", pairs)
+
+
+def join(blocks):
+    rows = blocks[0].shape[0]
+    whole = jnp.zeros((rows * len(blocks), blocks[0].shape[1]), blocks[0].dtype)
+    for k, block in enumerate(blocks):
+        whole = lax.dynamic_update_slice(whole, block, (k * rows, 0))
+    return whole
 
 
 def layer_norm(feats, gain, offset):
@@ -87,7 +96,7 @@
     normed = normed.reshape(SEQS * rows, -1).astype(jnp.bfloat16)
     right = dot_last(normed, weight_ref[...]) + bias_ref[...]
     right_ref[...] = right.astype(jnp.bfloat16)
-    step = 2
+    step = 16
 
     def body(b, carry):
         start = pl.multiple_of(b * step * rows, step * rows)
@@ -113,8 +122,11 @@
     table_ref, bias_ref = refs[len(pieces) : len(pieces) + 2]
     out_ref, left_all, acc_ref, ready, sems = refs[len(pieces) + 2 + aliased :]
     rows = lefts[0].shape[0]
-    for n, left_ref in enumerate(lefts):
-        left_all[n * rows : (n + 1) * rows, :] = left_ref[...]
+    if len(lefts) == 1:
+        left_all = lefts[0]
+    else:
+        for n, left_ref in enumerate(lefts):
+            left_all[n * rows : (n + 1) * rows, :] = left_ref[...]
     acc_ref[...] = jnp.dot(left_all[...], table_ref[...], preferred_element_type=jnp.float32)
     me = lax.axis_index("dap")
     core = lax.rem(me, NC)
@@ -206,10 +218,8 @@
 
     bias = output_bias[None]
 
-    ring = jnp.concatenate([left] + [send(left, Z_EVEN[k]) for k in (4, 2, 6)], axis=0)
-    block = jnp.concatenate(
-        [ring, send(ring, Y_PAIR), send(ring, Z_PAIR), send(ring, YZ_PAIR)], axis=0
-    )
+    ring = join([left] + [send(left, Z_EVEN[k]) for k in BACKS])
+    block = join([ring, send(ring, Y_PAIR), send(ring, Z_PAIR), send(ring, YZ_PAIR)])
     ahead, behind = send(block, X_BACK), send(block, X_SIDE)
     out = pair_block([block, send(block, CORE_PAIR)], [(0, 0), (1, 0)], table, bias, None)
     ahead, behind, table, out = lax.optimization_barrier((ahead, behind, table, out))

time: 56.8 us -> 55.3 us (0.974)
  Pallas kernels: 18.7 us -> 15.3 us
  waiting for transfers between devices: 12.5 us -> 14.7 us
  starting transfers between devices: 22.2 us -> 23.6 us
  local copies, waits for them, and re-layouts: 2.02 us -> 1.12 us
  other arithmetic: 0.77 us -> 0 us
    pallas_call x1, Pallas kernels: 6.75 us -> 3.34 us  [per_device(): pl.pallas_call(table_kernel, out_shape=jax.ShapeDtypeStruct((SEQS * HID,...]
    ppermute x13, waiting for transfers between devices: 12.5 us -> 14.7 us  [send(): return lax.ppermute(block, 'dap', pairs)]
    ppermute x13, starting transfers between devices: 22.2 us -> 23.6 us  [send(): return lax.ppermute(block, 'dap', pairs)]
    reshape x1, local copies, waits for them, and re-layouts: 1.05 us -> 0.1 us  [per_device(): output_weight.reshape(HID, HID, C_Z).transpose(1, 0, 2)]
    dynamic_update_slice x0 -> x8, local copies, waits for them, and re-layouts: none -> 0.88 us  [join(): whole = lax.dynamic_update_slice(whole, block, (k * rows, 0))]
    unnamed x19 -> x15, local copies, waits for them, and re-layouts: 0.96 us -> 0.14 us
    concatenate x1 -> x0, other arithmetic: 0.77 us -> none  [per_device(): jnp.concatenate([left] + [send(left, Z_EVEN[k]) for k in (4, 2, 6)], axis=0)]
  transfers between devices with their start and end apart: 13 -> 13, of which waited for: 6 -> 6; matrix products, arithmetic and copies ran while one was open for 4% -> 2% of each run, Pallas kernels for 27% -> 21%
where the time goes in v5:
time: 55.3 us; the launch traced here: 55.1 us
  starting transfers between devices  23.6 us (43%)
  Pallas kernels  15.3 us (28%)
  waiting for transfers between devices  14.7 us (27%)
  local copies, waits for them, and re-layouts  1.12 us (2%)
    ppermute x13, starting transfers between devices, send(): return lax.ppermute(block, 'dap', pairs)  23.6 us
    ppermute x13, waiting for transfers between devices, send(): return lax.ppermute(block, 'dap', pairs)  14.7 us
    pallas_call x5, Pallas kernels, pair_block(): pl.pallas_call(functools.partial(pair_kernel, pieces=pieces, aliased=int(...  9.89 us
    pallas_call x1, Pallas kernels, per_device(): pl.pallas_call(table_kernel, out_shape=jax.ShapeDtypeStruct((SEQS * HID,...  3.34 us
    pallas_call x1, Pallas kernels, per_device(): pl.pallas_call(left_kernel, out_shape=jax.ShapeDtypeStruct((rows, SEQS *...  2.06 us
  transfers between devices with their start and end apart: 13, of which 6 were waited for; matrix products, arithmetic and copies ran while one was open for 2% of the time, Pallas kernels for 21%

profile of v5, /device:TPU:1, one launch (start us, length us, event | category | flops | bytes accessed | tf_op | source)
XLA Modules:
  0.0 55.1 jit_solution(5696335590201530620)
XLA Ops:
  0.0 0.0 copy-start
  0.0 0.0 copy-start.6
  0.0 0.0 copy-start.5
  0.0 0.0 copy-start.1
  0.0 2.1 %shard_map.91 = bf16[8,2048]{1,0:T(8,128)(2,1)} custom-call(bf16[64,8,256]{2,1,0:T(8,128)(2,1)} %feats_ref.3, f32[1,256]{1,0:T(1,128)} %bitcast.21, f32[1,256]{1,0:T(1,128)} %bitcast.23, bf16[32,256]{1,0:T(8,128)(2,1)} %bitcast.28, f32[1,32]{1,0:T(1,128)} %bitcast.29), custom_call_target="tpu_custom_call" | custom-call | tf_op jit(solution)/shard_map/pallas_call | solution.py:192
  2.1 7.7 %collective-permute-start = (bf16[8,2048]{1,0:T(8,128)(2,1)}, bf16[8,2048]{1,0:T(8,128)(2,1)S(1)}, u32[]{:S(2)}, u32[]{:S(2)}) collective-permute-start(bf16[8,2048]{1,0:T(8,128)(2,1)} %shard_map.91), channel_id=1, source_target_pairs={{0,64},{2,66},{4,68},{6,70},{8,72},{10,74},{12,76},{14,78},{16,80}... | collective-permute-start | bytes 98312 | tf_op jit(solution)/shard_map/ppermute | solution.py:51
  9.8 0.0 collective-permute-start.2
  9.8 2.4 %collective-permute-start.1 = (bf16[8,2048]{1,0:T(8,128)(2,1)}, bf16[8,2048]{1,0:T(8,128)(2,1)S(1)}, u32[]{:S(2)}, u32[]{:S(2)}) collective-permute-start(bf16[8,2048]{1,0:T(8,128)(2,1)} %shard_map.91), channel_id=1, source_target_pairs={{0,32},{2,34},{4,36},{6,38},{8,40},{10,42},{12,44},{14,46},{16,48}... | collective-permute-start | bytes 98312 | tf_op jit(solution)/shard_map/ppermute | solution.py:51
  12.2 0.8 %dynamic_update_slice.24 = bf16[32,2048]{1,0:T(8,128)(2,1)S(1)} pad(bf16[8,2048]{1,0:T(8,128)(2,1)} %shard_map.91, bf16[]{:T(256)} %constant.8.clone.1), padding=0_24x0_0 | pad | bytes 163842 | tf_op jit(solution)/shard_map/dynamic_update_slice | solution.py:58
  13.0 0.0 collective-permute-done
  13.0 2.0 %collective-permute-done.1 = bf16[8,2048]{1,0:T(8,128)(2,1)S(1)} collective-permute-done((bf16[8,2048]{1,0:T(8,128)(2,1)}, bf16[8,2048]{1,0:T(8,128)(2,1)S(1)}, u32[]{:S(2)}, u32[]{:S(2)}) %collective-permute-start.1) | collective-permute-done | bytes 32800 | tf_op jit(solution)/shard_map/ppermute | solution.py:51
  15.0 0.0 collective-permute-done.2
  15.0 1.4 %collective-permute-start.3 = (bf16[32,2048]{1,0:T(8,128)(2,1)S(1)}, bf16[32,2048]{1,0:T(8,128)(2,1)S(1)}, u32[]{:S(2)}, u32[]{:S(2)}) collective-permute-start(bf16[32,2048]{1,0:T(8,128)(2,1)S(1)} %constant_dynamic-update-slice_fusion.3), channel_id=1, source_target_pairs={{0,128},{2,130},{4,132},{6,134},{8,136},{10,138},{12,140},{14,142}... | collective-permute-start | bytes 393224 | tf_op jit(solution)/shard_map/ppermute | solution.py:51
  16.4 1.1 %collective-permute-start.5 = (bf16[32,2048]{1,0:T(8,128)(2,1)S(1)}, bf16[32,2048]{1,0:T(8,128)(2,1)S(1)}, u32[]{:S(2)}, u32[]{:S(2)}) collective-permute-start(bf16[32,2048]{1,0:T(8,128)(2,1)S(1)} %constant_dynamic-update-slice_fusion.3), channel_id=1, source_target_pairs={{0,144},{2,146},{4,148},{6,150},{8,152},{10,154},{12,156},{14,158}... | collective-permute-start | bytes 393224 | tf_op jit(solution)/shard_map/ppermute | solution.py:51
  17.6 0.2 collective-permute-start.4
  17.8 1.9 %collective-permute-done.3 = bf16[32,2048]{1,0:T(8,128)(2,1)S(1)} collective-permute-done((bf16[32,2048]{1,0:T(8,128)(2,1)S(1)}, bf16[32,2048]{1,0:T(8,128)(2,1)S(1)}, u32[]{:S(2)}, u32[]{:S(2)}) %collective-permute-start.3) | collective-permute-done | bytes 131104 | tf_op jit(solution)/shard_map/ppermute | solution.py:51
  19.8 2.1 %collective-permute-done.4 = bf16[32,2048]{1,0:T(8,128)(2,1)S(1)} collective-permute-done((bf16[32,2048]{1,0:T(8,128)(2,1)S(1)}, bf16[32,2048]{1,0:T(8,128)(2,1)S(1)}, u32[]{:S(2)}, u32[]{:S(2)}) %collective-permute-start.4) | collective-permute-done | bytes 131104 | tf_op jit(solution)/shard_map/ppermute | solution.py:51
  21.9 0.0 collective-permute-done.5
  21.9 3.6 %collective-permute-start.8 = (bf16[128,2048]{1,0:T(8,128)(2,1)S(1)}, bf16[128,2048]{1,0:T(8,128)(2,1)S(1)}, u32[]{:S(2)}, u32[]{:S(2)}) collective-permute-start(bf16[128,2048]{1,0:T(8,128)(2,1)S(1)} %constant_dynamic-update-slice_fusion.refs_0_), channel_id=1, source_target_pairs={{0,2},{2,0},{4,6},{6,4},{8,10},{10,8},{12,14},{14,12},{16,18},{18,... | collective-permute-start | bytes 1572872 | tf_op jit(solution)/shard_map/ppermute | solution.py:51
  25.5 2.5 %collective-permute-start.7 = (bf16[128,2048]{1,0:T(8,128)(2,1)S(1)}, bf16[128,2048]{1,0:T(8,128)(2,1)S(1)}, u32[]{:S(2)}, u32[]{:S(2)}) collective-permute-start(bf16[128,2048]{1,0:T(8,128)(2,1)S(1)} %constant_dynamic-update-slice_fusion.refs_0_), channel_id=1, source_target_pairs={{0,4},{2,14},{4,8},{6,2},{8,12},{10,6},{12,0},{14,10},{16,20},{18,... | collective-permute-start | bytes 1572872 | tf_op jit(solution)/shard_map/ppermute | solution.py:51
  28.0 0.0 collective-permute-start.6
  28.0 0.0 copy-done.6
  28.0 0.1 copy.14
  28.1 0.1 copy.17
  28.2 0.0 copy-done
  28.2 0.0 copy-done.4
  28.2 0.0 copy-done.3
  28.3 0.0 copy-done.5
  28.3 0.0 copy-done.1
  28.3 0.0 copy-start.2
  28.3 3.3 %shard_map.92.refs_2_.refs_1_ = bf16[2048,1024]{1,0:T(8,128)(2,1)S(1)} custom-call(bf16[64,8,256]{2,1,0:T(8,128)(2,1)S(1)} %copy-done, f32[1,256]{1,0:T(1,128)S(1)} %bitcast.22, f32[1,256]{1,0:T(1,128)S(1)} %bitcast.24, bf16[32,256]{1,0:T(8,128)(2,1)S(1)} %bitcast.15, f32[1,32]{1,0:T(1,128)S(1)} %bitcast.25, bf16[32,4096]{1,0:T(8,128)(2,1)S(1)} %bitcast.14), custom_call_target="tpu_custom_call" | custom-call | flops 1073741824 | bytes 25165824 | tf_op jit(solution)/shard_map/pallas_call | solution.py:204
  31.6 0.0 collective-permute-done.8.refs_1_
  31.6 0.0 copy-done.2
  31.7 2.3 %shard_map.93.refs_4_ = bf16[128,8,8,128]{3,2,1,0:T(8,128)(2,1)} custom-call(bf16[128,2048]{1,0:T(8,128)(2,1)S(1)} %constant_dynamic-update-slice_fusion.refs_0_, bf16[128,2048]{1,0:T(8,128)(2,1)S(1)} %collective-permute-done.8.refs_1_, bf16[2048,1024]{1,0:T(8,128)(2,1)S(1)} %shard_map.92.refs_2_.refs_1_, f32[1,128]{1,0:T(1,128)S(1)} %bitcast.16), custom_call_target="tpu_custom_call" | custom-call | flops 1073741824 | bytes 10485760 | tf_op jit(solution)/shard_map/pallas_call | solution.py:161
  33.9 4.8 %collective-permute-done.7.refs_1_ = bf16[128,2048]{1,0:T(8,128)(2,1)S(1)} collective-permute-done((bf16[128,2048]{1,0:T(8,128)(2,1)S(1)}, bf16[128,2048]{1,0:T(8,128)(2,1)S(1)}, u32[]{:S(2)}, u32[]{:S(2)}) %collective-permute-start.7) | collective-permute-done | bytes 524320 | tf_op jit(solution)/shard_map/ppermute | solution.py:51
  38.7 2.2 %collective-permute-done.6.refs_0_ = bf16[128,2048]{1,0:T(8,128)(2,1)S(1)} collective-permute-done((bf16[128,2048]{1,0:T(8,128)(2,1)S(1)}, bf16[128,2048]{1,0:T(8,128)(2,1)S(1)}, u32[]{:S(2)}, u32[]{:S(2)}) %collective-permute-start.6) | collective-permute-done | bytes 524320 | tf_op jit(solution)/shard_map/ppermute | solution.py:51
  40.9 0.0 collective-permute-start.10
  40.9 0.5 collective-permute-start.11
  41.4 2.1 %collective-permute-start.9 = (bf16[128,2048]{1,0:T(8,128)(2,1)S(1)}, bf16[128,2048]{1,0:T(8,128)(2,1)S(1)}, u32[]{:S(2)}, u32[]{:S(2)}) collective-permute-start(bf16[128,2048]{1,0:T(8,128)(2,1)S(1)} %collective-permute-done.7.refs_1_), channel_id=1, source_target_pairs={{0,4},{2,14},{4,8},{6,2},{8,12},{10,6},{12,0},{14,10},{16,20},{18,... | collective-permute-start | bytes 1572872 | tf_op jit(solution)/shard_map/ppermute | solution.py:51
  43.6 2.3 %shard_map.94.refs_4_ = bf16[128,8,8,128]{3,2,1,0:T(8,128)(2,1)} custom-call(bf16[128,2048]{1,0:T(8,128)(2,1)S(1)} %collective-permute-done.6.refs_0_, bf16[128,2048]{1,0:T(8,128)(2,1)S(1)} %collective-permute-done.7.refs_1_, bf16[2048,1024]{1,0:T(8,128)(2,1)S(1)} %shard_map.92.refs_2_.refs_1_, ...), custom_call_target="tpu_custom_call", output_to_operand_aliasing={{}: (4, {})} | custom-call | flops 1073741824 | bytes 10485760 | tf_op jit(solution)/shard_map/pallas_call | solution.py:161
  45.8 0.0 collective-permute-done.10.refs_0_
  45.8 0.0 collective-permute-done.11.refs_1_
  45.8 2.3 %shard_map.95.refs_3_ = bf16[128,8,8,128]{3,2,1,0:T(8,128)(2,1)} custom-call(bf16[128,2048]{1,0:T(8,128)(2,1)S(1)} %collective-permute-done.10.refs_0_, bf16[128,2048]{1,0:T(8,128)(2,1)S(1)} %collective-permute-done.11.refs_1_, bf16[2048,1024]{1,0:T(8,128)(2,1)S(1)} %shard_map.92.refs_2_.refs_1_, ...), custom_call_target="tpu_custom_call", output_to_operand_aliasing={{}: (4, {})} | custom-call | flops 1073741824 | bytes 10485760 | tf_op jit(solution)/shard_map/pallas_call | solution.py:161
  48.1 1.6 %collective-permute-done.9.refs_0_ = bf16[128,2048]{1,0:T(8,128)(2,1)S(1)} collective-permute-done((bf16[128,2048]{1,0:T(8,128)(2,1)S(1)}, bf16[128,2048]{1,0:T(8,128)(2,1)S(1)}, u32[]{:S(2)}, u32[]{:S(2)}) %collective-permute-start.9) | collective-permute-done | bytes 524320 | tf_op jit(solution)/shard_map/ppermute | solution.py:51
  49.8 2.1 %collective-permute-start.12 = (bf16[128,2048]{1,0:T(8,128)(2,1)S(1)}, bf16[128,2048]{1,0:T(8,128)(2,1)S(1)}, u32[]{:S(2)}, u32[]{:S(2)}) collective-permute-start(bf16[128,2048]{1,0:T(8,128)(2,1)S(1)} %collective-permute-done.9.refs_0_), channel_id=1, source_target_pairs={{0,2},{2,0},{4,6},{6,4},{8,10},{10,8},{12,14},{14,12},{16,18},{18,... | collective-permute-start | bytes 1572872 | tf_op jit(solution)/shard_map/ppermute | solution.py:51
  51.8 1.5 %shard_map.96.refs_3_ = bf16[128,8,8,128]{3,2,1,0:T(8,128)(2,1)} custom-call(bf16[128,2048]{1,0:T(8,128)(2,1)S(1)} %collective-permute-done.9.refs_0_, bf16[2048,1024]{1,0:T(8,128)(2,1)S(1)} %shard_map.92.refs_2_.refs_1_, f32[1,128]{1,0:T(1,128)S(1)} %bitcast.19, bf16[128,8,8,128]{3,2,1,0:T(8,128)(2,1)} %shard_map.95.refs_3_), custom_call_target="tpu_custom_call", output_to_operand_aliasing={{}: (3, {})} | custom-call | flops 536870912 | bytes 10485760 | tf_op jit(solution)/shard_map/pallas_call | solution.py:161
  53.4 0.0 collective-permute-done.12.refs_0_
  53.4 1.5 %shard_map.97 = bf16[128,8,8,128]{3,2,1,0:T(8,128)(2,1)} custom-call(bf16[128,2048]{1,0:T(8,128)(2,1)S(1)} %collective-permute-done.12.refs_0_, bf16[2048,1024]{1,0:T(8,128)(2,1)S(1)} %shard_map.92.refs_2_.refs_1_, f32[1,128]{1,0:T(1,128)S(1)} %bitcast.20, bf16[128,8,8,128]{3,2,1,0:T(8,128)(2,1)} %shard_map.96.refs_3_), custom_call_target="tpu_custom_call", output_to_operand_aliasing={{}: (3, {})} | custom-call | flops 536870912 | bytes 10485760 | tf_op jit(solution)/shard_map/pallas_call | solution.py:161
  (9 shorter events, 0.1 us)
Async XLA Ops:
  0.0 28.2 %copy-start = (bf16[64,8,256]{2,1,0:T(8,128)(2,1)S(1)}, bf16[64,8,256]{2,1,0:T(8,128)(2,1)}, u32[]{:S(2)}) copy-start(bf16[64,8,256]{2,1,0:T(8,128)(2,1)} %feats_ref.3) | copy-start | bytes 786436
  0.0 28.2 %copy-start.4 = (f32[256]{0:T(256)S(1)}, f32[256]{0:T(256)}, u32[]{:S(2)}) copy-start(f32[256]{0:T(256)} %param.11) | copy-start | bytes 3076
  0.0 28.2 %copy-start.3 = (f32[256]{0:T(256)S(1)}, f32[256]{0:T(256)}, u32[]{:S(2)}) copy-start(f32[256]{0:T(256)} %param.10) | copy-start | bytes 3076
  0.0 28.0 %copy-start.6 = (bf16[1024,128]{1,0:T(8,128)(2,1)S(1)}, bf16[1024,128]{1,0:T(8,128)(2,1)}, u32[]{:S(2)}) copy-start(bf16[1024,128]{1,0:T(8,128)(2,1)} %param.16) | copy-start | bytes 786436
  0.0 28.2 %copy-start.5 = (f32[32]{0:T(128)S(1)}, f32[32]{0:T(128)}, u32[]{:S(2)}) copy-start(f32[32]{0:T(128)} %param.15) | copy-start | bytes 388
  0.0 28.2 %copy-start.1 = (bf16[256,32]{0,1:T(8,128)(2,1)S(1)}, bf16[256,32]{0,1:T(8,128)(2,1)}, u32[]{:S(2)}) copy-start(bf16[256,32]{0,1:T(8,128)(2,1)} %param.14) | copy-start | bytes 49156
  2.1 10.9 %collective-permute-start = (bf16[8,2048]{1,0:T(8,128)(2,1)}, bf16[8,2048]{1,0:T(8,128)(2,1)S(1)}, u32[]{:S(2)}, u32[]{:S(2)}) collective-permute-start(bf16[8,2048]{1,0:T(8,128)(2,1)} %shard_map.91), channel_id=1, source_target_pairs={{0,64},{2,66},{4,68},{6,70},{8,72},{10,74},{12,76},{14,78},{16,80}... | collective-permute-start | bytes 98312 | tf_op jit(solution)/shard_map/ppermute | solution.py:51
  9.8 5.2 %collective-permute-start.2 = (bf16[8,2048]{1,0:T(8,128)(2,1)}, bf16[8,2048]{1,0:T(8,128)(2,1)S(1)}, u32[]{:S(2)}, u32[]{:S(2)}) collective-permute-start(bf16[8,2048]{1,0:T(8,128)(2,1)} %shard_map.91), channel_id=1, source_target_pairs={{0,96},{2,98},{4,100},{6,102},{8,104},{10,106},{12,108},{14,110},{... | collective-permute-start | bytes 98312 | tf_op jit(solution)/shard_map/ppermute | solution.py:51
  9.8 5.2 %collective-permute-start.1 = (bf16[8,2048]{1,0:T(8,128)(2,1)}, bf16[8,2048]{1,0:T(8,128)(2,1)S(1)}, u32[]{:S(2)}, u32[]{:S(2)}) collective-permute-start(bf16[8,2048]{1,0:T(8,128)(2,1)} %shard_map.91), channel_id=1, source_target_pairs={{0,32},{2,34},{4,36},{6,38},{8,40},{10,42},{12,44},{14,46},{16,48}... | collective-permute-start | bytes 98312 | tf_op jit(solution)/shard_map/ppermute | solution.py:51
  15.0 4.7 %collective-permute-start.3 = (bf16[32,2048]{1,0:T(8,128)(2,1)S(1)}, bf16[32,2048]{1,0:T(8,128)(2,1)S(1)}, u32[]{:S(2)}, u32[]{:S(2)}) collective-permute-start(bf16[32,2048]{1,0:T(8,128)(2,1)S(1)} %constant_dynamic-update-slice_fusion.3), channel_id=1, source_target_pairs={{0,128},{2,130},{4,132},{6,134},{8,136},{10,138},{12,140},{14,142}... | collective-permute-start | bytes 393224 | tf_op jit(solution)/shard_map/ppermute | solution.py:51
  16.4 5.5 %collective-permute-start.5 = (bf16[32,2048]{1,0:T(8,128)(2,1)S(1)}, bf16[32,2048]{1,0:T(8,128)(2,1)S(1)}, u32[]{:S(2)}, u32[]{:S(2)}) collective-permute-start(bf16[32,2048]{1,0:T(8,128)(2,1)S(1)} %constant_dynamic-update-slice_fusion.3), channel_id=1, source_target_pairs={{0,144},{2,146},{4,148},{6,150},{8,152},{10,154},{12,156},{14,158}... | collective-permute-start | bytes 393224 | tf_op jit(solution)/shard_map/ppermute | solution.py:51
  17.6 4.3 %collective-permute-start.4 = (bf16[32,2048]{1,0:T(8,128)(2,1)S(1)}, bf16[32,2048]{1,0:T(8,128)(2,1)S(1)}, u32[]{:S(2)}, u32[]{:S(2)}) collective-permute-start(bf16[32,2048]{1,0:T(8,128)(2,1)S(1)} %constant_dynamic-update-slice_fusion.3), channel_id=1, source_target_pairs={{0,16},{2,18},{4,20},{6,22},{8,24},{10,26},{12,28},{14,30},{16,0},... | collective-permute-start | bytes 393224 | tf_op jit(solution)/shard_map/ppermute | solution.py:51
  21.9 9.7 %collective-permute-start.8 = (bf16[128,2048]{1,0:T(8,128)(2,1)S(1)}, bf16[128,2048]{1,0:T(8,128)(2,1)S(1)}, u32[]{:S(2)}, u32[]{:S(2)}) collective-permute-start(bf16[128,2048]{1,0:T(8,128)(2,1)S(1)} %constant_dynamic-update-slice_fusion.refs_0_), channel_id=1, source_target_pairs={{0,2},{2,0},{4,6},{6,4},{8,10},{10,8},{12,14},{14,12},{16,18},{18,... | collective-permute-start | bytes 1572872 | tf_op jit(solution)/shard_map/ppermute | solution.py:51
  25.5 13.2 %collective-permute-start.7 = (bf16[128,2048]{1,0:T(8,128)(2,1)S(1)}, bf16[128,2048]{1,0:T(8,128)(2,1)S(1)}, u32[]{:S(2)}, u32[]{:S(2)}) collective-permute-start(bf16[128,2048]{1,0:T(8,128)(2,1)S(1)} %constant_dynamic-update-slice_fusion.refs_0_), channel_id=1, source_target_pairs={{0,4},{2,14},{4,8},{6,2},{8,12},{10,6},{12,0},{14,10},{16,20},{18,... | collective-permute-start | bytes 1572872 | tf_op jit(solution)/shard_map/ppermute | solution.py:51
  28.0 12.9 %collective-permute-start.6 = (bf16[128,2048]{1,0:T(8,128)(2,1)S(1)}, bf16[128,2048]{1,0:T(8,128)(2,1)S(1)}, u32[]{:S(2)}, u32[]{:S(2)}) collective-permute-start(bf16[128,2048]{1,0:T(8,128)(2,1)S(1)} %constant_dynamic-update-slice_fusion.refs_0_), channel_id=1, source_target_pairs={{0,12},{2,6},{4,0},{6,10},{8,4},{10,14},{12,8},{14,2},{16,28},{18,... | collective-permute-start | bytes 1572872 | tf_op jit(solution)/shard_map/ppermute | solution.py:51
  28.3 3.4 %copy-start.2 = (f32[128]{0:T(128)S(1)}, f32[128]{0:T(128)}, u32[]{:S(2)}) copy-start(f32[128]{0:T(128)} %param.17) | copy-start | bytes 1540
  40.9 4.9 %collective-permute-start.10 = (bf16[128,2048]{1,0:T(8,128)(2,1)S(1)}, bf16[128,2048]{1,0:T(8,128)(2,1)S(1)}, u32[]{:S(2)}, u32[]{:S(2)}) collective-permute-start(bf16[128,2048]{1,0:T(8,128)(2,1)S(1)} %collective-permute-done.6.refs_0_), channel_id=1, source_target_pairs={{0,2},{2,0},{4,6},{6,4},{8,10},{10,8},{12,14},{14,12},{16,18},{18,... | collective-permute-start | bytes 1572872 | tf_op jit(solution)/shard_map/ppermute | solution.py:51
  40.9 4.9 %collective-permute-start.11 = (bf16[128,2048]{1,0:T(8,128)(2,1)S(1)}, bf16[128,2048]{1,0:T(8,128)(2,1)S(1)}, u32[]{:S(2)}, u32[]{:S(2)}) collective-permute-start(bf16[128,2048]{1,0:T(8,128)(2,1)S(1)} %collective-permute-done.7.refs_1_), channel_id=1, source_target_pairs={{0,2},{2,0},{4,6},{6,4},{8,10},{10,8},{12,14},{14,12},{16,18},{18,... | collective-permute-start | bytes 1572872 | tf_op jit(solution)/shard_map/ppermute | solution.py:51
  41.4 8.3 %collective-permute-start.9 = (bf16[128,2048]{1,0:T(8,128)(2,1)S(1)}, bf16[128,2048]{1,0:T(8,128)(2,1)S(1)}, u32[]{:S(2)}, u32[]{:S(2)}) collective-permute-start(bf16[128,2048]{1,0:T(8,128)(2,1)S(1)} %collective-permute-done.7.refs_1_), channel_id=1, source_target_pairs={{0,4},{2,14},{4,8},{6,2},{8,12},{10,6},{12,0},{14,10},{16,20},{18,... | collective-permute-start | bytes 1572872 | tf_op jit(solution)/shard_map/ppermute | solution.py:51
  49.8 3.6 %collective-permute-start.12 = (bf16[128,2048]{1,0:T(8,128)(2,1)S(1)}, bf16[128,2048]{1,0:T(8,128)(2,1)S(1)}, u32[]{:S(2)}, u32[]{:S(2)}) collective-permute-start(bf16[128,2048]{1,0:T(8,128)(2,1)S(1)} %collective-permute-done.9.refs_0_), channel_id=1, source_target_pairs={{0,2},{2,0},{4,6},{6,4},{8,10},{10,8},{12,14},{14,12},{16,18},{18,... | collective-permute-start | bytes 1572872 | tf_op jit(solution)/shard_map/ppermute | solution.py:51

commit v6 on v5

--- a/solution.py
+++ b/solution.py
@@ -137,8 +137,10 @@
     for n, (lane, ahead) in enumerate(pieces):
         c = core if lane == 0 else 1 - core
         to_x = lax.rem(x + ahead * side(core) + NX, NX)
-        for k, (t, b, back) in enumerate(PARTS):
-            slot = n * len(PARTS) + k
+        count = rows // 8
+        first = n * count % len(PARTS)
+        for k, (t, b, back) in enumerate(PARTS[first : first + count]):
+            slot = n * count + k
             part = acc_ref[slot * 8 : slot * 8 + 8, :].reshape(8, 8, C_Z) + bias_ref[...]
             ready[slot] = part.astype(jnp.bfloat16)
             to_y = lax.rem(y + t, NY)
@@ -151,7 +153,7 @@
         copy.wait()
 
 
-def pair_block(lefts, pieces, table, bias, out):
+def pair_block(lefts, pieces, table, bias, out, reach=10 << 20):
     aliased = out is not None
     vmem, anywhere = pl.BlockSpec(memory_space=pltpu.VMEM), pl.BlockSpec(memory_space=pl.ANY)
     operands = [*lefts, table, bias] + ([out] if aliased else [])
@@ -171,7 +173,7 @@
         ],
         input_output_aliases={len(operands) - 1: 0} if aliased else {},
         compiler_params=pltpu.CompilerParams(vmem_limit_bytes=24 * 1024 * 1024),
-        cost_estimate=cost(2 * rows * depth * width, 10 << 20),
+        cost_estimate=cost(2 * rows * depth * width, reach),
     )(*operands)
 
 
@@ -191,7 +193,8 @@
     vmem = pltpu.CompilerParams(vmem_limit_bytes=32 * 1024 * 1024)
     left = pl.pallas_call(
         left_kernel,
-        out_shape=jax.ShapeDtypeStruct((rows, SEQS * HID), jnp.bfloat16),
+        out_shape=pltpu.VMEM((rows, SEQS * HID), jnp.bfloat16),
+        out_specs=pl.BlockSpec(memory_space=pltpu.VMEM),
         compiler_params=pltpu.CompilerParams(vmem_limit_bytes=60 * 1024 * 1024),
     )(
         alignment_features,
@@ -223,10 +226,12 @@
     ahead, behind = send(block, X_BACK), send(block, X_SIDE)
     out = pair_block([block, send(block, CORE_PAIR)], [(0, 0), (1, 0)], table, bias, None)
     ahead, behind, table, out = lax.optimization_barrier((ahead, behind, table, out))
-    others = [send(ahead, CORE_PAIR), send(behind, CORE_PAIR)]
     far = send(behind, X_SIDE)
-    out = pair_block([ahead, behind], [(0, 1), (0, -1)], table, bias, out)
-    out = pair_block(others, [(1, -1), (1, 1)], table, bias, out)
+    out = pair_block([ahead, behind], [(0, 1), (0, -1)], table, bias, out, 100 << 20)
+    ahead, behind, out = lax.optimization_barrier((ahead, behind, out))
+    half = block.shape[0] // 2
+    others = [send(part, CORE_PAIR) for b in (ahead, behind) for part in (b[:half], b[half:])]
+    out = pair_block(others, [(1, -1), (1, -1), (1, 1), (1, 1)], table, bias, out, 1 << 10)
     far, out = lax.optimization_barrier((far, out))
     far_other = send(far, CORE_PAIR)
     out = pair_block([far], [(0, 2)], table, bias, out)

time: 55.3 us -> 53.6 us (0.969)
  local copies, waits for them, and re-layouts: 1.12 us -> 0.4 us
  Pallas kernels: 15.3 us -> 14.7 us
  starting transfers between devices: 23.6 us -> 23 us
    dynamic_update_slice x8, local copies, waits for them, and re-layouts: 0.88 us -> 0.09 us  [join(): whole = lax.dynamic_update_slice(whole, block, (k * rows, 0))]
    ppermute x13 -> x15, starting transfers between devices: 23.6 us -> 23 us  [send(): return lax.ppermute(block, 'dap', pairs)]
    pallas_call x1, Pallas kernels: 2.06 us -> 1.44 us  [per_device(): pl.pallas_call(left_kernel, out_shape=pltpu.VMEM((rows, SEQS * HID), jnp....]
    ppermute x13 -> x15, waiting for transfers between devices: 14.7 us -> 15 us  [send(): return lax.ppermute(block, 'dap', pairs)]
  transfers between devices with their start and end apart: 13 -> 15, of which waited for: 6 -> 9; matrix products, arithmetic and copies ran while one was open for 2% -> 1% of each run, Pallas kernels for 21% -> 22%
where the time goes in v6:
time: 53.6 us; the launch traced here: 53.5 us
  starting transfers between devices  23 us (43%)
  waiting for transfers between devices  15 us (28%)
  Pallas kernels  14.7 us (27%)
    ppermute x15, starting transfers between devices, send(): return lax.ppermute(block, 'dap', pairs)  23 us
    ppermute x15, waiting for transfers between devices, send(): return lax.ppermute(block, 'dap', pairs)  15 us
    pallas_call x5, Pallas kernels, pair_block(): pl.pallas_call(functools.partial(pair_kernel, pieces=pieces, aliased=int(...  9.93 us
    pallas_call x1, Pallas kernels, per_device(): pl.pallas_call(table_kernel, out_shape=jax.ShapeDtypeStruct((SEQS * HID,...  3.32 us
    pallas_call x1, Pallas kernels, per_device(): pl.pallas_call(left_kernel, out_shape=pltpu.VMEM((rows, SEQS * HID), jnp....  1.44 us
  transfers between devices with their start and end apart: 15, of which 9 were waited for; matrix products, arithmetic and copies ran while one was open for 1% of the time, Pallas kernels for 22%

profile of v6, /device:TPU:1, one launch (start us, length us, event | category | flops | bytes accessed | tf_op | source)
XLA Modules:
  0.0 53.5 jit_solution(10843500625864802889)
XLA Ops:
  0.0 0.0 copy-start.6
  0.0 0.0 copy-start.5
  0.0 0.0 copy-start.1
  0.0 1.4 %shard_map.91 = bf16[8,2048]{1,0:T(8,128)(2,1)S(1)} custom-call(bf16[64,8,256]{2,1,0:T(8,128)(2,1)} %feats_ref.3, f32[1,256]{1,0:T(1,128)} %bitcast.21, f32[1,256]{1,0:T(1,128)} %bitcast.23, bf16[32,256]{1,0:T(8,128)(2,1)} %bitcast.28, f32[1,32]{1,0:T(1,128)} %bitcast.29), custom_call_target="tpu_custom_call" | custom-call | tf_op jit(solution)/shard_map/pallas_call | solution.py:194
  1.5 7.8 %collective-permute-start = (bf16[8,2048]{1,0:T(8,128)(2,1)S(1)}, bf16[8,2048]{1,0:T(8,128)(2,1)S(1)}, u32[]{:S(2)}, u32[]{:S(2)}) collective-permute-start(bf16[8,2048]{1,0:T(8,128)(2,1)S(1)} %shard_map.91), channel_id=1, source_target_pairs={{0,64},{2,66},{4,68},{6,70},{8,72},{10,74},{12,76},{14,78},{16,80}... | collective-permute-start | bytes 98312 | tf_op jit(solution)/shard_map/ppermute | solution.py:51
  9.3 0.0 collective-permute-start.2
  9.3 2.4 %collective-permute-start.1 = (bf16[8,2048]{1,0:T(8,128)(2,1)S(1)}, bf16[8,2048]{1,0:T(8,128)(2,1)S(1)}, u32[]{:S(2)}, u32[]{:S(2)}) collective-permute-start(bf16[8,2048]{1,0:T(8,128)(2,1)S(1)} %shard_map.91), channel_id=1, source_target_pairs={{0,32},{2,34},{4,36},{6,38},{8,40},{10,42},{12,44},{14,46},{16,48}... | collective-permute-start | bytes 98312 | tf_op jit(solution)/shard_map/ppermute | solution.py:51
  11.7 0.0 collective-permute-done
  11.7 2.6 %collective-permute-done.1 = bf16[8,2048]{1,0:T(8,128)(2,1)S(1)} collective-permute-done((bf16[8,2048]{1,0:T(8,128)(2,1)S(1)}, bf16[8,2048]{1,0:T(8,128)(2,1)S(1)}, u32[]{:S(2)}, u32[]{:S(2)}) %collective-permute-start.1) | collective-permute-done | bytes 32800 | tf_op jit(solution)/shard_map/ppermute | solution.py:51
  14.3 0.0 collective-permute-done.2
  14.3 1.4 %collective-permute-start.3 = (bf16[32,2048]{1,0:T(8,128)(2,1)S(1)}, bf16[32,2048]{1,0:T(8,128)(2,1)S(1)}, u32[]{:S(2)}, u32[]{:S(2)}) collective-permute-start(bf16[32,2048]{1,0:T(8,128)(2,1)S(1)} %constant_dynamic-update-slice_fusion.3), channel_id=1, source_target_pairs={{0,128},{2,130},{4,132},{6,134},{8,136},{10,138},{12,140},{14,142}... | collective-permute-start | bytes 393224 | tf_op jit(solution)/shard_map/ppermute | solution.py:51
  15.7 1.1 %collective-permute-start.5 = (bf16[32,2048]{1,0:T(8,128)(2,1)S(1)}, bf16[32,2048]{1,0:T(8,128)(2,1)S(1)}, u32[]{:S(2)}, u32[]{:S(2)}) collective-permute-start(bf16[32,2048]{1,0:T(8,128)(2,1)S(1)} %constant_dynamic-update-slice_fusion.3), channel_id=1, source_target_pairs={{0,144},{2,146},{4,148},{6,150},{8,152},{10,154},{12,156},{14,158}... | collective-permute-start | bytes 393224 | tf_op jit(solution)/shard_map/ppermute | solution.py:51
  16.8 0.2 collective-permute-start.4
  17.1 1.9 %collective-permute-done.3 = bf16[32,2048]{1,0:T(8,128)(2,1)S(1)} collective-permute-done((bf16[32,2048]{1,0:T(8,128)(2,1)S(1)}, bf16[32,2048]{1,0:T(8,128)(2,1)S(1)}, u32[]{:S(2)}, u32[]{:S(2)}) %collective-permute-start.3) | collective-permute-done | bytes 131104 | tf_op jit(solution)/shard_map/ppermute | solution.py:51
  19.0 2.1 %collective-permute-done.4 = bf16[32,2048]{1,0:T(8,128)(2,1)S(1)} collective-permute-done((bf16[32,2048]{1,0:T(8,128)(2,1)S(1)}, bf16[32,2048]{1,0:T(8,128)(2,1)S(1)}, u32[]{:S(2)}, u32[]{:S(2)}) %collective-permute-start.4) | collective-permute-done | bytes 131104 | tf_op jit(solution)/shard_map/ppermute | solution.py:51
  21.1 0.0 collective-permute-done.5
  21.2 3.6 %collective-permute-start.8 = (bf16[128,2048]{1,0:T(8,128)(2,1)S(1)}, bf16[128,2048]{1,0:T(8,128)(2,1)S(1)}, u32[]{:S(2)}, u32[]{:S(2)}) collective-permute-start(bf16[128,2048]{1,0:T(8,128)(2,1)S(1)} %constant_dynamic-update-slice_fusion.refs_0_), channel_id=1, source_target_pairs={{0,2},{2,0},{4,6},{6,4},{8,10},{10,8},{12,14},{14,12},{16,18},{18,... | collective-permute-start | bytes 1572872 | tf_op jit(solution)/shard_map/ppermute | solution.py:51
  24.8 2.5 %collective-permute-start.7 = (bf16[128,2048]{1,0:T(8,128)(2,1)S(1)}, bf16[128,2048]{1,0:T(8,128)(2,1)S(1)}, u32[]{:S(2)}, u32[]{:S(2)}) collective-permute-start(bf16[128,2048]{1,0:T(8,128)(2,1)S(1)} %constant_dynamic-update-slice_fusion.refs_0_), channel_id=1, source_target_pairs={{0,4},{2,14},{4,8},{6,2},{8,12},{10,6},{12,0},{14,10},{16,20},{18,... | collective-permute-start | bytes 1572872 | tf_op jit(solution)/shard_map/ppermute | solution.py:51
  27.2 0.0 collective-permute-start.6
  27.3 0.0 copy-done.6
  27.3 0.1 copy.14
  27.4 0.1 copy.17
  27.5 0.0 copy-done
  27.5 0.0 copy-done.4
  27.5 0.0 copy-done.3
  27.5 0.0 copy-done.5
  27.5 0.0 copy-start.2
  27.5 3.3 %shard_map.92.refs_2_.refs_4_.refs_1_ = bf16[2048,1024]{1,0:T(8,128)(2,1)S(1)} custom-call(bf16[64,8,256]{2,1,0:T(8,128)(2,1)S(1)} %copy-done, f32[1,256]{1,0:T(1,128)S(1)} %bitcast.22, f32[1,256]{1,0:T(1,128)S(1)} %bitcast.24, bf16[32,256]{1,0:T(8,128)(2,1)S(1)} %bitcast.15, f32[1,32]{1,0:T(1,128)S(1)} %bitcast.25, bf16[32,4096]{1,0:T(8,128)(2,1)S(1)} %bitcast.14), custom_call_target="tpu_custom_call" | custom-call | flops 1073741824 | bytes 25165824 | tf_op jit(solution)/shard_map/pallas_call | solution.py:207
  30.9 0.0 collective-permute-done.8.refs_1_
  30.9 2.3 %shard_map.93.refs_4_ = bf16[128,8,8,128]{3,2,1,0:T(8,128)(2,1)} custom-call(bf16[128,2048]{1,0:T(8,128)(2,1)S(1)} %constant_dynamic-update-slice_fusion.refs_0_, bf16[128,2048]{1,0:T(8,128)(2,1)S(1)} %collective-permute-done.8.refs_1_, bf16[2048,1024]{1,0:T(8,128)(2,1)S(1)} %shard_map.92.refs_2_.refs_4_.refs_1_, f32[1,128]{1,0:T(1,128)S(1)} %bitcast.16), custom_call_target="tpu_custom_call" | custom-call | flops 1073741824 | bytes 10485760 | tf_op jit(solution)/shard_map/pallas_call | solution.py:163
  33.2 4.8 %collective-permute-done.7.refs_1_ = bf16[128,2048]{1,0:T(8,128)(2,1)S(1)} collective-permute-done((bf16[128,2048]{1,0:T(8,128)(2,1)S(1)}, bf16[128,2048]{1,0:T(8,128)(2,1)S(1)}, u32[]{:S(2)}, u32[]{:S(2)}) %collective-permute-start.7) | collective-permute-done | bytes 524320 | tf_op jit(solution)/shard_map/ppermute | solution.py:51
  38.0 2.2 %collective-permute-done.6.refs_0_ = bf16[128,2048]{1,0:T(8,128)(2,1)S(1)} collective-permute-done((bf16[128,2048]{1,0:T(8,128)(2,1)S(1)}, bf16[128,2048]{1,0:T(8,128)(2,1)S(1)}, u32[]{:S(2)}, u32[]{:S(2)}) %collective-permute-start.6) | collective-permute-done | bytes 524320 | tf_op jit(solution)/shard_map/ppermute | solution.py:51
  40.2 1.6 %collective-permute-start.9 = (bf16[128,2048]{1,0:T(8,128)(2,1)S(1)}, bf16[128,2048]{1,0:T(8,128)(2,1)S(1)}, u32[]{:S(2)}, u32[]{:S(2)}) collective-permute-start(bf16[128,2048]{1,0:T(8,128)(2,1)S(1)} %collective-permute-done.7.refs_1_), channel_id=1, source_target_pairs={{0,4},{2,14},{4,8},{6,2},{8,12},{10,6},{12,0},{14,10},{16,20},{18,... | collective-permute-start | bytes 1572872 | tf_op jit(solution)/shard_map/ppermute | solution.py:51
  41.7 2.3 %shard_map.94.refs_6_ = bf16[128,8,8,128]{3,2,1,0:T(8,128)(2,1)} custom-call(bf16[128,2048]{1,0:T(8,128)(2,1)S(1)} %collective-permute-done.6.refs_0_, bf16[128,2048]{1,0:T(8,128)(2,1)S(1)} %collective-permute-done.7.refs_1_, bf16[2048,1024]{1,0:T(8,128)(2,1)S(1)} %shard_map.92.refs_2_.refs_4_.refs_1_, ...), custom_call_target="tpu_custom_call", output_to_operand_aliasing={{}: (4, {})} | custom-call | flops 1073741824 | bytes 104857600 | tf_op jit(solution)/shard_map/pallas_call | solution.py:163
  44.1 0.1 collective-permute-start.11
  44.2 0.5 collective-permute-start.10
  44.7 0.4 collective-permute-start.13
  45.1 0.4 collective-permute-start.12
  45.5 0.2 collective-permute-done.11.refs_1_
  45.7 0.4 collective-permute-done.10.refs_0_
  46.1 0.4 collective-permute-done.13.refs_3_
  46.5 0.4 collective-permute-done.12.refs_2_
  46.9 2.3 %shard_map.95.refs_3_ = bf16[128,8,8,128]{3,2,1,0:T(8,128)(2,1)} custom-call(bf16[64,2048]{1,0:T(8,128)(2,1)S(1)} %collective-permute-done.10.refs_0_, bf16[64,2048]{1,0:T(8,128)(2,1)S(1)} %collective-permute-done.11.refs_1_, bf16[64,2048]{1,0:T(8,128)(2,1)S(1)} %collective-permute-done.12.refs_2_, ...), custom_call_target="tpu_custom_call", output_to_operand_aliasing={{}: (6, {})} | custom-call | flops 1073741824 | bytes 1024 | tf_op jit(solution)/shard_map/pallas_call | solution.py:163
  49.2 0.0 collective-permute-done.9.refs_0_
  49.2 1.1 %collective-permute-start.14 = (bf16[128,2048]{1,0:T(8,128)(2,1)S(1)}, bf16[128,2048]{1,0:T(8,128)(2,1)S(1)}, u32[]{:S(2)}, u32[]{:S(2)}) collective-permute-start(bf16[128,2048]{1,0:T(8,128)(2,1)S(1)} %collective-permute-done.9.refs_0_), channel_id=1, source_target_pairs={{0,2},{2,0},{4,6},{6,4},{8,10},{10,8},{12,14},{14,12},{16,18},{18,... | collective-permute-start | bytes 1572872 | tf_op jit(solution)/shard_map/ppermute | solution.py:51
  50.2 1.5 %shard_map.96.refs_3_ = bf16[128,8,8,128]{3,2,1,0:T(8,128)(2,1)} custom-call(bf16[128,2048]{1,0:T(8,128)(2,1)S(1)} %collective-permute-done.9.refs_0_, bf16[2048,1024]{1,0:T(8,128)(2,1)S(1)} %shard_map.92.refs_2_.refs_4_.refs_1_, f32[1,128]{1,0:T(1,128)S(1)} %bitcast.19, bf16[128,8,8,128]{3,2,1,0:T(8,128)(2,1)} %shard_map.95.refs_3_), custom_call_target="tpu_custom_call", output_to_operand_aliasing={{}: (3, {})} | custom-call | flops 536870912 | bytes 10485760 | tf_op jit(solution)/shard_map/pallas_call | solution.py:163
  51.8 0.0 collective-permute-done.14.refs_0_
  51.8 1.6 %shard_map.97 = bf16[128,8,8,128]{3,2,1,0:T(8,128)(2,1)} custom-call(bf16[128,2048]{1,0:T(8,128)(2,1)S(1)} %collective-permute-done.14.refs_0_, bf16[2048,1024]{1,0:T(8,128)(2,1)S(1)} %shard_map.92.refs_2_.refs_4_.refs_1_, f32[1,128]{1,0:T(1,128)S(1)} %bitcast.20, bf16[128,8,8,128]{3,2,1,0:T(8,128)(2,1)} %shard_map.96.refs_3_), custom_call_target="tpu_custom_call", output_to_operand_aliasing={{}: (3, {})} | custom-call | flops 536870912 | bytes 10485760 | tf_op jit(solution)/shard_map/pallas_call | solution.py:163
  (15 shorter events, 0.2 us)
Async XLA Ops:
  0.0 27.5 %copy-start = (bf16[64,8,256]{2,1,0:T(8,128)(2,1)S(1)}, bf16[64,8,256]{2,1,0:T(8,128)(2,1)}, u32[]{:S(2)}) copy-start(bf16[64,8,256]{2,1,0:T(8,128)(2,1)} %feats_ref.3) | copy-start | bytes 786436
  0.0 27.5 %copy-start.4 = (f32[256]{0:T(256)S(1)}, f32[256]{0:T(256)}, u32[]{:S(2)}) copy-start(f32[256]{0:T(256)} %param.11) | copy-start | bytes 3076
  0.0 27.5 %copy-start.3 = (f32[256]{0:T(256)S(1)}, f32[256]{0:T(256)}, u32[]{:S(2)}) copy-start(f32[256]{0:T(256)} %param.10) | copy-start | bytes 3076
  0.0 27.2 %copy-start.6 = (bf16[1024,128]{1,0:T(8,128)(2,1)S(1)}, bf16[1024,128]{1,0:T(8,128)(2,1)}, u32[]{:S(2)}) copy-start(bf16[1024,128]{1,0:T(8,128)(2,1)} %param.16) | copy-start | bytes 786436
  0.0 27.5 %copy-start.5 = (f32[32]{0:T(128)S(1)}, f32[32]{0:T(128)}, u32[]{:S(2)}) copy-start(f32[32]{0:T(128)} %param.15) | copy-start | bytes 388
  0.0 27.5 %copy-start.1 = (bf16[256,32]{0,1:T(8,128)(2,1)S(1)}, bf16[256,32]{0,1:T(8,128)(2,1)}, u32[]{:S(2)}) copy-start(bf16[256,32]{0,1:T(8,128)(2,1)} %param.14) | copy-start | bytes 49156
  1.5 10.2 %collective-permute-start = (bf16[8,2048]{1,0:T(8,128)(2,1)S(1)}, bf16[8,2048]{1,0:T(8,128)(2,1)S(1)}, u32[]{:S(2)}, u32[]{:S(2)}) collective-permute-start(bf16[8,2048]{1,0:T(8,128)(2,1)S(1)} %shard_map.91), channel_id=1, source_target_pairs={{0,64},{2,66},{4,68},{6,70},{8,72},{10,74},{12,76},{14,78},{16,80}... | collective-permute-start | bytes 98312 | tf_op jit(solution)/shard_map/ppermute | solution.py:51
  9.3 5.0 %collective-permute-start.2 = (bf16[8,2048]{1,0:T(8,128)(2,1)S(1)}, bf16[8,2048]{1,0:T(8,128)(2,1)S(1)}, u32[]{:S(2)}, u32[]{:S(2)}) collective-permute-start(bf16[8,2048]{1,0:T(8,128)(2,1)S(1)} %shard_map.91), channel_id=1, source_target_pairs={{0,96},{2,98},{4,100},{6,102},{8,104},{10,106},{12,108},{14,110},{... | collective-permute-start | bytes 98312 | tf_op jit(solution)/shard_map/ppermute | solution.py:51
  9.3 5.0 %collective-permute-start.1 = (bf16[8,2048]{1,0:T(8,128)(2,1)S(1)}, bf16[8,2048]{1,0:T(8,128)(2,1)S(1)}, u32[]{:S(2)}, u32[]{:S(2)}) collective-permute-start(bf16[8,2048]{1,0:T(8,128)(2,1)S(1)} %shard_map.91), channel_id=1, source_target_pairs={{0,32},{2,34},{4,36},{6,38},{8,40},{10,42},{12,44},{14,46},{16,48}... | collective-permute-start | bytes 98312 | tf_op jit(solution)/shard_map/ppermute | solution.py:51
  14.3 4.7 %collective-permute-start.3 = (bf16[32,2048]{1,0:T(8,128)(2,1)S(1)}, bf16[32,2048]{1,0:T(8,128)(2,1)S(1)}, u32[]{:S(2)}, u32[]{:S(2)}) collective-permute-start(bf16[32,2048]{1,0:T(8,128)(2,1)S(1)} %constant_dynamic-update-slice_fusion.3), channel_id=1, source_target_pairs={{0,128},{2,130},{4,132},{6,134},{8,136},{10,138},{12,140},{14,142}... | collective-permute-start | bytes 393224 | tf_op jit(solution)/shard_map/ppermute | solution.py:51
  15.7 5.5 %collective-permute-start.5 = (bf16[32,2048]{1,0:T(8,128)(2,1)S(1)}, bf16[32,2048]{1,0:T(8,128)(2,1)S(1)}, u32[]{:S(2)}, u32[]{:S(2)}) collective-permute-start(bf16[32,2048]{1,0:T(8,128)(2,1)S(1)} %constant_dynamic-update-slice_fusion.3), channel_id=1, source_target_pairs={{0,144},{2,146},{4,148},{6,150},{8,152},{10,154},{12,156},{14,158}... | collective-permute-start | bytes 393224 | tf_op jit(solution)/shard_map/ppermute | solution.py:51
  16.8 4.3 %collective-permute-start.4 = (bf16[32,2048]{1,0:T(8,128)(2,1)S(1)}, bf16[32,2048]{1,0:T(8,128)(2,1)S(1)}, u32[]{:S(2)}, u32[]{:S(2)}) collective-permute-start(bf16[32,2048]{1,0:T(8,128)(2,1)S(1)} %constant_dynamic-update-slice_fusion.3), channel_id=1, source_target_pairs={{0,16},{2,18},{4,20},{6,22},{8,24},{10,26},{12,28},{14,30},{16,0},... | collective-permute-start | bytes 393224 | tf_op jit(solution)/shard_map/ppermute | solution.py:51
  21.2 9.7 %collective-permute-start.8 = (bf16[128,2048]{1,0:T(8,128)(2,1)S(1)}, bf16[128,2048]{1,0:T(8,128)(2,1)S(1)}, u32[]{:S(2)}, u32[]{:S(2)}) collective-permute-start(bf16[128,2048]{1,0:T(8,128)(2,1)S(1)} %constant_dynamic-update-slice_fusion.refs_0_), channel_id=1, source_target_pairs={{0,2},{2,0},{4,6},{6,4},{8,10},{10,8},{12,14},{14,12},{16,18},{18,... | collective-permute-start | bytes 1572872 | tf_op jit(solution)/shard_map/ppermute | solution.py:51
  24.8 13.2 %collective-permute-start.7 = (bf16[128,2048]{1,0:T(8,128)(2,1)S(1)}, bf16[128,2048]{1,0:T(8,128)(2,1)S(1)}, u32[]{:S(2)}, u32[]{:S(2)}) collective-permute-start(bf16[128,2048]{1,0:T(8,128)(2,1)S(1)} %constant_dynamic-update-slice_fusion.refs_0_), channel_id=1, source_target_pairs={{0,4},{2,14},{4,8},{6,2},{8,12},{10,6},{12,0},{14,10},{16,20},{18,... | collective-permute-start | bytes 1572872 | tf_op jit(solution)/shard_map/ppermute | solution.py:51
  27.2 12.9 %collective-permute-start.6 = (bf16[128,2048]{1,0:T(8,128)(2,1)S(1)}, bf16[128,2048]{1,0:T(8,128)(2,1)S(1)}, u32[]{:S(2)}, u32[]{:S(2)}) collective-permute-start(bf16[128,2048]{1,0:T(8,128)(2,1)S(1)} %constant_dynamic-update-slice_fusion.refs_0_), channel_id=1, source_target_pairs={{0,12},{2,6},{4,0},{6,10},{8,4},{10,14},{12,8},{14,2},{16,28},{18,... | collective-permute-start | bytes 1572872 | tf_op jit(solution)/shard_map/ppermute | solution.py:51
  27.5 3.4 %copy-start.2 = (f32[128]{0:T(128)S(1)}, f32[128]{0:T(128)}, u32[]{:S(2)}) copy-start(f32[128]{0:T(128)} %param.17) | copy-start | bytes 1540
  40.2 9.0 %collective-permute-start.9 = (bf16[128,2048]{1,0:T(8,128)(2,1)S(1)}, bf16[128,2048]{1,0:T(8,128)(2,1)S(1)}, u32[]{:S(2)}, u32[]{:S(2)}) collective-permute-start(bf16[128,2048]{1,0:T(8,128)(2,1)S(1)} %collective-permute-done.7.refs_1_), channel_id=1, source_target_pairs={{0,4},{2,14},{4,8},{6,2},{8,12},{10,6},{12,0},{14,10},{16,20},{18,... | collective-permute-start | bytes 1572872 | tf_op jit(solution)/shard_map/ppermute | solution.py:51
  44.1 1.6 %collective-permute-start.11 = (bf16[64,2048]{1,0:T(8,128)(2,1)S(1)}, bf16[64,2048]{1,0:T(8,128)(2,1)S(1)}, u32[]{:S(2)}, u32[]{:S(2)}) collective-permute-start(bf16[64,2048]{1,0:T(8,128)(2,1)S(1)} %get-tuple-element.25), channel_id=1, source_target_pairs={{0,2},{2,0},{4,6},{6,4},{8,10},{10,8},{12,14},{14,12},{16,18},{18,... | collective-permute-start | bytes 786440 | tf_op jit(solution)/shard_map/ppermute | solution.py:51
  44.2 1.9 %collective-permute-start.10 = (bf16[64,2048]{1,0:T(8,128)(2,1)S(1)}, bf16[64,2048]{1,0:T(8,128)(2,1)S(1)}, u32[]{:S(2)}, u32[]{:S(2)}) collective-permute-start(bf16[64,2048]{1,0:T(8,128)(2,1)S(1)} %get-tuple-element.26), channel_id=1, source_target_pairs={{0,2},{2,0},{4,6},{6,4},{8,10},{10,8},{12,14},{14,12},{16,18},{18,... | collective-permute-start | bytes 786440 | tf_op jit(solution)/shard_map/ppermute | solution.py:51
  44.7 1.8 %collective-permute-start.13 = (bf16[64,2048]{1,0:T(8,128)(2,1)S(1)}, bf16[64,2048]{1,0:T(8,128)(2,1)S(1)}, u32[]{:S(2)}, u32[]{:S(2)}) collective-permute-start(bf16[64,2048]{1,0:T(8,128)(2,1)S(1)} %get-tuple-element.23), channel_id=1, source_target_pairs={{0,2},{2,0},{4,6},{6,4},{8,10},{10,8},{12,14},{14,12},{16,18},{18,... | collective-permute-start | bytes 786440 | tf_op jit(solution)/shard_map/ppermute | solution.py:51
  45.1 1.8 %collective-permute-start.12 = (bf16[64,2048]{1,0:T(8,128)(2,1)S(1)}, bf16[64,2048]{1,0:T(8,128)(2,1)S(1)}, u32[]{:S(2)}, u32[]{:S(2)}) collective-permute-start(bf16[64,2048]{1,0:T(8,128)(2,1)S(1)} %get-tuple-element.24), channel_id=1, source_target_pairs={{0,2},{2,0},{4,6},{6,4},{8,10},{10,8},{12,14},{14,12},{16,18},{18,... | collective-permute-start | bytes 786440 | tf_op jit(solution)/shard_map/ppermute | solution.py:51
  49.2 2.6 %collective-permute-start.14 = (bf16[128,2048]{1,0:T(8,128)(2,1)S(1)}, bf16[128,2048]{1,0:T(8,128)(2,1)S(1)}, u32[]{:S(2)}, u32[]{:S(2)}) collective-permute-start(bf16[128,2048]{1,0:T(8,128)(2,1)S(1)} %collective-permute-done.9.refs_0_), channel_id=1, source_target_pairs={{0,2},{2,0},{4,6},{6,4},{8,10},{10,8},{12,14},{14,12},{16,18},{18,... | collective-permute-start | bytes 1572872 | tf_op jit(solution)/shard_map/ppermute | solution.py:51

commit v7 on v6

--- a/solution.py
+++ b/solution.py
@@ -224,12 +224,14 @@
     ring = join([left] + [send(left, Z_EVEN[k]) for k in BACKS])
     block = join([ring, send(ring, Y_PAIR), send(ring, Z_PAIR), send(ring, YZ_PAIR)])
     ahead, behind = send(block, X_BACK), send(block, X_SIDE)
-    out = pair_block([block, send(block, CORE_PAIR)], [(0, 0), (1, 0)], table, bias, None)
+    half = block.shape[0] // 2
+    parts = [block[:half], block[half:]]
+    parts += [send(part, CORE_PAIR) for part in parts]
+    out = pair_block(parts, [(0, 0), (0, 0), (1, 0), (1, 0)], table, bias, None)
     ahead, behind, table, out = lax.optimization_barrier((ahead, behind, table, out))
     far = send(behind, X_SIDE)
     out = pair_block([ahead, behind], [(0, 1), (0, -1)], table, bias, out, 100 << 20)
     ahead, behind, out = lax.optimization_barrier((ahead, behind, out))
-    half = block.shape[0] // 2
     others = [send(part, CORE_PAIR) for b in (ahead, behind) for part in (b[:half], b[half:])]
     out = pair_block(others, [(1, -1), (1, -1), (1, 1), (1, 1)], table, bias, out, 1 << 10)
     far, out = lax.optimization_barrier((far, out))

time: 53.6 us -> 53.1 us (level)
  waiting for transfers between devices: 15 us -> 11.2 us
  starting transfers between devices: 23 us -> 26.2 us
    ppermute x15 -> x16, waiting for transfers between devices: 15 us -> 11.2 us  [send(): return lax.ppermute(block, 'dap', pairs)]
    ppermute x15 -> x16, starting transfers between devices: 23 us -> 26.2 us  [send(): return lax.ppermute(block, 'dap', pairs)]
  transfers between devices with their start and end apart: 15 -> 16, of which waited for: 9 -> 8; matrix products, arithmetic and copies ran while one was open for 1% -> 1% of each run, Pallas kernels for 22% -> 22%
where the time goes in v7:
time: 53.1 us; the launch traced here: 53 us
  starting transfers between devices  26.2 us (49%)
  Pallas kernels  14.7 us (28%)
  waiting for transfers between devices  11.2 us (21%)
    ppermute x16, starting transfers between devices, send(): return lax.ppermute(block, 'dap', pairs)  26.2 us
    ppermute x16, waiting for transfers between devices, send(): return lax.ppermute(block, 'dap', pairs)  11.2 us
    pallas_call x5, Pallas kernels, pair_block(): pl.pallas_call(functools.partial(pair_kernel, pieces=pieces, aliased=int(...  9.95 us
    pallas_call x1, Pallas kernels, per_device(): pl.pallas_call(table_kernel, out_shape=jax.ShapeDtypeStruct((SEQS * HID,...  3.33 us
    pallas_call x1, Pallas kernels, per_device(): pl.pallas_call(left_kernel, out_shape=pltpu.VMEM((rows, SEQS * HID), jnp....  1.43 us
  transfers between devices with their start and end apart: 16, of which 8 were waited for; matrix products, arithmetic and copies ran while one was open for 1% of the time, Pallas kernels for 22%

profile of v7, /device:TPU:1, one launch (start us, length us, event | category | flops | bytes accessed | tf_op | source)
XLA Modules:
  0.0 53.0 jit_solution(447555774973841902)
XLA Ops:
  0.0 0.0 copy-start.3
  0.0 0.0 copy-start.4
  0.0 0.0 copy-start.5
  0.0 1.4 %shard_map.91 = bf16[8,2048]{1,0:T(8,128)(2,1)S(1)} custom-call(bf16[64,8,256]{2,1,0:T(8,128)(2,1)} %feats_ref.3, f32[1,256]{1,0:T(1,128)} %bitcast.21, f32[1,256]{1,0:T(1,128)} %bitcast.23, bf16[32,256]{1,0:T(8,128)(2,1)} %bitcast.28, f32[1,32]{1,0:T(1,128)} %bitcast.29), custom_call_target="tpu_custom_call" | custom-call | tf_op jit(solution)/shard_map/pallas_call | solution.py:194
  1.5 7.8 %collective-permute-start = (bf16[8,2048]{1,0:T(8,128)(2,1)S(1)}, bf16[8,2048]{1,0:T(8,128)(2,1)S(1)}, u32[]{:S(2)}, u32[]{:S(2)}) collective-permute-start(bf16[8,2048]{1,0:T(8,128)(2,1)S(1)} %shard_map.91), channel_id=1, source_target_pairs={{0,64},{2,66},{4,68},{6,70},{8,72},{10,74},{12,76},{14,78},{16,80}... | collective-permute-start | bytes 98312 | tf_op jit(solution)/shard_map/ppermute | solution.py:51
  9.3 0.0 collective-permute-start.2
  9.3 2.4 %collective-permute-start.1 = (bf16[8,2048]{1,0:T(8,128)(2,1)S(1)}, bf16[8,2048]{1,0:T(8,128)(2,1)S(1)}, u32[]{:S(2)}, u32[]{:S(2)}) collective-permute-start(bf16[8,2048]{1,0:T(8,128)(2,1)S(1)} %shard_map.91), channel_id=1, source_target_pairs={{0,32},{2,34},{4,36},{6,38},{8,40},{10,42},{12,44},{14,46},{16,48}... | collective-permute-start | bytes 98312 | tf_op jit(solution)/shard_map/ppermute | solution.py:51
  11.7 0.0 collective-permute-done
  11.7 2.6 %collective-permute-done.1 = bf16[8,2048]{1,0:T(8,128)(2,1)S(1)} collective-permute-done((bf16[8,2048]{1,0:T(8,128)(2,1)S(1)}, bf16[8,2048]{1,0:T(8,128)(2,1)S(1)}, u32[]{:S(2)}, u32[]{:S(2)}) %collective-permute-start.1) | collective-permute-done | bytes 32800 | tf_op jit(solution)/shard_map/ppermute | solution.py:51
  14.3 0.0 collective-permute-done.2
  14.3 1.4 %collective-permute-start.3 = (bf16[32,2048]{1,0:T(8,128)(2,1)S(1)}, bf16[32,2048]{1,0:T(8,128)(2,1)S(1)}, u32[]{:S(2)}, u32[]{:S(2)}) collective-permute-start(bf16[32,2048]{1,0:T(8,128)(2,1)S(1)} %constant_dynamic-update-slice_fusion.3), channel_id=1, source_target_pairs={{0,128},{2,130},{4,132},{6,134},{8,136},{10,138},{12,140},{14,142}... | collective-permute-start | bytes 393224 | tf_op jit(solution)/shard_map/ppermute | solution.py:51
  15.7 1.1 %collective-permute-start.5 = (bf16[32,2048]{1,0:T(8,128)(2,1)S(1)}, bf16[32,2048]{1,0:T(8,128)(2,1)S(1)}, u32[]{:S(2)}, u32[]{:S(2)}) collective-permute-start(bf16[32,2048]{1,0:T(8,128)(2,1)S(1)} %constant_dynamic-update-slice_fusion.3), channel_id=1, source_target_pairs={{0,144},{2,146},{4,148},{6,150},{8,152},{10,154},{12,156},{14,158}... | collective-permute-start | bytes 393224 | tf_op jit(solution)/shard_map/ppermute | solution.py:51
  16.8 0.2 collective-permute-start.4
  17.1 1.9 %collective-permute-done.3 = bf16[32,2048]{1,0:T(8,128)(2,1)S(1)} collective-permute-done((bf16[32,2048]{1,0:T(8,128)(2,1)S(1)}, bf16[32,2048]{1,0:T(8,128)(2,1)S(1)}, u32[]{:S(2)}, u32[]{:S(2)}) %collective-permute-start.3) | collective-permute-done | bytes 131104 | tf_op jit(solution)/shard_map/ppermute | solution.py:51
  19.0 2.1 %collective-permute-done.4 = bf16[32,2048]{1,0:T(8,128)(2,1)S(1)} collective-permute-done((bf16[32,2048]{1,0:T(8,128)(2,1)S(1)}, bf16[32,2048]{1,0:T(8,128)(2,1)S(1)}, u32[]{:S(2)}, u32[]{:S(2)}) %collective-permute-start.4) | collective-permute-done | bytes 131104 | tf_op jit(solution)/shard_map/ppermute | solution.py:51
  21.1 0.0 collective-permute-done.5
  21.2 2.6 %collective-permute-start.7 = (bf16[128,2048]{1,0:T(8,128)(2,1)S(1)}, bf16[128,2048]{1,0:T(8,128)(2,1)S(1)}, u32[]{:S(2)}, u32[]{:S(2)}) collective-permute-start(bf16[128,2048]{1,0:T(8,128)(2,1)S(1)} %constant_dynamic-update-slice_fusion), channel_id=1, source_target_pairs={{0,4},{2,14},{4,8},{6,2},{8,12},{10,6},{12,0},{14,10},{16,20},{18,... | collective-permute-start | bytes 1572872 | tf_op jit(solution)/shard_map/ppermute | solution.py:51
  23.7 0.0 collective-permute-start.6
  23.8 4.4 %collective-permute-start.9 = (bf16[64,2048]{1,0:T(8,128)(2,1)S(1)}, bf16[64,2048]{1,0:T(8,128)(2,1)S(1)}, u32[]{:S(2)}, u32[]{:S(2)}) collective-permute-start(bf16[64,2048]{1,0:T(8,128)(2,1)S(1)} %get-tuple-element.27.refs_1_), channel_id=1, source_target_pairs={{0,2},{2,0},{4,6},{6,4},{8,10},{10,8},{12,14},{14,12},{16,18},{18,... | collective-permute-start | bytes 786440 | tf_op jit(solution)/shard_map/ppermute | solution.py:51
  28.1 0.1 collective-permute-start.8
  28.2 0.0 copy-done.6
  28.2 0.1 copy.14
  28.3 0.1 copy.17
  28.4 0.0 copy-done
  28.5 0.0 copy-done.1
  28.5 0.0 copy-start.2
  28.5 3.3 %shard_map.92.refs_4_.refs_2_.refs_1_ = bf16[2048,1024]{1,0:T(8,128)(2,1)S(1)} custom-call(bf16[64,8,256]{2,1,0:T(8,128)(2,1)S(1)} %copy-done, f32[1,256]{1,0:T(1,128)S(1)} %bitcast.22, f32[1,256]{1,0:T(1,128)S(1)} %bitcast.24, bf16[32,256]{1,0:T(8,128)(2,1)S(1)} %bitcast.15, f32[1,32]{1,0:T(1,128)S(1)} %bitcast.25, bf16[32,4096]{1,0:T(8,128)(2,1)S(1)} %bitcast.14), custom_call_target="tpu_custom_call" | custom-call | flops 1073741824 | bytes 25165824 | tf_op jit(solution)/shard_map/pallas_call | solution.py:207
  31.8 0.0 collective-permute-done.9.refs_3_
  31.9 0.0 collective-permute-done.8.refs_2_
  31.9 2.3 %shard_map.93.refs_4_ = bf16[128,8,8,128]{3,2,1,0:T(8,128)(2,1)} custom-call(bf16[64,2048]{1,0:T(8,128)(2,1)S(1)} %get-tuple-element.28.refs_0_, bf16[64,2048]{1,0:T(8,128)(2,1)S(1)} %get-tuple-element.27.refs_1_, bf16[64,2048]{1,0:T(8,128)(2,1)S(1)} %collective-permute-done.8.refs_2_, bf16[64,2048]{1,0:T(8,128)(2,1)S(1)} %collective-permute-done.9.refs_3_, ...), custom_call_target="tpu_custom_call" | custom-call | flops 1073741824 | bytes 10485760 | tf_op jit(solution)/shard_map/pallas_call | solution.py:163
  34.1 0.0 collective-permute-done.7.refs_1_
  34.2 3.1 %collective-permute-done.6.refs_0_ = bf16[128,2048]{1,0:T(8,128)(2,1)S(1)} collective-permute-done((bf16[128,2048]{1,0:T(8,128)(2,1)S(1)}, bf16[128,2048]{1,0:T(8,128)(2,1)S(1)}, u32[]{:S(2)}, u32[]{:S(2)}) %collective-permute-start.6) | collective-permute-done | bytes 524320 | tf_op jit(solution)/shard_map/ppermute | solution.py:51
  37.3 0.0 collective-permute-start.10
  37.3 2.3 %shard_map.94.refs_6_ = bf16[128,8,8,128]{3,2,1,0:T(8,128)(2,1)} custom-call(bf16[128,2048]{1,0:T(8,128)(2,1)S(1)} %collective-permute-done.6.refs_0_, bf16[128,2048]{1,0:T(8,128)(2,1)S(1)} %collective-permute-done.7.refs_1_, bf16[2048,1024]{1,0:T(8,128)(2,1)S(1)} %shard_map.92.refs_4_.refs_2_.refs_1_, ...), custom_call_target="tpu_custom_call", output_to_operand_aliasing={{}: (4, {})} | custom-call | flops 1073741824 | bytes 104857600 | tf_op jit(solution)/shard_map/pallas_call | solution.py:163
  39.6 2.0 %collective-permute-start.12 = (bf16[64,2048]{1,0:T(8,128)(2,1)S(1)}, bf16[64,2048]{1,0:T(8,128)(2,1)S(1)}, u32[]{:S(2)}, u32[]{:S(2)}) collective-permute-start(bf16[64,2048]{1,0:T(8,128)(2,1)S(1)} %get-tuple-element.25), channel_id=1, source_target_pairs={{0,2},{2,0},{4,6},{6,4},{8,10},{10,8},{12,14},{14,12},{16,18},{18,... | collective-permute-start | bytes 786440 | tf_op jit(solution)/shard_map/ppermute | solution.py:51
  41.7 0.3 collective-permute-start.11
  42.0 0.3 collective-permute-start.14
  42.3 0.3 collective-permute-start.13
  42.6 0.2 collective-permute-done.12.refs_1_
  42.8 0.4 collective-permute-done.11.refs_0_
  43.2 0.4 collective-permute-done.14.refs_3_
  43.6 0.4 collective-permute-done.13.refs_2_
  44.0 2.3 %shard_map.95.refs_3_ = bf16[128,8,8,128]{3,2,1,0:T(8,128)(2,1)} custom-call(bf16[64,2048]{1,0:T(8,128)(2,1)S(1)} %collective-permute-done.11.refs_0_, bf16[64,2048]{1,0:T(8,128)(2,1)S(1)} %collective-permute-done.12.refs_1_, bf16[64,2048]{1,0:T(8,128)(2,1)S(1)} %collective-permute-done.13.refs_2_, ...), custom_call_target="tpu_custom_call", output_to_operand_aliasing={{}: (6, {})} | custom-call | flops 1073741824 | bytes 1024 | tf_op jit(solution)/shard_map/pallas_call | solution.py:163
  46.3 0.0 collective-permute-done.10.refs_0_
  46.3 3.4 %collective-permute-start.15 = (bf16[128,2048]{1,0:T(8,128)(2,1)S(1)}, bf16[128,2048]{1,0:T(8,128)(2,1)S(1)}, u32[]{:S(2)}, u32[]{:S(2)}) collective-permute-start(bf16[128,2048]{1,0:T(8,128)(2,1)S(1)} %collective-permute-done.10.refs_0_), channel_id=1, source_target_pairs={{0,2},{2,0},{4,6},{6,4},{8,10},{10,8},{12,14},{14,12},{16,18},{18,... | collective-permute-start | bytes 1572872 | tf_op jit(solution)/shard_map/ppermute | solution.py:51
  49.7 1.6 %shard_map.96.refs_3_ = bf16[128,8,8,128]{3,2,1,0:T(8,128)(2,1)} custom-call(bf16[128,2048]{1,0:T(8,128)(2,1)S(1)} %collective-permute-done.10.refs_0_, bf16[2048,1024]{1,0:T(8,128)(2,1)S(1)} %shard_map.92.refs_4_.refs_2_.refs_1_, f32[1,128]{1,0:T(1,128)S(1)} %bitcast.19, bf16[128,8,8,128]{3,2,1,0:T(8,128)(2,1)} %shard_map.95.refs_3_), custom_call_target="tpu_custom_call", output_to_operand_aliasing={{}: (3, {})} | custom-call | flops 536870912 | bytes 10485760 | tf_op jit(solution)/shard_map/pallas_call | solution.py:163
  51.2 0.0 collective-permute-done.15.refs_0_
  51.2 1.6 %shard_map.97 = bf16[128,8,8,128]{3,2,1,0:T(8,128)(2,1)} custom-call(bf16[128,2048]{1,0:T(8,128)(2,1)S(1)} %collective-permute-done.15.refs_0_, bf16[2048,1024]{1,0:T(8,128)(2,1)S(1)} %shard_map.92.refs_4_.refs_2_.refs_1_, f32[1,128]{1,0:T(1,128)S(1)} %bitcast.20, bf16[128,8,8,128]{3,2,1,0:T(8,128)(2,1)} %shard_map.96.refs_3_), custom_call_target="tpu_custom_call", output_to_operand_aliasing={{}: (3, {})} | custom-call | flops 536870912 | bytes 10485760 | tf_op jit(solution)/shard_map/pallas_call | solution.py:163
  (18 shorter events, 0.2 us)
Async XLA Ops:
  0.0 28.2 %copy-start.6 = (bf16[1024,128]{1,0:T(8,128)(2,1)S(1)}, bf16[1024,128]{1,0:T(8,128)(2,1)}, u32[]{:S(2)}) copy-start(bf16[1024,128]{1,0:T(8,128)(2,1)} %param.16) | copy-start | bytes 786436
  0.0 28.4 %copy-start = (bf16[64,8,256]{2,1,0:T(8,128)(2,1)S(1)}, bf16[64,8,256]{2,1,0:T(8,128)(2,1)}, u32[]{:S(2)}) copy-start(bf16[64,8,256]{2,1,0:T(8,128)(2,1)} %feats_ref.3) | copy-start | bytes 786436
  0.0 28.4 %copy-start.1 = (bf16[256,32]{0,1:T(8,128)(2,1)S(1)}, bf16[256,32]{0,1:T(8,128)(2,1)}, u32[]{:S(2)}) copy-start(bf16[256,32]{0,1:T(8,128)(2,1)} %param.14) | copy-start | bytes 49156
  0.0 28.5 %copy-start.3 = (f32[256]{0:T(256)S(1)}, f32[256]{0:T(256)}, u32[]{:S(2)}) copy-start(f32[256]{0:T(256)} %param.10) | copy-start | bytes 3076
  0.0 28.5 %copy-start.4 = (f32[256]{0:T(256)S(1)}, f32[256]{0:T(256)}, u32[]{:S(2)}) copy-start(f32[256]{0:T(256)} %param.11) | copy-start | bytes 3076
  0.0 28.5 %copy-start.5 = (f32[32]{0:T(128)S(1)}, f32[32]{0:T(128)}, u32[]{:S(2)}) copy-start(f32[32]{0:T(128)} %param.15) | copy-start | bytes 388
  1.5 10.2 %collective-permute-start = (bf16[8,2048]{1,0:T(8,128)(2,1)S(1)}, bf16[8,2048]{1,0:T(8,128)(2,1)S(1)}, u32[]{:S(2)}, u32[]{:S(2)}) collective-permute-start(bf16[8,2048]{1,0:T(8,128)(2,1)S(1)} %shard_map.91), channel_id=1, source_target_pairs={{0,64},{2,66},{4,68},{6,70},{8,72},{10,74},{12,76},{14,78},{16,80}... | collective-permute-start | bytes 98312 | tf_op jit(solution)/shard_map/ppermute | solution.py:51
  9.3 5.0 %collective-permute-start.2 = (bf16[8,2048]{1,0:T(8,128)(2,1)S(1)}, bf16[8,2048]{1,0:T(8,128)(2,1)S(1)}, u32[]{:S(2)}, u32[]{:S(2)}) collective-permute-start(bf16[8,2048]{1,0:T(8,128)(2,1)S(1)} %shard_map.91), channel_id=1, source_target_pairs={{0,96},{2,98},{4,100},{6,102},{8,104},{10,106},{12,108},{14,110},{... | collective-permute-start | bytes 98312 | tf_op jit(solution)/shard_map/ppermute | solution.py:51
  9.3 5.0 %collective-permute-start.1 = (bf16[8,2048]{1,0:T(8,128)(2,1)S(1)}, bf16[8,2048]{1,0:T(8,128)(2,1)S(1)}, u32[]{:S(2)}, u32[]{:S(2)}) collective-permute-start(bf16[8,2048]{1,0:T(8,128)(2,1)S(1)} %shard_map.91), channel_id=1, source_target_pairs={{0,32},{2,34},{4,36},{6,38},{8,40},{10,42},{12,44},{14,46},{16,48}... | collective-permute-start | bytes 98312 | tf_op jit(solution)/shard_map/ppermute | solution.py:51
  14.3 4.7 %collective-permute-start.3 = (bf16[32,2048]{1,0:T(8,128)(2,1)S(1)}, bf16[32,2048]{1,0:T(8,128)(2,1)S(1)}, u32[]{:S(2)}, u32[]{:S(2)}) collective-permute-start(bf16[32,2048]{1,0:T(8,128)(2,1)S(1)} %constant_dynamic-update-slice_fusion.3), channel_id=1, source_target_pairs={{0,128},{2,130},{4,132},{6,134},{8,136},{10,138},{12,140},{14,142}... | collective-permute-start | bytes 393224 | tf_op jit(solution)/shard_map/ppermute | solution.py:51
  15.7 5.5 %collective-permute-start.5 = (bf16[32,2048]{1,0:T(8,128)(2,1)S(1)}, bf16[32,2048]{1,0:T(8,128)(2,1)S(1)}, u32[]{:S(2)}, u32[]{:S(2)}) collective-permute-start(bf16[32,2048]{1,0:T(8,128)(2,1)S(1)} %constant_dynamic-update-slice_fusion.3), channel_id=1, source_target_pairs={{0,144},{2,146},{4,148},{6,150},{8,152},{10,154},{12,156},{14,158}... | collective-permute-start | bytes 393224 | tf_op jit(solution)/shard_map/ppermute | solution.py:51
  16.8 4.3 %collective-permute-start.4 = (bf16[32,2048]{1,0:T(8,128)(2,1)S(1)}, bf16[32,2048]{1,0:T(8,128)(2,1)S(1)}, u32[]{:S(2)}, u32[]{:S(2)}) collective-permute-start(bf16[32,2048]{1,0:T(8,128)(2,1)S(1)} %constant_dynamic-update-slice_fusion.3), channel_id=1, source_target_pairs={{0,16},{2,18},{4,20},{6,22},{8,24},{10,26},{12,28},{14,30},{16,0},... | collective-permute-start | bytes 393224 | tf_op jit(solution)/shard_map/ppermute | solution.py:51
  21.2 13.0 %collective-permute-start.7 = (bf16[128,2048]{1,0:T(8,128)(2,1)S(1)}, bf16[128,2048]{1,0:T(8,128)(2,1)S(1)}, u32[]{:S(2)}, u32[]{:S(2)}) collective-permute-start(bf16[128,2048]{1,0:T(8,128)(2,1)S(1)} %constant_dynamic-update-slice_fusion), channel_id=1, source_target_pairs={{0,4},{2,14},{4,8},{6,2},{8,12},{10,6},{12,0},{14,10},{16,20},{18,... | collective-permute-start | bytes 1572872 | tf_op jit(solution)/shard_map/ppermute | solution.py:51
  23.7 13.6 %collective-permute-start.6 = (bf16[128,2048]{1,0:T(8,128)(2,1)S(1)}, bf16[128,2048]{1,0:T(8,128)(2,1)S(1)}, u32[]{:S(2)}, u32[]{:S(2)}) collective-permute-start(bf16[128,2048]{1,0:T(8,128)(2,1)S(1)} %constant_dynamic-update-slice_fusion), channel_id=1, source_target_pairs={{0,12},{2,6},{4,0},{6,10},{8,4},{10,14},{12,8},{14,2},{16,28},{18,... | collective-permute-start | bytes 1572872 | tf_op jit(solution)/shard_map/ppermute | solution.py:51
  23.8 8.1 %collective-permute-start.9 = (bf16[64,2048]{1,0:T(8,128)(2,1)S(1)}, bf16[64,2048]{1,0:T(8,128)(2,1)S(1)}, u32[]{:S(2)}, u32[]{:S(2)}) collective-permute-start(bf16[64,2048]{1,0:T(8,128)(2,1)S(1)} %get-tuple-element.27.refs_1_), channel_id=1, source_target_pairs={{0,2},{2,0},{4,6},{6,4},{8,10},{10,8},{12,14},{14,12},{16,18},{18,... | collective-permute-start | bytes 786440 | tf_op jit(solution)/shard_map/ppermute | solution.py:51
  28.1 3.7 %collective-permute-start.8 = (bf16[64,2048]{1,0:T(8,128)(2,1)S(1)}, bf16[64,2048]{1,0:T(8,128)(2,1)S(1)}, u32[]{:S(2)}, u32[]{:S(2)}) collective-permute-start(bf16[64,2048]{1,0:T(8,128)(2,1)S(1)} %get-tuple-element.28.refs_0_), channel_id=1, source_target_pairs={{0,2},{2,0},{4,6},{6,4},{8,10},{10,8},{12,14},{14,12},{16,18},{18,... | collective-permute-start | bytes 786440 | tf_op jit(solution)/shard_map/ppermute | solution.py:51
  28.5 3.4 %copy-start.2 = (f32[128]{0:T(128)S(1)}, f32[128]{0:T(128)}, u32[]{:S(2)}) copy-start(f32[128]{0:T(128)} %param.17) | copy-start | bytes 1540
  37.3 9.0 %collective-permute-start.10 = (bf16[128,2048]{1,0:T(8,128)(2,1)S(1)}, bf16[128,2048]{1,0:T(8,128)(2,1)S(1)}, u32[]{:S(2)}, u32[]{:S(2)}) collective-permute-start(bf16[128,2048]{1,0:T(8,128)(2,1)S(1)} %collective-permute-done.7.refs_1_), channel_id=1, source_target_pairs={{0,4},{2,14},{4,8},{6,2},{8,12},{10,6},{12,0},{14,10},{16,20},{18,... | collective-permute-start | bytes 1572872 | tf_op jit(solution)/shard_map/ppermute | solution.py:51
  39.6 3.2 %collective-permute-start.12 = (bf16[64,2048]{1,0:T(8,128)(2,1)S(1)}, bf16[64,2048]{1,0:T(8,128)(2,1)S(1)}, u32[]{:S(2)}, u32[]{:S(2)}) collective-permute-start(bf16[64,2048]{1,0:T(8,128)(2,1)S(1)} %get-tuple-element.25), channel_id=1, source_target_pairs={{0,2},{2,0},{4,6},{6,4},{8,10},{10,8},{12,14},{14,12},{16,18},{18,... | collective-permute-start | bytes 786440 | tf_op jit(solution)/shard_map/ppermute | solution.py:51
  41.7 1.5 %collective-permute-start.11 = (bf16[64,2048]{1,0:T(8,128)(2,1)S(1)}, bf16[64,2048]{1,0:T(8,128)(2,1)S(1)}, u32[]{:S(2)}, u32[]{:S(2)}) collective-permute-start(bf16[64,2048]{1,0:T(8,128)(2,1)S(1)} %get-tuple-element.26), channel_id=1, source_target_pairs={{0,2},{2,0},{4,6},{6,4},{8,10},{10,8},{12,14},{14,12},{16,18},{18,... | collective-permute-start | bytes 786440 | tf_op jit(solution)/shard_map/ppermute | solution.py:51
  42.0 1.6 %collective-permute-start.14 = (bf16[64,2048]{1,0:T(8,128)(2,1)S(1)}, bf16[64,2048]{1,0:T(8,128)(2,1)S(1)}, u32[]{:S(2)}, u32[]{:S(2)}) collective-permute-start(bf16[64,2048]{1,0:T(8,128)(2,1)S(1)} %get-tuple-element.23), channel_id=1, source_target_pairs={{0,2},{2,0},{4,6},{6,4},{8,10},{10,8},{12,14},{14,12},{16,18},{18,... | collective-permute-start | bytes 786440 | tf_op jit(solution)/shard_map/ppermute | solution.py:51
  42.3 1.7 %collective-permute-start.13 = (bf16[64,2048]{1,0:T(8,128)(2,1)S(1)}, bf16[64,2048]{1,0:T(8,128)(2,1)S(1)}, u32[]{:S(2)}, u32[]{:S(2)}) collective-permute-start(bf16[64,2048]{1,0:T(8,128)(2,1)S(1)} %get-tuple-element.24), channel_id=1, source_target_pairs={{0,2},{2,0},{4,6},{6,4},{8,10},{10,8},{12,14},{14,12},{16,18},{18,... | collective-permute-start | bytes 786440 | tf_op jit(solution)/shard_map/ppermute | solution.py:51
  46.3 4.9 %collective-permute-start.15 = (bf16[128,2048]{1,0:T(8,128)(2,1)S(1)}, bf16[128,2048]{1,0:T(8,128)(2,1)S(1)}, u32[]{:S(2)}, u32[]{:S(2)}) collective-permute-start(bf16[128,2048]{1,0:T(8,128)(2,1)S(1)} %collective-permute-done.10.refs_0_), channel_id=1, source_target_pairs={{0,2},{2,0},{4,6},{6,4},{8,10},{10,8},{12,14},{14,12},{16,18},{18,... | collective-permute-start | bytes 1572872 | tf_op jit(solution)/shard_map/ppermute | solution.py:51

commit v8 on v7

--- a/solution.py
+++ b/solution.py
@@ -228,7 +228,7 @@
     parts = [block[:half], block[half:]]
     parts += [send(part, CORE_PAIR) for part in parts]
     out = pair_block(parts, [(0, 0), (0, 0), (1, 0), (1, 0)], table, bias, None)
-    ahead, behind, table, out = lax.optimization_barrier((ahead, behind, table, out))
+    behind, table, out = lax.optimization_barrier((behind, table, out))
     far = send(behind, X_SIDE)
     out = pair_block([ahead, behind], [(0, 1), (0, -1)], table, bias, out, 100 << 20)
     ahead, behind, out = lax.optimization_barrier((ahead, behind, out))

time: 53.1 us -> 51.7 us (0.974)
  waiting for transfers between devices: 11.2 us -> 8.04 us
  starting transfers between devices: 26.2 us -> 28 us
    ppermute x16, waiting for transfers between devices: 11.2 us -> 8.04 us  [send(): return lax.ppermute(block, 'dap', pairs)]
    ppermute x16, starting transfers between devices: 26.2 us -> 28 us  [send(): return lax.ppermute(block, 'dap', pairs)]
  transfers between devices with their start and end apart: 16 -> 16, of which waited for: 8 -> 7; matrix products, arithmetic and copies ran while one was open for 1% -> 1% of each run, Pallas kernels for 22% -> 23%
where the time goes in v8:
time: 51.7 us; the launch traced here: 51.6 us
  starting transfers between devices  28 us (54%)
  Pallas kernels  14.7 us (28%)
  waiting for transfers between devices  8.04 us (16%)
    ppermute x16, starting transfers between devices, send(): return lax.ppermute(block, 'dap', pairs)  28 us
    pallas_call x5, Pallas kernels, pair_block(): pl.pallas_call(functools.partial(pair_kernel, pieces=pieces, aliased=int(...  9.94 us
    ppermute x16, waiting for transfers between devices, send(): return lax.ppermute(block, 'dap', pairs)  8.04 us
    pallas_call x1, Pallas kernels, per_device(): pl.pallas_call(table_kernel, out_shape=jax.ShapeDtypeStruct((SEQS * HID,...  3.33 us
    pallas_call x1, Pallas kernels, per_device(): pl.pallas_call(left_kernel, out_shape=pltpu.VMEM((rows, SEQS * HID), jnp....  1.43 us
  transfers between devices with their start and end apart: 16, of which 7 were waited for; matrix products, arithmetic and copies ran while one was open for 1% of the time, Pallas kernels for 23%

profile of v8, /device:TPU:1, one launch (start us, length us, event | category | flops | bytes accessed | tf_op | source)
XLA Modules:
  0.0 51.6 jit_solution(1652165591227933249)
XLA Ops:
  0.0 0.0 copy-start.3
  0.0 0.0 copy-start.4
  0.0 0.0 copy-start.5
  0.0 1.4 %shard_map.91 = bf16[8,2048]{1,0:T(8,128)(2,1)S(1)} custom-call(bf16[64,8,256]{2,1,0:T(8,128)(2,1)} %feats_ref.3, f32[1,256]{1,0:T(1,128)} %bitcast.21, f32[1,256]{1,0:T(1,128)} %bitcast.23, bf16[32,256]{1,0:T(8,128)(2,1)} %bitcast.28, f32[1,32]{1,0:T(1,128)} %bitcast.29), custom_call_target="tpu_custom_call" | custom-call | tf_op jit(solution)/shard_map/pallas_call | solution.py:194
  1.5 7.8 %collective-permute-start = (bf16[8,2048]{1,0:T(8,128)(2,1)S(1)}, bf16[8,2048]{1,0:T(8,128)(2,1)S(1)}, u32[]{:S(2)}, u32[]{:S(2)}) collective-permute-start(bf16[8,2048]{1,0:T(8,128)(2,1)S(1)} %shard_map.91), channel_id=1, source_target_pairs={{0,64},{2,66},{4,68},{6,70},{8,72},{10,74},{12,76},{14,78},{16,80}... | collective-permute-start | bytes 98312 | tf_op jit(solution)/shard_map/ppermute | solution.py:51
  9.3 0.0 collective-permute-start.2
  9.3 2.4 %collective-permute-start.1 = (bf16[8,2048]{1,0:T(8,128)(2,1)S(1)}, bf16[8,2048]{1,0:T(8,128)(2,1)S(1)}, u32[]{:S(2)}, u32[]{:S(2)}) collective-permute-start(bf16[8,2048]{1,0:T(8,128)(2,1)S(1)} %shard_map.91), channel_id=1, source_target_pairs={{0,32},{2,34},{4,36},{6,38},{8,40},{10,42},{12,44},{14,46},{16,48}... | collective-permute-start | bytes 98312 | tf_op jit(solution)/shard_map/ppermute | solution.py:51
  11.7 0.0 collective-permute-done
  11.7 2.6 %collective-permute-done.1 = bf16[8,2048]{1,0:T(8,128)(2,1)S(1)} collective-permute-done((bf16[8,2048]{1,0:T(8,128)(2,1)S(1)}, bf16[8,2048]{1,0:T(8,128)(2,1)S(1)}, u32[]{:S(2)}, u32[]{:S(2)}) %collective-permute-start.1) | collective-permute-done | bytes 32800 | tf_op jit(solution)/shard_map/ppermute | solution.py:51
  14.3 0.0 collective-permute-done.2
  14.3 1.4 %collective-permute-start.3 = (bf16[32,2048]{1,0:T(8,128)(2,1)S(1)}, bf16[32,2048]{1,0:T(8,128)(2,1)S(1)}, u32[]{:S(2)}, u32[]{:S(2)}) collective-permute-start(bf16[32,2048]{1,0:T(8,128)(2,1)S(1)} %constant_dynamic-update-slice_fusion.3), channel_id=1, source_target_pairs={{0,128},{2,130},{4,132},{6,134},{8,136},{10,138},{12,140},{14,142}... | collective-permute-start | bytes 393224 | tf_op jit(solution)/shard_map/ppermute | solution.py:51
  15.7 1.1 %collective-permute-start.5 = (bf16[32,2048]{1,0:T(8,128)(2,1)S(1)}, bf16[32,2048]{1,0:T(8,128)(2,1)S(1)}, u32[]{:S(2)}, u32[]{:S(2)}) collective-permute-start(bf16[32,2048]{1,0:T(8,128)(2,1)S(1)} %constant_dynamic-update-slice_fusion.3), channel_id=1, source_target_pairs={{0,144},{2,146},{4,148},{6,150},{8,152},{10,154},{12,156},{14,158}... | collective-permute-start | bytes 393224 | tf_op jit(solution)/shard_map/ppermute | solution.py:51
  16.8 0.2 collective-permute-start.4
  17.1 1.9 %collective-permute-done.3 = bf16[32,2048]{1,0:T(8,128)(2,1)S(1)} collective-permute-done((bf16[32,2048]{1,0:T(8,128)(2,1)S(1)}, bf16[32,2048]{1,0:T(8,128)(2,1)S(1)}, u32[]{:S(2)}, u32[]{:S(2)}) %collective-permute-start.3) | collective-permute-done | bytes 131104 | tf_op jit(solution)/shard_map/ppermute | solution.py:51
  19.0 2.1 %collective-permute-done.4 = bf16[32,2048]{1,0:T(8,128)(2,1)S(1)} collective-permute-done((bf16[32,2048]{1,0:T(8,128)(2,1)S(1)}, bf16[32,2048]{1,0:T(8,128)(2,1)S(1)}, u32[]{:S(2)}, u32[]{:S(2)}) %collective-permute-start.4) | collective-permute-done | bytes 131104 | tf_op jit(solution)/shard_map/ppermute | solution.py:51
  21.1 0.0 collective-permute-done.5
  21.2 1.3 %collective-permute-start.10 = (bf16[128,2048]{1,0:T(8,128)(2,1)S(1)}, bf16[128,2048]{1,0:T(8,128)(2,1)S(1)}, u32[]{:S(2)}, u32[]{:S(2)}) collective-permute-start(bf16[128,2048]{1,0:T(8,128)(2,1)S(1)} %constant_dynamic-update-slice_fusion), channel_id=1, source_target_pairs={{0,12},{2,6},{4,0},{6,10},{8,4},{10,14},{12,8},{14,2},{16,28},{18,... | collective-permute-start | bytes 1572872 | tf_op jit(solution)/shard_map/ppermute | solution.py:51
  22.4 1.5 %collective-permute-start.6 = (bf16[128,2048]{1,0:T(8,128)(2,1)S(1)}, bf16[128,2048]{1,0:T(8,128)(2,1)S(1)}, u32[]{:S(2)}, u32[]{:S(2)}) collective-permute-start(bf16[128,2048]{1,0:T(8,128)(2,1)S(1)} %constant_dynamic-update-slice_fusion), channel_id=1, source_target_pairs={{0,4},{2,14},{4,8},{6,2},{8,12},{10,6},{12,0},{14,10},{16,20},{18,... | collective-permute-start | bytes 1572872 | tf_op jit(solution)/shard_map/ppermute | solution.py:51
  24.0 3.7 %collective-permute-start.8 = (bf16[64,2048]{1,0:T(8,128)(2,1)S(1)}, bf16[64,2048]{1,0:T(8,128)(2,1)S(1)}, u32[]{:S(2)}, u32[]{:S(2)}) collective-permute-start(bf16[64,2048]{1,0:T(8,128)(2,1)S(1)} %get-tuple-element.25.refs_1_), channel_id=1, source_target_pairs={{0,2},{2,0},{4,6},{6,4},{8,10},{10,8},{12,14},{14,12},{16,18},{18,... | collective-permute-start | bytes 786440 | tf_op jit(solution)/shard_map/ppermute | solution.py:51
  27.6 0.1 collective-permute-start.7
  27.7 0.0 copy-done.6
  27.7 0.1 copy.14
  27.9 0.1 copy.17
  28.0 0.0 copy-done
  28.0 0.0 copy-done.1
  28.0 0.0 copy-start.2
  28.0 3.3 %shard_map.92.refs_4_.refs_2_.refs_1_ = bf16[2048,1024]{1,0:T(8,128)(2,1)S(1)} custom-call(bf16[64,8,256]{2,1,0:T(8,128)(2,1)S(1)} %copy-done, f32[1,256]{1,0:T(1,128)S(1)} %bitcast.22, f32[1,256]{1,0:T(1,128)S(1)} %bitcast.24, bf16[32,256]{1,0:T(8,128)(2,1)S(1)} %bitcast.15, f32[1,32]{1,0:T(1,128)S(1)} %bitcast.25, bf16[32,4096]{1,0:T(8,128)(2,1)S(1)} %bitcast.14), custom_call_target="tpu_custom_call" | custom-call | flops 1073741824 | bytes 25165824 | tf_op jit(solution)/shard_map/pallas_call | solution.py:207
  31.4 0.0 collective-permute-done.8.refs_3_
  31.4 0.0 collective-permute-done.7.refs_2_
  31.4 2.3 %shard_map.93.refs_4_ = bf16[128,8,8,128]{3,2,1,0:T(8,128)(2,1)} custom-call(bf16[64,2048]{1,0:T(8,128)(2,1)S(1)} %get-tuple-element.26.refs_0_, bf16[64,2048]{1,0:T(8,128)(2,1)S(1)} %get-tuple-element.25.refs_1_, bf16[64,2048]{1,0:T(8,128)(2,1)S(1)} %collective-permute-done.7.refs_2_, bf16[64,2048]{1,0:T(8,128)(2,1)S(1)} %collective-permute-done.8.refs_3_, ...), custom_call_target="tpu_custom_call" | custom-call | flops 1073741824 | bytes 10485760 | tf_op jit(solution)/shard_map/pallas_call | solution.py:163
  33.7 0.0 collective-permute-done.6.refs_1_
  33.7 3.0 %collective-permute-start.9 = (bf16[128,2048]{1,0:T(8,128)(2,1)S(1)}, bf16[128,2048]{1,0:T(8,128)(2,1)S(1)}, u32[]{:S(2)}, u32[]{:S(2)}) collective-permute-start(bf16[128,2048]{1,0:T(8,128)(2,1)S(1)} %collective-permute-done.6.refs_1_), channel_id=1, source_target_pairs={{0,4},{2,14},{4,8},{6,2},{8,12},{10,6},{12,0},{14,10},{16,20},{18,... | collective-permute-start | bytes 1572872 | tf_op jit(solution)/shard_map/ppermute | solution.py:51
  36.7 0.0 collective-permute-done.10.refs_0_
  36.7 2.3 %shard_map.94.refs_6_ = bf16[128,8,8,128]{3,2,1,0:T(8,128)(2,1)} custom-call(bf16[128,2048]{1,0:T(8,128)(2,1)S(1)} %collective-permute-done.10.refs_0_, bf16[128,2048]{1,0:T(8,128)(2,1)S(1)} %collective-permute-done.6.refs_1_, bf16[2048,1024]{1,0:T(8,128)(2,1)S(1)} %shard_map.92.refs_4_.refs_2_.refs_1_, ...), custom_call_target="tpu_custom_call", output_to_operand_aliasing={{}: (4, {})} | custom-call | flops 1073741824 | bytes 104857600 | tf_op jit(solution)/shard_map/pallas_call | solution.py:163
  39.0 1.3 %collective-permute-start.12 = (bf16[64,2048]{1,0:T(8,128)(2,1)S(1)}, bf16[64,2048]{1,0:T(8,128)(2,1)S(1)}, u32[]{:S(2)}, u32[]{:S(2)}) collective-permute-start(bf16[64,2048]{1,0:T(8,128)(2,1)S(1)} %get-tuple-element.23), channel_id=1, source_target_pairs={{0,2},{2,0},{4,6},{6,4},{8,10},{10,8},{12,14},{14,12},{16,18},{18,... | collective-permute-start | bytes 786440 | tf_op jit(solution)/shard_map/ppermute | solution.py:51
  40.3 0.3 collective-permute-start.11
  40.6 0.3 collective-permute-start.14
  41.0 0.3 collective-permute-start.13
  41.2 0.2 collective-permute-done.12.refs_1_
  41.5 0.4 collective-permute-done.11.refs_0_
  41.9 0.4 collective-permute-done.14.refs_3_
  42.3 0.4 collective-permute-done.13.refs_2_
  42.6 2.3 %shard_map.95.refs_3_ = bf16[128,8,8,128]{3,2,1,0:T(8,128)(2,1)} custom-call(bf16[64,2048]{1,0:T(8,128)(2,1)S(1)} %collective-permute-done.11.refs_0_, bf16[64,2048]{1,0:T(8,128)(2,1)S(1)} %collective-permute-done.12.refs_1_, bf16[64,2048]{1,0:T(8,128)(2,1)S(1)} %collective-permute-done.13.refs_2_, ...), custom_call_target="tpu_custom_call", output_to_operand_aliasing={{}: (6, {})} | custom-call | flops 1073741824 | bytes 1024 | tf_op jit(solution)/shard_map/pallas_call | solution.py:163
  44.9 0.0 collective-permute-done.9.refs_0_
  44.9 3.3 %collective-permute-start.15 = (bf16[128,2048]{1,0:T(8,128)(2,1)S(1)}, bf16[128,2048]{1,0:T(8,128)(2,1)S(1)}, u32[]{:S(2)}, u32[]{:S(2)}) collective-permute-start(bf16[128,2048]{1,0:T(8,128)(2,1)S(1)} %collective-permute-done.9.refs_0_), channel_id=1, source_target_pairs={{0,2},{2,0},{4,6},{6,4},{8,10},{10,8},{12,14},{14,12},{16,18},{18,... | collective-permute-start | bytes 1572872 | tf_op jit(solution)/shard_map/ppermute | solution.py:51
  48.3 1.6 %shard_map.96.refs_3_ = bf16[128,8,8,128]{3,2,1,0:T(8,128)(2,1)} custom-call(bf16[128,2048]{1,0:T(8,128)(2,1)S(1)} %collective-permute-done.9.refs_0_, bf16[2048,1024]{1,0:T(8,128)(2,1)S(1)} %shard_map.92.refs_4_.refs_2_.refs_1_, f32[1,128]{1,0:T(1,128)S(1)} %bitcast.19, bf16[128,8,8,128]{3,2,1,0:T(8,128)(2,1)} %shard_map.95.refs_3_), custom_call_target="tpu_custom_call", output_to_operand_aliasing={{}: (3, {})} | custom-call | flops 536870912 | bytes 10485760 | tf_op jit(solution)/shard_map/pallas_call | solution.py:163
  49.8 0.0 collective-permute-done.15.refs_0_
  49.9 1.6 %shard_map.97 = bf16[128,8,8,128]{3,2,1,0:T(8,128)(2,1)} custom-call(bf16[128,2048]{1,0:T(8,128)(2,1)S(1)} %collective-permute-done.15.refs_0_, bf16[2048,1024]{1,0:T(8,128)(2,1)S(1)} %shard_map.92.refs_4_.refs_2_.refs_1_, f32[1,128]{1,0:T(1,128)S(1)} %bitcast.20, bf16[128,8,8,128]{3,2,1,0:T(8,128)(2,1)} %shard_map.96.refs_3_), custom_call_target="tpu_custom_call", output_to_operand_aliasing={{}: (3, {})} | custom-call | flops 536870912 | bytes 10485760 | tf_op jit(solution)/shard_map/pallas_call | solution.py:163
  (18 shorter events, 0.2 us)
Async XLA Ops:
  0.0 27.7 %copy-start.6 = (bf16[1024,128]{1,0:T(8,128)(2,1)S(1)}, bf16[1024,128]{1,0:T(8,128)(2,1)}, u32[]{:S(2)}) copy-start(bf16[1024,128]{1,0:T(8,128)(2,1)} %param.16) | copy-start | bytes 786436
  0.0 28.0 %copy-start = (bf16[64,8,256]{2,1,0:T(8,128)(2,1)S(1)}, bf16[64,8,256]{2,1,0:T(8,128)(2,1)}, u32[]{:S(2)}) copy-start(bf16[64,8,256]{2,1,0:T(8,128)(2,1)} %feats_ref.3) | copy-start | bytes 786436
  0.0 28.0 %copy-start.1 = (bf16[256,32]{0,1:T(8,128)(2,1)S(1)}, bf16[256,32]{0,1:T(8,128)(2,1)}, u32[]{:S(2)}) copy-start(bf16[256,32]{0,1:T(8,128)(2,1)} %param.14) | copy-start | bytes 49156
  0.0 28.0 %copy-start.3 = (f32[256]{0:T(256)S(1)}, f32[256]{0:T(256)}, u32[]{:S(2)}) copy-start(f32[256]{0:T(256)} %param.10) | copy-start | bytes 3076
  0.0 28.0 %copy-start.4 = (f32[256]{0:T(256)S(1)}, f32[256]{0:T(256)}, u32[]{:S(2)}) copy-start(f32[256]{0:T(256)} %param.11) | copy-start | bytes 3076
  0.0 28.0 %copy-start.5 = (f32[32]{0:T(128)S(1)}, f32[32]{0:T(128)}, u32[]{:S(2)}) copy-start(f32[32]{0:T(128)} %param.15) | copy-start | bytes 388
  1.5 10.2 %collective-permute-start = (bf16[8,2048]{1,0:T(8,128)(2,1)S(1)}, bf16[8,2048]{1,0:T(8,128)(2,1)S(1)}, u32[]{:S(2)}, u32[]{:S(2)}) collective-permute-start(bf16[8,2048]{1,0:T(8,128)(2,1)S(1)} %shard_map.91), channel_id=1, source_target_pairs={{0,64},{2,66},{4,68},{6,70},{8,72},{10,74},{12,76},{14,78},{16,80}... | collective-permute-start | bytes 98312 | tf_op jit(solution)/shard_map/ppermute | solution.py:51
  9.3 5.0 %collective-permute-start.2 = (bf16[8,2048]{1,0:T(8,128)(2,1)S(1)}, bf16[8,2048]{1,0:T(8,128)(2,1)S(1)}, u32[]{:S(2)}, u32[]{:S(2)}) collective-permute-start(bf16[8,2048]{1,0:T(8,128)(2,1)S(1)} %shard_map.91), channel_id=1, source_target_pairs={{0,96},{2,98},{4,100},{6,102},{8,104},{10,106},{12,108},{14,110},{... | collective-permute-start | bytes 98312 | tf_op jit(solution)/shard_map/ppermute | solution.py:51
  9.3 5.0 %collective-permute-start.1 = (bf16[8,2048]{1,0:T(8,128)(2,1)S(1)}, bf16[8,2048]{1,0:T(8,128)(2,1)S(1)}, u32[]{:S(2)}, u32[]{:S(2)}) collective-permute-start(bf16[8,2048]{1,0:T(8,128)(2,1)S(1)} %shard_map.91), channel_id=1, source_target_pairs={{0,32},{2,34},{4,36},{6,38},{8,40},{10,42},{12,44},{14,46},{16,48}... | collective-permute-start | bytes 98312 | tf_op jit(solution)/shard_map/ppermute | solution.py:51
  14.3 4.7 %collective-permute-start.3 = (bf16[32,2048]{1,0:T(8,128)(2,1)S(1)}, bf16[32,2048]{1,0:T(8,128)(2,1)S(1)}, u32[]{:S(2)}, u32[]{:S(2)}) collective-permute-start(bf16[32,2048]{1,0:T(8,128)(2,1)S(1)} %constant_dynamic-update-slice_fusion.3), channel_id=1, source_target_pairs={{0,128},{2,130},{4,132},{6,134},{8,136},{10,138},{12,140},{14,142}... | collective-permute-start | bytes 393224 | tf_op jit(solution)/shard_map/ppermute | solution.py:51
  15.7 5.5 %collective-permute-start.5 = (bf16[32,2048]{1,0:T(8,128)(2,1)S(1)}, bf16[32,2048]{1,0:T(8,128)(2,1)S(1)}, u32[]{:S(2)}, u32[]{:S(2)}) collective-permute-start(bf16[32,2048]{1,0:T(8,128)(2,1)S(1)} %constant_dynamic-update-slice_fusion.3), channel_id=1, source_target_pairs={{0,144},{2,146},{4,148},{6,150},{8,152},{10,154},{12,156},{14,158}... | collective-permute-start | bytes 393224 | tf_op jit(solution)/shard_map/ppermute | solution.py:51
  16.8 4.3 %collective-permute-start.4 = (bf16[32,2048]{1,0:T(8,128)(2,1)S(1)}, bf16[32,2048]{1,0:T(8,128)(2,1)S(1)}, u32[]{:S(2)}, u32[]{:S(2)}) collective-permute-start(bf16[32,2048]{1,0:T(8,128)(2,1)S(1)} %constant_dynamic-update-slice_fusion.3), channel_id=1, source_target_pairs={{0,16},{2,18},{4,20},{6,22},{8,24},{10,26},{12,28},{14,30},{16,0},... | collective-permute-start | bytes 393224 | tf_op jit(solution)/shard_map/ppermute | solution.py:51
  21.2 15.6 %collective-permute-start.10 = (bf16[128,2048]{1,0:T(8,128)(2,1)S(1)}, bf16[128,2048]{1,0:T(8,128)(2,1)S(1)}, u32[]{:S(2)}, u32[]{:S(2)}) collective-permute-start(bf16[128,2048]{1,0:T(8,128)(2,1)S(1)} %constant_dynamic-update-slice_fusion), channel_id=1, source_target_pairs={{0,12},{2,6},{4,0},{6,10},{8,4},{10,14},{12,8},{14,2},{16,28},{18,... | collective-permute-start | bytes 1572872 | tf_op jit(solution)/shard_map/ppermute | solution.py:51
  22.4 11.2 %collective-permute-start.6 = (bf16[128,2048]{1,0:T(8,128)(2,1)S(1)}, bf16[128,2048]{1,0:T(8,128)(2,1)S(1)}, u32[]{:S(2)}, u32[]{:S(2)}) collective-permute-start(bf16[128,2048]{1,0:T(8,128)(2,1)S(1)} %constant_dynamic-update-slice_fusion), channel_id=1, source_target_pairs={{0,4},{2,14},{4,8},{6,2},{8,12},{10,6},{12,0},{14,10},{16,20},{18,... | collective-permute-start | bytes 1572872 | tf_op jit(solution)/shard_map/ppermute | solution.py:51
  24.0 7.4 %collective-permute-start.8 = (bf16[64,2048]{1,0:T(8,128)(2,1)S(1)}, bf16[64,2048]{1,0:T(8,128)(2,1)S(1)}, u32[]{:S(2)}, u32[]{:S(2)}) collective-permute-start(bf16[64,2048]{1,0:T(8,128)(2,1)S(1)} %get-tuple-element.25.refs_1_), channel_id=1, source_target_pairs={{0,2},{2,0},{4,6},{6,4},{8,10},{10,8},{12,14},{14,12},{16,18},{18,... | collective-permute-start | bytes 786440 | tf_op jit(solution)/shard_map/ppermute | solution.py:51
  27.6 3.7 %collective-permute-start.7 = (bf16[64,2048]{1,0:T(8,128)(2,1)S(1)}, bf16[64,2048]{1,0:T(8,128)(2,1)S(1)}, u32[]{:S(2)}, u32[]{:S(2)}) collective-permute-start(bf16[64,2048]{1,0:T(8,128)(2,1)S(1)} %get-tuple-element.26.refs_0_), channel_id=1, source_target_pairs={{0,2},{2,0},{4,6},{6,4},{8,10},{10,8},{12,14},{14,12},{16,18},{18,... | collective-permute-start | bytes 786440 | tf_op jit(solution)/shard_map/ppermute | solution.py:51
  28.0 3.4 %copy-start.2 = (f32[128]{0:T(128)S(1)}, f32[128]{0:T(128)}, u32[]{:S(2)}) copy-start(f32[128]{0:T(128)} %param.17) | copy-start | bytes 1540
  33.7 11.2 %collective-permute-start.9 = (bf16[128,2048]{1,0:T(8,128)(2,1)S(1)}, bf16[128,2048]{1,0:T(8,128)(2,1)S(1)}, u32[]{:S(2)}, u32[]{:S(2)}) collective-permute-start(bf16[128,2048]{1,0:T(8,128)(2,1)S(1)} %collective-permute-done.6.refs_1_), channel_id=1, source_target_pairs={{0,4},{2,14},{4,8},{6,2},{8,12},{10,6},{12,0},{14,10},{16,20},{18,... | collective-permute-start | bytes 1572872 | tf_op jit(solution)/shard_map/ppermute | solution.py:51
  39.0 2.4 %collective-permute-start.12 = (bf16[64,2048]{1,0:T(8,128)(2,1)S(1)}, bf16[64,2048]{1,0:T(8,128)(2,1)S(1)}, u32[]{:S(2)}, u32[]{:S(2)}) collective-permute-start(bf16[64,2048]{1,0:T(8,128)(2,1)S(1)} %get-tuple-element.23), channel_id=1, source_target_pairs={{0,2},{2,0},{4,6},{6,4},{8,10},{10,8},{12,14},{14,12},{16,18},{18,... | collective-permute-start | bytes 786440 | tf_op jit(solution)/shard_map/ppermute | solution.py:51
  40.3 1.5 %collective-permute-start.11 = (bf16[64,2048]{1,0:T(8,128)(2,1)S(1)}, bf16[64,2048]{1,0:T(8,128)(2,1)S(1)}, u32[]{:S(2)}, u32[]{:S(2)}) collective-permute-start(bf16[64,2048]{1,0:T(8,128)(2,1)S(1)} %get-tuple-element.24), channel_id=1, source_target_pairs={{0,2},{2,0},{4,6},{6,4},{8,10},{10,8},{12,14},{14,12},{16,18},{18,... | collective-permute-start | bytes 786440 | tf_op jit(solution)/shard_map/ppermute | solution.py:51
  40.6 1.6 %collective-permute-start.14 = (bf16[64,2048]{1,0:T(8,128)(2,1)S(1)}, bf16[64,2048]{1,0:T(8,128)(2,1)S(1)}, u32[]{:S(2)}, u32[]{:S(2)}) collective-permute-start(bf16[64,2048]{1,0:T(8,128)(2,1)S(1)} %get-tuple-element.21), channel_id=1, source_target_pairs={{0,2},{2,0},{4,6},{6,4},{8,10},{10,8},{12,14},{14,12},{16,18},{18,... | collective-permute-start | bytes 786440 | tf_op jit(solution)/shard_map/ppermute | solution.py:51
  41.0 1.7 %collective-permute-start.13 = (bf16[64,2048]{1,0:T(8,128)(2,1)S(1)}, bf16[64,2048]{1,0:T(8,128)(2,1)S(1)}, u32[]{:S(2)}, u32[]{:S(2)}) collective-permute-start(bf16[64,2048]{1,0:T(8,128)(2,1)S(1)} %get-tuple-element.22), channel_id=1, source_target_pairs={{0,2},{2,0},{4,6},{6,4},{8,10},{10,8},{12,14},{14,12},{16,18},{18,... | collective-permute-start | bytes 786440 | tf_op jit(solution)/shard_map/ppermute | solution.py:51
  44.9 4.9 %collective-permute-start.15 = (bf16[128,2048]{1,0:T(8,128)(2,1)S(1)}, bf16[128,2048]{1,0:T(8,128)(2,1)S(1)}, u32[]{:S(2)}, u32[]{:S(2)}) collective-permute-start(bf16[128,2048]{1,0:T(8,128)(2,1)S(1)} %collective-permute-done.9.refs_0_), channel_id=1, source_target_pairs={{0,2},{2,0},{4,6},{6,4},{8,10},{10,8},{12,14},{14,12},{16,18},{18,... | collective-permute-start | bytes 1572872 | tf_op jit(solution)/shard_map/ppermute | solution.py:51

commit v9 on v8

--- a/solution.py
+++ b/solution.py
@@ -127,7 +127,8 @@
     else:
         for n, left_ref in enumerate(lefts):
             left_all[n * rows : (n + 1) * rows, :] = left_ref[...]
-    acc_ref[...] = jnp.dot(left_all[...], table_ref[...], preferred_element_type=jnp.float32)
+    bias = jnp.concatenate([bias_ref[...]] * 8, axis=1)
+    acc_ref[...] = jnp.dot(left_all[...], table_ref[...], preferred_element_type=jnp.float32) + bias
     me = lax.axis_index("dap")
     core = lax.rem(me, NC)
     x = lax.rem(lax.div(me, NC), NX)
@@ -141,7 +142,7 @@
         first = n * count % len(PARTS)
         for k, (t, b, back) in enumerate(PARTS[first : first + count]):
             slot = n * count + k
-            part = acc_ref[slot * 8 : slot * 8 + 8, :].reshape(8, 8, C_Z) + bias_ref[...]
+            part = acc_ref[slot * 8 : slot * 8 + 8, :].reshape(8, 8, C_Z)
             ready[slot] = part.astype(jnp.bfloat16)
             to_y = lax.rem(y + t, NY)
             to_z = lax.rem((z + b * (1 - 2 * lax.rem(z, 2))) - back + NZ, NZ)

time: 51.7 us -> 51.7 us (level)
  no operation moved by 1% of the time
where the time goes in v9:
time: 51.7 us; the launch traced here: 51.6 us
  starting transfers between devices  28 us (54%)
  Pallas kernels  14.7 us (28%)
  waiting for transfers between devices  8.04 us (16%)
    ppermute x16, starting transfers between devices, send(): return lax.ppermute(block, 'dap', pairs)  28 us
    pallas_call x5, Pallas kernels, pair_block(): pl.pallas_call(functools.partial(pair_kernel, pieces=pieces, aliased=int(...  9.93 us
    ppermute x16, waiting for transfers between devices, send(): return lax.ppermute(block, 'dap', pairs)  8.04 us
    pallas_call x1, Pallas kernels, per_device(): pl.pallas_call(table_kernel, out_shape=jax.ShapeDtypeStruct((SEQS * HID,...  3.33 us
    pallas_call x1, Pallas kernels, per_device(): pl.pallas_call(left_kernel, out_shape=pltpu.VMEM((rows, SEQS * HID), jnp....  1.43 us
  transfers between devices with their start and end apart: 16, of which 7 were waited for; matrix products, arithmetic and copies ran while one was open for 1% of the time, Pallas kernels for 23%

profile of v9, /device:TPU:1, one launch (start us, length us, event | category | flops | bytes accessed | tf_op | source)
XLA Modules:
  0.0 51.6 jit_solution(10034163618818072256)
XLA Ops:
  0.0 0.0 copy-start.3
  0.0 0.0 copy-start.4
  0.0 0.0 copy-start.5
  0.0 1.4 %shard_map.91 = bf16[8,2048]{1,0:T(8,128)(2,1)S(1)} custom-call(bf16[64,8,256]{2,1,0:T(8,128)(2,1)} %feats_ref.3, f32[1,256]{1,0:T(1,128)} %bitcast.21, f32[1,256]{1,0:T(1,128)} %bitcast.23, bf16[32,256]{1,0:T(8,128)(2,1)} %bitcast.28, f32[1,32]{1,0:T(1,128)} %bitcast.29), custom_call_target="tpu_custom_call" | custom-call | tf_op jit(solution)/shard_map/pallas_call | solution.py:195
  1.5 7.8 %collective-permute-start = (bf16[8,2048]{1,0:T(8,128)(2,1)S(1)}, bf16[8,2048]{1,0:T(8,128)(2,1)S(1)}, u32[]{:S(2)}, u32[]{:S(2)}) collective-permute-start(bf16[8,2048]{1,0:T(8,128)(2,1)S(1)} %shard_map.91), channel_id=1, source_target_pairs={{0,64},{2,66},{4,68},{6,70},{8,72},{10,74},{12,76},{14,78},{16,80}... | collective-permute-start | bytes 98312 | tf_op jit(solution)/shard_map/ppermute | solution.py:51
  9.3 0.0 collective-permute-start.2
  9.3 2.4 %collective-permute-start.1 = (bf16[8,2048]{1,0:T(8,128)(2,1)S(1)}, bf16[8,2048]{1,0:T(8,128)(2,1)S(1)}, u32[]{:S(2)}, u32[]{:S(2)}) collective-permute-start(bf16[8,2048]{1,0:T(8,128)(2,1)S(1)} %shard_map.91), channel_id=1, source_target_pairs={{0,32},{2,34},{4,36},{6,38},{8,40},{10,42},{12,44},{14,46},{16,48}... | collective-permute-start | bytes 98312 | tf_op jit(solution)/shard_map/ppermute | solution.py:51
  11.7 0.0 collective-permute-done
  11.7 2.6 %collective-permute-done.1 = bf16[8,2048]{1,0:T(8,128)(2,1)S(1)} collective-permute-done((bf16[8,2048]{1,0:T(8,128)(2,1)S(1)}, bf16[8,2048]{1,0:T(8,128)(2,1)S(1)}, u32[]{:S(2)}, u32[]{:S(2)}) %collective-permute-start.1) | collective-permute-done | bytes 32800 | tf_op jit(solution)/shard_map/ppermute | solution.py:51
  14.3 0.0 collective-permute-done.2
  14.3 1.4 %collective-permute-start.3 = (bf16[32,2048]{1,0:T(8,128)(2,1)S(1)}, bf16[32,2048]{1,0:T(8,128)(2,1)S(1)}, u32[]{:S(2)}, u32[]{:S(2)}) collective-permute-start(bf16[32,2048]{1,0:T(8,128)(2,1)S(1)} %constant_dynamic-update-slice_fusion.3), channel_id=1, source_target_pairs={{0,128},{2,130},{4,132},{6,134},{8,136},{10,138},{12,140},{14,142}... | collective-permute-start | bytes 393224 | tf_op jit(solution)/shard_map/ppermute | solution.py:51
  15.7 1.1 %collective-permute-start.5 = (bf16[32,2048]{1,0:T(8,128)(2,1)S(1)}, bf16[32,2048]{1,0:T(8,128)(2,1)S(1)}, u32[]{:S(2)}, u32[]{:S(2)}) collective-permute-start(bf16[32,2048]{1,0:T(8,128)(2,1)S(1)} %constant_dynamic-update-slice_fusion.3), channel_id=1, source_target_pairs={{0,144},{2,146},{4,148},{6,150},{8,152},{10,154},{12,156},{14,158}... | collective-permute-start | bytes 393224 | tf_op jit(solution)/shard_map/ppermute | solution.py:51
  16.8 0.2 collective-permute-start.4
  17.1 1.9 %collective-permute-done.3 = bf16[32,2048]{1,0:T(8,128)(2,1)S(1)} collective-permute-done((bf16[32,2048]{1,0:T(8,128)(2,1)S(1)}, bf16[32,2048]{1,0:T(8,128)(2,1)S(1)}, u32[]{:S(2)}, u32[]{:S(2)}) %collective-permute-start.3) | collective-permute-done | bytes 131104 | tf_op jit(solution)/shard_map/ppermute | solution.py:51
  19.0 2.1 %collective-permute-done.4 = bf16[32,2048]{1,0:T(8,128)(2,1)S(1)} collective-permute-done((bf16[32,2048]{1,0:T(8,128)(2,1)S(1)}, bf16[32,2048]{1,0:T(8,128)(2,1)S(1)}, u32[]{:S(2)}, u32[]{:S(2)}) %collective-permute-start.4) | collective-permute-done | bytes 131104 | tf_op jit(solution)/shard_map/ppermute | solution.py:51
  21.1 0.0 collective-permute-done.5
  21.2 1.3 %collective-permute-start.10 = (bf16[128,2048]{1,0:T(8,128)(2,1)S(1)}, bf16[128,2048]{1,0:T(8,128)(2,1)S(1)}, u32[]{:S(2)}, u32[]{:S(2)}) collective-permute-start(bf16[128,2048]{1,0:T(8,128)(2,1)S(1)} %constant_dynamic-update-slice_fusion), channel_id=1, source_target_pairs={{0,12},{2,6},{4,0},{6,10},{8,4},{10,14},{12,8},{14,2},{16,28},{18,... | collective-permute-start | bytes 1572872 | tf_op jit(solution)/shard_map/ppermute | solution.py:51
  22.4 1.5 %collective-permute-start.6 = (bf16[128,2048]{1,0:T(8,128)(2,1)S(1)}, bf16[128,2048]{1,0:T(8,128)(2,1)S(1)}, u32[]{:S(2)}, u32[]{:S(2)}) collective-permute-start(bf16[128,2048]{1,0:T(8,128)(2,1)S(1)} %constant_dynamic-update-slice_fusion), channel_id=1, source_target_pairs={{0,4},{2,14},{4,8},{6,2},{8,12},{10,6},{12,0},{14,10},{16,20},{18,... | collective-permute-start | bytes 1572872 | tf_op jit(solution)/shard_map/ppermute | solution.py:51
  24.0 3.7 %collective-permute-start.8 = (bf16[64,2048]{1,0:T(8,128)(2,1)S(1)}, bf16[64,2048]{1,0:T(8,128)(2,1)S(1)}, u32[]{:S(2)}, u32[]{:S(2)}) collective-permute-start(bf16[64,2048]{1,0:T(8,128)(2,1)S(1)} %get-tuple-element.25.refs_1_), channel_id=1, source_target_pairs={{0,2},{2,0},{4,6},{6,4},{8,10},{10,8},{12,14},{14,12},{16,18},{18,... | collective-permute-start | bytes 786440 | tf_op jit(solution)/shard_map/ppermute | solution.py:51
  27.6 0.1 collective-permute-start.7
  27.7 0.0 copy-done.6
  27.7 0.1 copy.14
  27.9 0.1 copy.17
  28.0 0.0 copy-done
  28.0 0.0 copy-done.1
  28.0 0.0 copy-start.2
  28.0 3.3 %shard_map.92.refs_4_.refs_2_.refs_1_ = bf16[2048,1024]{1,0:T(8,128)(2,1)S(1)} custom-call(bf16[64,8,256]{2,1,0:T(8,128)(2,1)S(1)} %copy-done, f32[1,256]{1,0:T(1,128)S(1)} %bitcast.22, f32[1,256]{1,0:T(1,128)S(1)} %bitcast.24, bf16[32,256]{1,0:T(8,128)(2,1)S(1)} %bitcast.15, f32[1,32]{1,0:T(1,128)S(1)} %bitcast.25, bf16[32,4096]{1,0:T(8,128)(2,1)S(1)} %bitcast.14), custom_call_target="tpu_custom_call" | custom-call | flops 1073741824 | bytes 25165824 | tf_op jit(solution)/shard_map/pallas_call | solution.py:208
  31.4 0.0 collective-permute-done.8.refs_3_
  31.4 0.0 collective-permute-done.7.refs_2_
  31.4 2.3 %shard_map.93.refs_4_ = bf16[128,8,8,128]{3,2,1,0:T(8,128)(2,1)} custom-call(bf16[64,2048]{1,0:T(8,128)(2,1)S(1)} %get-tuple-element.26.refs_0_, bf16[64,2048]{1,0:T(8,128)(2,1)S(1)} %get-tuple-element.25.refs_1_, bf16[64,2048]{1,0:T(8,128)(2,1)S(1)} %collective-permute-done.7.refs_2_, bf16[64,2048]{1,0:T(8,128)(2,1)S(1)} %collective-permute-done.8.refs_3_, ...), custom_call_target="tpu_custom_call" | custom-call | flops 1073741824 | bytes 10485760 | tf_op jit(solution)/shard_map/pallas_call | solution.py:164
  33.7 0.0 collective-permute-done.6.refs_1_
  33.7 3.0 %collective-permute-start.9 = (bf16[128,2048]{1,0:T(8,128)(2,1)S(1)}, bf16[128,2048]{1,0:T(8,128)(2,1)S(1)}, u32[]{:S(2)}, u32[]{:S(2)}) collective-permute-start(bf16[128,2048]{1,0:T(8,128)(2,1)S(1)} %collective-permute-done.6.refs_1_), channel_id=1, source_target_pairs={{0,4},{2,14},{4,8},{6,2},{8,12},{10,6},{12,0},{14,10},{16,20},{18,... | collective-permute-start | bytes 1572872 | tf_op jit(solution)/shard_map/ppermute | solution.py:51
  36.7 0.0 collective-permute-done.10.refs_0_
  36.7 2.3 %shard_map.94.refs_6_ = bf16[128,8,8,128]{3,2,1,0:T(8,128)(2,1)} custom-call(bf16[128,2048]{1,0:T(8,128)(2,1)S(1)} %collective-permute-done.10.refs_0_, bf16[128,2048]{1,0:T(8,128)(2,1)S(1)} %collective-permute-done.6.refs_1_, bf16[2048,1024]{1,0:T(8,128)(2,1)S(1)} %shard_map.92.refs_4_.refs_2_.refs_1_, ...), custom_call_target="tpu_custom_call", output_to_operand_aliasing={{}: (4, {})} | custom-call | flops 1073741824 | bytes 104857600 | tf_op jit(solution)/shard_map/pallas_call | solution.py:164
  39.0 1.3 %collective-permute-start.12 = (bf16[64,2048]{1,0:T(8,128)(2,1)S(1)}, bf16[64,2048]{1,0:T(8,128)(2,1)S(1)}, u32[]{:S(2)}, u32[]{:S(2)}) collective-permute-start(bf16[64,2048]{1,0:T(8,128)(2,1)S(1)} %get-tuple-element.23), channel_id=1, source_target_pairs={{0,2},{2,0},{4,6},{6,4},{8,10},{10,8},{12,14},{14,12},{16,18},{18,... | collective-permute-start | bytes 786440 | tf_op jit(solution)/shard_map/ppermute | solution.py:51
  40.3 0.3 collective-permute-start.11
  40.6 0.3 collective-permute-start.14
  41.0 0.3 collective-permute-start.13
  41.2 0.2 collective-permute-done.12.refs_1_
  41.5 0.4 collective-permute-done.11.refs_0_
  41.9 0.4 collective-permute-done.14.refs_3_
  42.3 0.4 collective-permute-done.13.refs_2_
  42.6 2.3 %shard_map.95.refs_3_ = bf16[128,8,8,128]{3,2,1,0:T(8,128)(2,1)} custom-call(bf16[64,2048]{1,0:T(8,128)(2,1)S(1)} %collective-permute-done.11.refs_0_, bf16[64,2048]{1,0:T(8,128)(2,1)S(1)} %collective-permute-done.12.refs_1_, bf16[64,2048]{1,0:T(8,128)(2,1)S(1)} %collective-permute-done.13.refs_2_, ...), custom_call_target="tpu_custom_call", output_to_operand_aliasing={{}: (6, {})} | custom-call | flops 1073741824 | bytes 1024 | tf_op jit(solution)/shard_map/pallas_call | solution.py:164
  44.9 0.0 collective-permute-done.9.refs_0_
  44.9 3.4 %collective-permute-start.15 = (bf16[128,2048]{1,0:T(8,128)(2,1)S(1)}, bf16[128,2048]{1,0:T(8,128)(2,1)S(1)}, u32[]{:S(2)}, u32[]{:S(2)}) collective-permute-start(bf16[128,2048]{1,0:T(8,128)(2,1)S(1)} %collective-permute-done.9.refs_0_), channel_id=1, source_target_pairs={{0,2},{2,0},{4,6},{6,4},{8,10},{10,8},{12,14},{14,12},{16,18},{18,... | collective-permute-start | bytes 1572872 | tf_op jit(solution)/shard_map/ppermute | solution.py:51
  48.3 1.6 %shard_map.96.refs_3_ = bf16[128,8,8,128]{3,2,1,0:T(8,128)(2,1)} custom-call(bf16[128,2048]{1,0:T(8,128)(2,1)S(1)} %collective-permute-done.9.refs_0_, bf16[2048,1024]{1,0:T(8,128)(2,1)S(1)} %shard_map.92.refs_4_.refs_2_.refs_1_, f32[1,128]{1,0:T(1,128)S(1)} %bitcast.19, bf16[128,8,8,128]{3,2,1,0:T(8,128)(2,1)} %shard_map.95.refs_3_), custom_call_target="tpu_custom_call", output_to_operand_aliasing={{}: (3, {})} | custom-call | flops 536870912 | bytes 10485760 | tf_op jit(solution)/shard_map/pallas_call | solution.py:164
  49.8 0.0 collective-permute-done.15.refs_0_
  49.9 1.6 %shard_map.97 = bf16[128,8,8,128]{3,2,1,0:T(8,128)(2,1)} custom-call(bf16[128,2048]{1,0:T(8,128)(2,1)S(1)} %collective-permute-done.15.refs_0_, bf16[2048,1024]{1,0:T(8,128)(2,1)S(1)} %shard_map.92.refs_4_.refs_2_.refs_1_, f32[1,128]{1,0:T(1,128)S(1)} %bitcast.20, bf16[128,8,8,128]{3,2,1,0:T(8,128)(2,1)} %shard_map.96.refs_3_), custom_call_target="tpu_custom_call", output_to_operand_aliasing={{}: (3, {})} | custom-call | flops 536870912 | bytes 10485760 | tf_op jit(solution)/shard_map/pallas_call | solution.py:164
  (18 shorter events, 0.2 us)
Async XLA Ops:
  0.0 27.7 %copy-start.6 = (bf16[1024,128]{1,0:T(8,128)(2,1)S(1)}, bf16[1024,128]{1,0:T(8,128)(2,1)}, u32[]{:S(2)}) copy-start(bf16[1024,128]{1,0:T(8,128)(2,1)} %param.16) | copy-start | bytes 786436
  0.0 28.0 %copy-start = (bf16[64,8,256]{2,1,0:T(8,128)(2,1)S(1)}, bf16[64,8,256]{2,1,0:T(8,128)(2,1)}, u32[]{:S(2)}) copy-start(bf16[64,8,256]{2,1,0:T(8,128)(2,1)} %feats_ref.3) | copy-start | bytes 786436
  0.0 28.0 %copy-start.1 = (bf16[256,32]{0,1:T(8,128)(2,1)S(1)}, bf16[256,32]{0,1:T(8,128)(2,1)}, u32[]{:S(2)}) copy-start(bf16[256,32]{0,1:T(8,128)(2,1)} %param.14) | copy-start | bytes 49156
  0.0 28.0 %copy-start.3 = (f32[256]{0:T(256)S(1)}, f32[256]{0:T(256)}, u32[]{:S(2)}) copy-start(f32[256]{0:T(256)} %param.10) | copy-start | bytes 3076
  0.0 28.0 %copy-start.4 = (f32[256]{0:T(256)S(1)}, f32[256]{0:T(256)}, u32[]{:S(2)}) copy-start(f32[256]{0:T(256)} %param.11) | copy-start | bytes 3076
  0.0 28.0 %copy-start.5 = (f32[32]{0:T(128)S(1)}, f32[32]{0:T(128)}, u32[]{:S(2)}) copy-start(f32[32]{0:T(128)} %param.15) | copy-start | bytes 388
  1.5 10.2 %collective-permute-start = (bf16[8,2048]{1,0:T(8,128)(2,1)S(1)}, bf16[8,2048]{1,0:T(8,128)(2,1)S(1)}, u32[]{:S(2)}, u32[]{:S(2)}) collective-permute-start(bf16[8,2048]{1,0:T(8,128)(2,1)S(1)} %shard_map.91), channel_id=1, source_target_pairs={{0,64},{2,66},{4,68},{6,70},{8,72},{10,74},{12,76},{14,78},{16,80}... | collective-permute-start | bytes 98312 | tf_op jit(solution)/shard_map/ppermute | solution.py:51
  9.3 5.0 %collective-permute-start.2 = (bf16[8,2048]{1,0:T(8,128)(2,1)S(1)}, bf16[8,2048]{1,0:T(8,128)(2,1)S(1)}, u32[]{:S(2)}, u32[]{:S(2)}) collective-permute-start(bf16[8,2048]{1,0:T(8,128)(2,1)S(1)} %shard_map.91), channel_id=1, source_target_pairs={{0,96},{2,98},{4,100},{6,102},{8,104},{10,106},{12,108},{14,110},{... | collective-permute-start | bytes 98312 | tf_op jit(solution)/shard_map/ppermute | solution.py:51
  9.3 5.0 %collective-permute-start.1 = (bf16[8,2048]{1,0:T(8,128)(2,1)S(1)}, bf16[8,2048]{1,0:T(8,128)(2,1)S(1)}, u32[]{:S(2)}, u32[]{:S(2)}) collective-permute-start(bf16[8,2048]{1,0:T(8,128)(2,1)S(1)} %shard_map.91), channel_id=1, source_target_pairs={{0,32},{2,34},{4,36},{6,38},{8,40},{10,42},{12,44},{14,46},{16,48}... | collective-permute-start | bytes 98312 | tf_op jit(solution)/shard_map/ppermute | solution.py:51
  14.3 4.7 %collective-permute-start.3 = (bf16[32,2048]{1,0:T(8,128)(2,1)S(1)}, bf16[32,2048]{1,0:T(8,128)(2,1)S(1)}, u32[]{:S(2)}, u32[]{:S(2)}) collective-permute-start(bf16[32,2048]{1,0:T(8,128)(2,1)S(1)} %constant_dynamic-update-slice_fusion.3), channel_id=1, source_target_pairs={{0,128},{2,130},{4,132},{6,134},{8,136},{10,138},{12,140},{14,142}... | collective-permute-start | bytes 393224 | tf_op jit(solution)/shard_map/ppermute | solution.py:51
  15.7 5.5 %collective-permute-start.5 = (bf16[32,2048]{1,0:T(8,128)(2,1)S(1)}, bf16[32,2048]{1,0:T(8,128)(2,1)S(1)}, u32[]{:S(2)}, u32[]{:S(2)}) collective-permute-start(bf16[32,2048]{1,0:T(8,128)(2,1)S(1)} %constant_dynamic-update-slice_fusion.3), channel_id=1, source_target_pairs={{0,144},{2,146},{4,148},{6,150},{8,152},{10,154},{12,156},{14,158}... | collective-permute-start | bytes 393224 | tf_op jit(solution)/shard_map/ppermute | solution.py:51
  16.8 4.3 %collective-permute-start.4 = (bf16[32,2048]{1,0:T(8,128)(2,1)S(1)}, bf16[32,2048]{1,0:T(8,128)(2,1)S(1)}, u32[]{:S(2)}, u32[]{:S(2)}) collective-permute-start(bf16[32,2048]{1,0:T(8,128)(2,1)S(1)} %constant_dynamic-update-slice_fusion.3), channel_id=1, source_target_pairs={{0,16},{2,18},{4,20},{6,22},{8,24},{10,26},{12,28},{14,30},{16,0},... | collective-permute-start | bytes 393224 | tf_op jit(solution)/shard_map/ppermute | solution.py:51
  21.2 15.6 %collective-permute-start.10 = (bf16[128,2048]{1,0:T(8,128)(2,1)S(1)}, bf16[128,2048]{1,0:T(8,128)(2,1)S(1)}, u32[]{:S(2)}, u32[]{:S(2)}) collective-permute-start(bf16[128,2048]{1,0:T(8,128)(2,1)S(1)} %constant_dynamic-update-slice_fusion), channel_id=1, source_target_pairs={{0,12},{2,6},{4,0},{6,10},{8,4},{10,14},{12,8},{14,2},{16,28},{18,... | collective-permute-start | bytes 1572872 | tf_op jit(solution)/shard_map/ppermute | solution.py:51
  22.4 11.2 %collective-permute-start.6 = (bf16[128,2048]{1,0:T(8,128)(2,1)S(1)}, bf16[128,2048]{1,0:T(8,128)(2,1)S(1)}, u32[]{:S(2)}, u32[]{:S(2)}) collective-permute-start(bf16[128,2048]{1,0:T(8,128)(2,1)S(1)} %constant_dynamic-update-slice_fusion), channel_id=1, source_target_pairs={{0,4},{2,14},{4,8},{6,2},{8,12},{10,6},{12,0},{14,10},{16,20},{18,... | collective-permute-start | bytes 1572872 | tf_op jit(solution)/shard_map/ppermute | solution.py:51
  24.0 7.4 %collective-permute-start.8 = (bf16[64,2048]{1,0:T(8,128)(2,1)S(1)}, bf16[64,2048]{1,0:T(8,128)(2,1)S(1)}, u32[]{:S(2)}, u32[]{:S(2)}) collective-permute-start(bf16[64,2048]{1,0:T(8,128)(2,1)S(1)} %get-tuple-element.25.refs_1_), channel_id=1, source_target_pairs={{0,2},{2,0},{4,6},{6,4},{8,10},{10,8},{12,14},{14,12},{16,18},{18,... | collective-permute-start | bytes 786440 | tf_op jit(solution)/shard_map/ppermute | solution.py:51
  27.6 3.7 %collective-permute-start.7 = (bf16[64,2048]{1,0:T(8,128)(2,1)S(1)}, bf16[64,2048]{1,0:T(8,128)(2,1)S(1)}, u32[]{:S(2)}, u32[]{:S(2)}) collective-permute-start(bf16[64,2048]{1,0:T(8,128)(2,1)S(1)} %get-tuple-element.26.refs_0_), channel_id=1, source_target_pairs={{0,2},{2,0},{4,6},{6,4},{8,10},{10,8},{12,14},{14,12},{16,18},{18,... | collective-permute-start | bytes 786440 | tf_op jit(solution)/shard_map/ppermute | solution.py:51
  28.0 3.4 %copy-start.2 = (f32[128]{0:T(128)S(1)}, f32[128]{0:T(128)}, u32[]{:S(2)}) copy-start(f32[128]{0:T(128)} %param.17) | copy-start | bytes 1540
  33.7 11.2 %collective-permute-start.9 = (bf16[128,2048]{1,0:T(8,128)(2,1)S(1)}, bf16[128,2048]{1,0:T(8,128)(2,1)S(1)}, u32[]{:S(2)}, u32[]{:S(2)}) collective-permute-start(bf16[128,2048]{1,0:T(8,128)(2,1)S(1)} %collective-permute-done.6.refs_1_), channel_id=1, source_target_pairs={{0,4},{2,14},{4,8},{6,2},{8,12},{10,6},{12,0},{14,10},{16,20},{18,... | collective-permute-start | bytes 1572872 | tf_op jit(solution)/shard_map/ppermute | solution.py:51
  39.0 2.4 %collective-permute-start.12 = (bf16[64,2048]{1,0:T(8,128)(2,1)S(1)}, bf16[64,2048]{1,0:T(8,128)(2,1)S(1)}, u32[]{:S(2)}, u32[]{:S(2)}) collective-permute-start(bf16[64,2048]{1,0:T(8,128)(2,1)S(1)} %get-tuple-element.23), channel_id=1, source_target_pairs={{0,2},{2,0},{4,6},{6,4},{8,10},{10,8},{12,14},{14,12},{16,18},{18,... | collective-permute-start | bytes 786440 | tf_op jit(solution)/shard_map/ppermute | solution.py:51
  40.3 1.5 %collective-permute-start.11 = (bf16[64,2048]{1,0:T(8,128)(2,1)S(1)}, bf16[64,2048]{1,0:T(8,128)(2,1)S(1)}, u32[]{:S(2)}, u32[]{:S(2)}) collective-permute-start(bf16[64,2048]{1,0:T(8,128)(2,1)S(1)} %get-tuple-element.24), channel_id=1, source_target_pairs={{0,2},{2,0},{4,6},{6,4},{8,10},{10,8},{12,14},{14,12},{16,18},{18,... | collective-permute-start | bytes 786440 | tf_op jit(solution)/shard_map/ppermute | solution.py:51
  40.6 1.6 %collective-permute-start.14 = (bf16[64,2048]{1,0:T(8,128)(2,1)S(1)}, bf16[64,2048]{1,0:T(8,128)(2,1)S(1)}, u32[]{:S(2)}, u32[]{:S(2)}) collective-permute-start(bf16[64,2048]{1,0:T(8,128)(2,1)S(1)} %get-tuple-element.21), channel_id=1, source_target_pairs={{0,2},{2,0},{4,6},{6,4},{8,10},{10,8},{12,14},{14,12},{16,18},{18,... | collective-permute-start | bytes 786440 | tf_op jit(solution)/shard_map/ppermute | solution.py:51
  41.0 1.7 %collective-permute-start.13 = (bf16[64,2048]{1,0:T(8,128)(2,1)S(1)}, bf16[64,2048]{1,0:T(8,128)(2,1)S(1)}, u32[]{:S(2)}, u32[]{:S(2)}) collective-permute-start(bf16[64,2048]{1,0:T(8,128)(2,1)S(1)} %get-tuple-element.22), channel_id=1, source_target_pairs={{0,2},{2,0},{4,6},{6,4},{8,10},{10,8},{12,14},{14,12},{16,18},{18,... | collective-permute-start | bytes 786440 | tf_op jit(solution)/shard_map/ppermute | solution.py:51
  44.9 4.9 %collective-permute-start.15 = (bf16[128,2048]{1,0:T(8,128)(2,1)S(1)}, bf16[128,2048]{1,0:T(8,128)(2,1)S(1)}, u32[]{:S(2)}, u32[]{:S(2)}) collective-permute-start(bf16[128,2048]{1,0:T(8,128)(2,1)S(1)} %collective-permute-done.9.refs_0_), channel_id=1, source_target_pairs={{0,2},{2,0},{4,6},{6,4},{8,10},{10,8},{12,14},{14,12},{16,18},{18,... | collective-permute-start | bytes 1572872 | tf_op jit(solution)/shard_map/ppermute | solution.py:51
